TPU v7x, 512 devices: a whole 4x4x16 slice. The times are simulated.
512 devices in a mesh: rows: 32 (over z, y_hi), samp: 16 (over x, y_lo, core).
Axes of the slice: x: 4, y: 4 (y_hi: 2, y_lo: 2; y = y_hi * 2 + y_lo), z: 16, core: 2. Of those that a mesh axis runs over, the one named last changes fastest.
Arguments:
- atom_noised: bfloat16 [48, 16384, 128], P('samp', 'rows'), may hold values from -6 to 6
- atom_single: bfloat16 [16384, 128], P('rows'), may hold values from -6 to 6
- atom_token: int32 [16384], P('rows'), may hold values from 0 to 2047, as said below
- atom_count: int32 [32], P('rows'), may hold values from 320 to 512, as said below
- token_single: bfloat16 [2048, 768], P('rows')
- pair_bias: bfloat16 [8, 2048, 2048], P(None, 'rows'), may hold values from -4 to 350
- w_atom: bfloat16 [128, 128], replicated, may hold values from -0.5 to 0.5
- w_up: bfloat16 [128, 768], P('samp'), may hold values from -0.5 to 0.5
- w_query: bfloat16 [768, 384], P('samp'), may hold values from -0.21875 to 0.21875
- w_key: bfloat16 [768, 384], P('samp'), may hold values from -0.21875 to 0.21875
- w_value: bfloat16 [768, 384], P('samp'), may hold values from -0.21875 to 0.21875
- w_out: bfloat16 [384, 768], P('samp'), may hold values from -0.3125 to 0.3125
- w_down: bfloat16 [768, 128], P('samp'), may hold values from -0.21875 to 0.21875
- d_atom_out: bfloat16 [48, 16384, 128], P('samp', 'rows'), may hold values from -6 to 6
Outputs:
- atom_out: bfloat16 [48, 16384, 128], P('samp', 'rows')
- bias_grad: float32 [8, 2048, 2048], P(None, 'rows', 'samp')
Inputs may be any that keep to these rules, and one draw needn't show every extreme that they name: Index r of rows holds the slots r * 512 to (r + 1) * 512 - 1; its first atom_count[r] slots are atoms, the rest padding. Some index is full in every draw. `atom_token`: A slot of index r of rows names a token between r * 64 - 32 and (r + 1) * 64 + 31; along one index's slots the tokens never fall. Padding slots name tokens too.
All inputs are finite; a program needn't handle non-finite values.
Results may differ from a plain program's by a relative error of at most 0.04.
Values may be sent and summed in bfloat16 or wider, within the bound.
No kernel may reach another device: no remote copies, remote signals or barrier semaphores. Data moves between devices by JAX's collectives and lax.ppermute only.
A program may use at most 128 MiB of HBM per device.

v0:
```python
import jax
import jax.numpy as jnp
from jax import lax
from jax.sharding import PartitionSpec as P

EPSILON = 1e-05


def extended_2(cells, sides, width):
    for axis, dim in sides:
        count = lax.axis_size(axis)
        ends = count - 1
        head = lax.slice_in_dim(cells, 0, width, axis=dim)
        tail = lax.slice_in_dim(cells, cells.shape[dim] - width, cells.shape[dim], axis=dim)
        cells = jnp.concatenate(
            [
                lax.ppermute(tail, axis, [(i, (i + 1) % count) for i in range(ends)]),
                cells,
                lax.ppermute(head, axis, [((i + 1) % count, i) for i in range(ends)]),
            ],
            axis=dim,
        )
    return cells


def normalize(values):
    average = jnp.mean(values, axis=-1, keepdims=True)
    centered = values - average
    variance = jnp.mean(centered * centered, axis=-1, keepdims=True)
    inverse = lax.rsqrt(variance + EPSILON)
    return (centered * inverse, inverse)


def split_rims(planes, margin, tok_dev):
    own_part = planes[:, margin : margin + tok_dev]
    edge_part = jnp.concatenate([planes[:, :margin], planes[:, margin + tok_dev :]], axis=1)
    return (own_part, edge_part)


def settle_rims(own_part, extended, margin, tok_dev):
    incoming = jnp.concatenate([extended[:, :margin], extended[:, margin + tok_dev :]], axis=1)
    return own_part + incoming


def local(
    atom_noised,
    atom_single,
    atom_token,
    atom_count,
    token_single,
    pair_bias,
    w_atom,
    w_up,
    w_query,
    w_key,
    w_value,
    w_out,
    w_down,
    d_atom_out,
):
    samples, atom_dev, channels = atom_noised.shape
    tok_dev = token_single.shape[0]
    margin = tok_dev // 2
    heads = pair_bias.shape[0]
    key_total = pair_bias.shape[2]
    w_up, w_query, w_key, w_value, w_out, w_down = (
        lax.all_gather(w_up, "samp", axis=0, tiled=True),
        lax.all_gather(w_query, "samp", axis=0, tiled=True),
        lax.all_gather(w_key, "samp", axis=0, tiled=True),
        lax.all_gather(w_value, "samp", axis=0, tiled=True),
        lax.all_gather(w_out, "samp", axis=0, tiled=True),
        lax.all_gather(w_down, "samp", axis=0, tiled=True),
    )
    inner = w_query.shape[1]
    head_dim = inner // heads
    rank = lax.axis_index("rows")
    living = (lax.iota(jnp.int32, atom_dev) < atom_count[0]).astype(jnp.float32)
    local_token = atom_token - (rank * tok_dev - margin)
    one_hot = (local_token[:, None] == lax.iota(jnp.int32, 2 * tok_dev)[None, :]).astype(
        jnp.float32
    )
    one_hot = (one_hot * living[:, None]).astype(jnp.bfloat16)
    atom_query = (atom_noised.astype(jnp.float32) + atom_single.astype(jnp.float32)[None]).astype(
        jnp.bfloat16
    )
    hidden_pre = jnp.einsum("sac,cd->sad", atom_query, w_atom, preferred_element_type=jnp.float32)
    atom_hidden = (atom_query.astype(jnp.float32) + jax.nn.silu(hidden_pre)).astype(jnp.bfloat16)
    slot_counts = jnp.sum(one_hot.astype(jnp.float32), axis=0)
    count_plane = jnp.broadcast_to(slot_counts[None, :, None], (1, 2 * tok_dev, channels))
    forward_sums = jnp.einsum(
        "au,sac->suc", one_hot, atom_hidden, preferred_element_type=jnp.float32
    )
    planes = jnp.concatenate([forward_sums, count_plane], axis=0)
    own_part, edge_part = split_rims(planes, margin, tok_dev)
    extended = extended_2(edge_part, (("rows", 1),), margin)
    settled = settle_rims(own_part, extended, margin, tok_dev)
    token_sums = settled[:samples]
    token_counts = settled[samples, :, 0]
    pooled = (token_sums / jnp.maximum(token_counts, 1.0)[None, :, None]).astype(jnp.bfloat16)
    tokens_in = jnp.einsum("stc,cd->std", pooled, w_up, preferred_element_type=jnp.float32)
    tokens_in = tokens_in + token_single.astype(jnp.float32)[None]
    normed, _ = normalize(tokens_in)
    normed_b = normed.astype(jnp.bfloat16)
    scaling = head_dim ** (-0.5)
    queries = (
        jnp.einsum("std,de->ste", normed_b, w_query, preferred_element_type=jnp.float32) * scaling
    ).astype(jnp.bfloat16)
    keys_tok = jnp.einsum(
        "std,de->ste", normed_b, w_key, preferred_element_type=jnp.float32
    ).astype(jnp.bfloat16)
    values_tok = jnp.einsum(
        "std,de->ste", normed_b, w_value, preferred_element_type=jnp.float32
    ).astype(jnp.bfloat16)
    key_all, value_all = (
        lax.all_gather(keys_tok, "rows", axis=1, tiled=True),
        lax.all_gather(values_tok, "rows", axis=1, tiled=True),
    )
    prob_list = []
    for sample in range(samples):
        query_s = queries[sample].reshape(tok_dev, heads, head_dim)
        key_s = key_all[sample].reshape(key_total, heads, head_dim)
        scores = jnp.einsum("ihe,jhe->hij", query_s, key_s, preferred_element_type=jnp.float32)
        scores = scores + pair_bias.astype(jnp.float32)
        prob_list.append(jax.nn.softmax(scores, axis=-1))
    mixed_list = []
    for sample in range(samples):
        value_s = value_all[sample].reshape(key_total, heads, head_dim)
        mixed_s = jnp.einsum(
            "hij,jhe->ihe",
            prob_list[sample].astype(jnp.bfloat16),
            value_s,
            preferred_element_type=jnp.float32,
        )
        mixed_list.append(mixed_s.reshape(tok_dev, inner).astype(jnp.bfloat16))
    mixed = jnp.stack(mixed_list)
    tokens_out = tokens_in + jnp.einsum(
        "ste,ed->std", mixed, w_out, preferred_element_type=jnp.float32
    )
    normed_out, inverse_out = normalize(tokens_out)
    token_proj = jnp.einsum(
        "std,dc->stc", normed_out.astype(jnp.bfloat16), w_down, preferred_element_type=jnp.float32
    ).astype(jnp.bfloat16)
    proj_wide = extended_2(token_proj, (("rows", 1),), margin)
    picked = jnp.einsum("au,suc->sac", one_hot, proj_wide, preferred_element_type=jnp.float32)
    atom_out = (living[None, :, None] * (atom_hidden.astype(jnp.float32) + picked)).astype(
        jnp.bfloat16
    )
    cotangent_sums = jnp.einsum(
        "au,sac->suc", one_hot, d_atom_out, preferred_element_type=jnp.float32
    )
    own_back, edge_back = split_rims(cotangent_sums, margin, tok_dev)
    extended_back = extended_2(edge_back.astype(jnp.bfloat16), (("rows", 1),), margin).astype(
        edge_back.dtype
    )
    d_token_sums = settle_rims(own_back, extended_back, margin, tok_dev)
    d_token = d_token_sums.astype(jnp.bfloat16)
    d_normed = jnp.einsum("stc,dc->std", d_token, w_down, preferred_element_type=jnp.float32)
    first_term = jnp.mean(d_normed, axis=-1, keepdims=True)
    second_term = jnp.mean(d_normed * normed_out, axis=-1, keepdims=True)
    d_tokens = inverse_out * (d_normed - first_term - normed_out * second_term)
    d_mixed = jnp.einsum(
        "std,ed->ste", d_tokens.astype(jnp.bfloat16), w_out, preferred_element_type=jnp.float32
    ).astype(jnp.bfloat16)
    grad_total = jnp.zeros((heads, tok_dev, key_total), jnp.float32)
    for sample in range(samples):
        value_s = value_all[sample].reshape(key_total, heads, head_dim)
        dmix_s = d_mixed[sample].reshape(tok_dev, heads, head_dim)
        d_probs = jnp.einsum("ihe,jhe->hij", dmix_s, value_s, preferred_element_type=jnp.float32)
        prob_rows = prob_list[sample]
        delta = jnp.sum(prob_rows * d_probs, axis=-1, keepdims=True)
        grad_total = grad_total + prob_rows * (d_probs - delta)
    groups = lax.axis_size("samp")
    factor = key_total / (samples * groups)
    bias_grad = lax.psum_scatter(
        (grad_total * factor).astype(jnp.bfloat16), "samp", scatter_dimension=2, tiled=True
    ).astype(jnp.float32)
    return (atom_out, bias_grad)


def solution(mesh):
    placed = (
        P("samp", "rows", None),
        P("rows", None),
        P("rows"),
        P("rows"),
        P("rows", None),
        P(None, "rows", None),
        P(),
        P("samp", None),
        P("samp", None),
        P("samp", None),
        P("samp", None),
        P("samp", None),
        P("samp", None),
        P("samp", "rows", None),
    )
    return jax.shard_map(
        local,
        mesh=mesh,
        in_specs=placed,
        out_specs=(P("samp", "rows", None), P(None, "rows", "samp")),
        check_vma=False,
    )
```

profile of v0, /device:TPU:32, one launch (start us, length us, event | category | flops | bytes accessed | tf_op | source)
XLA Modules:
  0.0 562.9 jit_solution(5254352499331399089)
XLA Ops:
  12.3 5.1 collective-permute-start
  20.7 21.3 %all_gather.28 = bf16[768,384]{1,0:T(8,128)(2,1)S(1)} all-gather(bf16[48,384]{1,0:T(8,128)(2,1)S(1)} %copy-done.8), channel_id=1, replica_groups=mesh['rows'=32,'samp'=16] {'samp'}, dimensions={0}, use_global_device_ids=true | all-gather | bytes 626688 | tf_op jit(solution)/shard_map/all_gather | solution.py:69
  42.0 16.9 %all_gather.24 = bf16[128,768]{1,0:T(8,128)(2,1)S(1)} all-gather(bf16[8,768]{1,0:T(8,128)(2,1)S(1)} %copy-done.12), channel_id=1, replica_groups=mesh['rows'=32,'samp'=16] {'samp'}, dimensions={0}, use_global_device_ids=true | all-gather | bytes 208896 | tf_op jit(solution)/shard_map/all_gather | solution.py:67
  60.8 19.3 %all_gather.25 = bf16[768,384]{1,0:T(8,128)(2,1)S(1)} all-gather(bf16[48,384]{1,0:T(8,128)(2,1)S(1)} %copy-done.9), channel_id=1, replica_groups=mesh['rows'=32,'samp'=16] {'samp'}, dimensions={0}, use_global_device_ids=true | all-gather | bytes 626688 | tf_op jit(solution)/shard_map/all_gather | solution.py:70
  81.4 3.9 collective-permute-start.4
  85.4 4.3 collective-permute-start.5
  89.7 19.2 %all_gather.30 = bf16[384,768]{1,0:T(8,128)(2,1)} all-gather(bf16[24,768]{1,0:T(8,128)(2,1)S(1)} %copy-done.10), channel_id=1, replica_groups=mesh['rows'=32,'samp'=16] {'samp'}, dimensions={0}, use_global_device_ids=true | all-gather | bytes 626688 | tf_op jit(solution)/shard_map/all_gather | solution.py:71
  108.9 19.8 %all_gather.27 = bf16[768,384]{1,0:T(8,128)(2,1)S(1)} all-gather(bf16[48,384]{1,0:T(8,128)(2,1)S(1)} %copy-done.11), channel_id=1, replica_groups=mesh['rows'=32,'samp'=16] {'samp'}, dimensions={0}, use_global_device_ids=true | all-gather | bytes 626688 | tf_op jit(solution)/shard_map/all_gather | solution.py:68
  128.7 16.8 %all_gather.31 = bf16[768,128]{1,0:T(8,128)(2,1)S(1)} all-gather(bf16[48,128]{1,0:T(8,128)(2,1)S(1)} %copy-done.13), channel_id=1, replica_groups=mesh['rows'=32,'samp'=16] {'samp'}, dimensions={0}, use_global_device_ids=true | all-gather | bytes 208896 | tf_op jit(solution)/shard_map/all_gather | solution.py:72
  146.8 83.6 %all-gather.5.cloned.1.call-done = bf16[3,2048,384]{2,1,0:T(8,128)(2,1)} async-done(((bf16[3,64,384]{2,1,0:T(8,128)(2,1)}), bf16[3,2048,384]{2,1,0:T(8,128)(2,1)}) %all-gather.5.cloned.1.call-update) | async-done | bytes 4718608 | tf_op jit(solution)/shard_map/all_gather | solution.py:115
  230.4 4.5 fusion.96
  236.6 160.1 %all-gather.3.cloned.1.call-done = bf16[3,2048,384]{2,1,0:T(8,128)(2,1)} async-done(((bf16[3,64,384]{2,1,0:T(8,128)(2,1)}), bf16[3,2048,384]{2,1,0:T(8,128)(2,1)}) %all-gather.3.cloned.1.call-update) | async-done | bytes 4718608 | tf_op jit(solution)/shard_map/all_gather | solution.py:116
  396.7 4.6 fusion.97
  413.5 4.8 fusion.104
  421.8 4.8 fusion.103
  430.2 4.8 fusion.105
  443.2 5.0 fusion.2
  448.2 4.2 fusion.108
  452.6 5.1 fusion.1
  460.5 15.6 %multiply_convert_fusion = bf16[8,64,2048]{2,1,0:T(8,128)(2,1)} fusion(f32[8,64,2048]{2,1,0:T(8,128)} %fusion.109, f32[8,64,2048]{2,1,0:T(8,128)} %fusion.1, f32[8,64,2048]{2,1,0:T(8,128)} %fusion.108, f32[8,64,2048]{2,1,0:T(8,128)} %fusion.2, bf16[64,8,48]{0,2,1:T(8,128)(2,1)S(1)} %bitcast.122, bf16[2048,8,48]{0,2,1:T(8,128)(2,1)} %bitcast.113, ...), kind=kOutput, calls=%fused_computation.9 | convolution fusion | flops 217057792 | bytes 33085440 | tf_op jit(solution)/shard_map/sub | solution.py:171
  476.1 5.9 %copy.83 = bf16[8,64,2048]{1,0,2:T(8,128)(2,1)} copy(bf16[8,64,2048]{2,1,0:T(8,128)(2,1)} %multiply_convert_fusion) | data formatting | bytes 4194304
  482.0 6.5 %reshape.106 = bf16[2048,512]{1,0:T(8,128)(2,1)} reshape(bf16[2048,8,64]{2,1,0:T(8,128)(2,1)} %bitcast.102) | data formatting | bytes 4194304
  491.3 5.8 %collective-permute-start.3 = (bf16[3,32,128]{2,1,0:T(8,128)(2,1)S(1)}, bf16[3,32,128]{2,1,0:T(8,128)(2,1)S(1)}, u32[]{:S(2)}, u32[]{:S(2)}) collective-permute-start(bf16[3,32,128]{2,1,0:T(8,128)(2,1)S(1)} %get-tuple-element.23), channel_id=1, source_target_pairs={{16,0},{32,16},{48,32},{64,48},{80,64},{96,80},{112,96},{128,112},... | collective-permute-start | bytes 73736 | tf_op jit(solution)/shard_map/ppermute | solution.py:19
  499.7 54.6 %reduce-scatter.4.cloned.1.call-done = bf16[128,512]{1,0:T(8,128)(2,1)} async-done(((bf16[2048,512]{1,0:T(8,128)(2,1)}), bf16[128,512]{1,0:T(8,128)(2,1)}) %reduce-scatter.4.cloned.1.call-update) | async-done | bytes 131088
  (102 shorter events, 51.5 us)
Async XLA Ops:
  7.2 74.0 %copy-start = (bf16[3,512,128]{2,1,0:T(8,128)(2,1)S(1)}, bf16[3,512,128]{2,1,0:T(8,128)(2,1)}, u32[]{:S(2)}) copy-start(bf16[3,512,128]{2,1,0:T(8,128)(2,1)} %param.27) | copy-start | bytes 1179652
  7.2 13.4 %copy-start.7 = (bf16[64,768]{1,0:T(8,128)(2,1)S(1)}, bf16[64,768]{1,0:T(8,128)(2,1)}, u32[]{:S(2)}) copy-start(bf16[64,768]{1,0:T(8,128)(2,1)} %param.18) | copy-start | bytes 294916
  7.2 13.4 %copy-start.8 = (bf16[48,384]{1,0:T(8,128)(2,1)S(1)}, bf16[48,384]{1,0:T(8,128)(2,1)}, u32[]{:S(2)}) copy-start(bf16[48,384]{1,0:T(8,128)(2,1)} %param.23) | copy-start | bytes 110596
  7.2 34.8 %copy-start.12 = (bf16[8,768]{1,0:T(8,128)(2,1)S(1)}, bf16[8,768]{1,0:T(8,128)(2,1)}, u32[]{:S(2)}) copy-start(bf16[8,768]{1,0:T(8,128)(2,1)} %param.21) | copy-start | bytes 36868
  7.2 223.2 %all-gather.5.cloned.1.call-start = ((), (), s32[]{:S(2)}) async-start(), calls=%async_computation.2 | async-start | bytes 4866048 | tf_op jit(solution)/shard_map/all_gather | solution.py:115
  12.0 48.8 %copy-start.9 = (bf16[48,384]{1,0:T(8,128)(2,1)S(1)}, bf16[48,384]{1,0:T(8,128)(2,1)}, u32[]{:S(2)}) copy-start(bf16[48,384]{1,0:T(8,128)(2,1)} %param.24) | copy-start | bytes 110596
  12.3 77.4 %copy-start.10 = (bf16[24,768]{1,0:T(8,128)(2,1)S(1)}, bf16[24,768]{1,0:T(8,128)(2,1)}, u32[]{:S(2)}) copy-start(bf16[24,768]{1,0:T(8,128)(2,1)} %param.25) | copy-start | bytes 110596
  12.3 46.5 %collective-permute-start = (f32[4,32,128]{2,1,0:T(8,128)S(1)}, f32[4,32,128]{2,1,0:T(8,128)S(1)}, u32[]{:S(2)}, u32[]{:S(2)}) collective-permute-start(f32[4,32,128]{2,1,0:T(8,128)S(1)} %get-tuple-element.10), channel_id=1, source_target_pairs={{0,16},{16,32},{32,48},{48,64},{64,80},{80,96},{96,112},{112,128},... | collective-permute-start | bytes 196616 | tf_op jit(solution)/shard_map/ppermute | solution.py:17
  17.5 41.4 %collective-permute-start.1 = (f32[4,32,128]{2,1,0:T(8,128)S(1)}, f32[4,32,128]{2,1,0:T(8,128)S(1)}, u32[]{:S(2)}, u32[]{:S(2)}) collective-permute-start(f32[4,32,128]{2,1,0:T(8,128)S(1)} %get-tuple-element.11), channel_id=1, source_target_pairs={{16,0},{32,16},{48,32},{64,48},{80,64},{96,80},{112,96},{128,112},... | collective-permute-start | bytes 196616 | tf_op jit(solution)/shard_map/ppermute | solution.py:19
  20.6 88.3 %copy-start.11 = (bf16[48,384]{1,0:T(8,128)(2,1)S(1)}, bf16[48,384]{1,0:T(8,128)(2,1)}, u32[]{:S(2)}) copy-start(bf16[48,384]{1,0:T(8,128)(2,1)} %param.22) | copy-start | bytes 110596
  42.0 86.7 %copy-start.13 = (bf16[48,128]{1,0:T(8,128)(2,1)S(1)}, bf16[48,128]{1,0:T(8,128)(2,1)}, u32[]{:S(2)}) copy-start(bf16[48,128]{1,0:T(8,128)(2,1)} %param.26) | copy-start | bytes 36868
  60.8 335.9 %all-gather.3.cloned.1.call-start = ((), (), s32[]{:S(2)}) async-start(), calls=%async_computation.1 | async-start | bytes 4866048 | tf_op jit(solution)/shard_map/all_gather | solution.py:116
  81.1 473.2 %reduce-scatter.4.cloned.1.call-start = ((), (), s32[]{:S(2)}) async-start(), calls=%async_computation.3 | async-start | bytes 2228224
  81.4 64.0 %collective-permute-start.4 = (bf16[3,32,128]{2,1,0:T(8,128)(2,1)S(1)}, bf16[3,32,128]{2,1,0:T(8,128)(2,1)S(1)}, u32[]{:S(2)}, u32[]{:S(2)}) collective-permute-start(bf16[3,32,128]{2,1,0:T(8,128)(2,1)S(1)} %get-tuple-element.20), channel_id=1, source_target_pairs={{0,16},{16,32},{32,48},{48,64},{64,80},{80,96},{96,112},{112,128},... | collective-permute-start | bytes 73736 | tf_op jit(solution)/shard_map/ppermute | solution.py:17
  85.4 60.1 %collective-permute-start.5 = (bf16[3,32,128]{2,1,0:T(8,128)(2,1)S(1)}, bf16[3,32,128]{2,1,0:T(8,128)(2,1)S(1)}, u32[]{:S(2)}, u32[]{:S(2)}) collective-permute-start(bf16[3,32,128]{2,1,0:T(8,128)(2,1)S(1)} %get-tuple-element.21), channel_id=1, source_target_pairs={{16,0},{32,16},{48,32},{64,48},{80,64},{96,80},{112,96},{128,112},... | collective-permute-start | bytes 73736 | tf_op jit(solution)/shard_map/ppermute | solution.py:19
  405.5 8.0 %copy-start.2 = (bf16[8,64,2048]{2,1,0:T(8,128)(2,1)S(1)}, bf16[8,64,2048]{2,1,0:T(8,128)(2,1)}, u32[]{:S(2)}) copy-start(bf16[8,64,2048]{2,1,0:T(8,128)(2,1)} %param.19) | copy-start | bytes 6291460
  435.0 3.4 copy-start.14
  438.4 4.8 copy-start.4
  440.1 3.1 copy-start.15
  448.2 4.4 copy-start.3
  482.0 16.6 %copy-start.6 = (bf16[3,512,128]{2,1,0:T(8,128)(2,1)S(1)}, bf16[3,512,128]{2,1,0:T(8,128)(2,1)}, u32[]{:S(2)}) copy-start(bf16[3,512,128]{2,1,0:T(8,128)(2,1)} %copy-done.5) | copy-start | bytes 1179652
  482.0 74.4 %copy-start.1 = (bf16[3,512,128]{2,1,0:T(8,128)(2,1)S(1)}, bf16[3,512,128]{2,1,0:T(8,128)(2,1)}, u32[]{:S(2)}) copy-start(bf16[3,512,128]{2,1,0:T(8,128)(2,1)} %param.27) | copy-start | bytes 1179652
  488.8 8.3 %collective-permute-start.2 = (bf16[3,32,128]{2,1,0:T(8,128)(2,1)S(1)}, bf16[3,32,128]{2,1,0:T(8,128)(2,1)S(1)}, u32[]{:S(2)}, u32[]{:S(2)}) collective-permute-start(bf16[3,32,128]{2,1,0:T(8,128)(2,1)S(1)} %get-tuple-element.22), channel_id=1, source_target_pairs={{0,16},{16,32},{32,48},{48,64},{64,80},{80,96},{96,112},{112,128},... | collective-permute-start | bytes 73736 | tf_op jit(solution)/shard_map/ppermute | solution.py:17
  491.3 7.3 %collective-permute-start.3 = (bf16[3,32,128]{2,1,0:T(8,128)(2,1)S(1)}, bf16[3,32,128]{2,1,0:T(8,128)(2,1)S(1)}, u32[]{:S(2)}, u32[]{:S(2)}) collective-permute-start(bf16[3,32,128]{2,1,0:T(8,128)(2,1)S(1)} %get-tuple-element.23), channel_id=1, source_target_pairs={{16,0},{32,16},{48,32},{64,48},{80,64},{96,80},{112,96},{128,112},... | collective-permute-start | bytes 73736 | tf_op jit(solution)/shard_map/ppermute | solution.py:19
  (1 other events, 0.7 us)
Sparse Core Ops, SparseCore 0:
  60.9 169.4 all-gather.4
  234.1 162.5 all-gather.2
  488.6 65.6 reduce-scatter.3
where the time goes:
time: 564 us; the launch traced here: 563 us
  waiting for transfers between devices  300 us (53%)
  blocking collectives  113 us (20%)
  matrix products  67.5 us (12%)
  local copies, waits for them, and re-layouts  38.7 us (7%)
  starting transfers between devices  24.9 us (4%)
  between operations  14.9 us (3%)
    all_gather x1, waiting for transfers between devices, local(): lax.all_gather(values_tok, 'rows', axis=1, tiled=True)  160 us
    all_gather x1, waiting for transfers between devices, local(): lax.all_gather(keys_tok, 'rows', axis=1, tiled=True)  83.6 us
    unnamed x4, waiting for transfers between devices  54.7 us
    sub x3, matrix products, local(): grad_total = grad_total + prob_rows * (d_probs - delta)  25.7 us
    all_gather x1, blocking collectives, local(): lax.all_gather(w_key, 'samp', axis=0, tiled=True)  21.3 us
    all_gather x1, blocking collectives, local(): lax.all_gather(w_query, 'samp', axis=0, tiled=True)  19.8 us
    all_gather x1, blocking collectives, local(): lax.all_gather(w_value, 'samp', axis=0, tiled=True)  19.3 us
    all_gather x1, blocking collectives, local(): lax.all_gather(w_out, 'samp', axis=0, tiled=True)  19.2 us
  transfers between devices with their start and end apart: 9, of which 4 were waited for; matrix products, arithmetic and copies ran while one was open for 2% of the time, Pallas kernels for 0%

commit v1 on v0

v1 whole, which is shorter than its diff:
```python
import functools

import jax
import jax.numpy as jnp
from jax import lax
from jax.experimental import pallas as pl
from jax.experimental.pallas import tpu as pltpu
from jax.sharding import PartitionSpec as P

EPSILON = 1e-05
F32 = jnp.float32
BF16 = jnp.bfloat16
VMEM_BYTES = 56 * 1024 * 1024
WHOLE = pl.BlockSpec(memory_space=pltpu.VMEM)
SCALAR = pl.BlockSpec(memory_space=pltpu.SMEM)
ANY = pl.BlockSpec(memory_space=pl.ANY)


def dot(left, right):
    return lax.dot_general(left, right, (((1,), (0,)), ((), ())), preferred_element_type=F32)


def dot_nt(left, right):
    return lax.dot_general(left, right, (((1,), (1,)), ((), ())), preferred_element_type=F32)


def params():
    return pltpu.CompilerParams(vmem_limit_bytes=VMEM_BYTES)


def normalize(values):
    average = jnp.mean(values, axis=-1, keepdims=True)
    centered = values - average
    variance = jnp.mean(centered * centered, axis=-1, keepdims=True)
    inverse = lax.rsqrt(variance + EPSILON)
    return centered * inverse, inverse


def pool_kernel(count, token, noised, single, w_atom, d_out, hidden, own, left, right):
    samples, atoms, channels = noised.shape
    wide = own.shape[1] + left.shape[1] + right.shape[1]
    margin = left.shape[1]
    middle = own.shape[1]
    slot = lax.broadcasted_iota(jnp.int32, (wide, atoms), 1)
    line = lax.broadcasted_iota(jnp.int32, (wide, atoms), 0)
    picked = (line == token[...]) & (slot < count[0])
    one_hot = jnp.where(picked, 1.0, 0.0).astype(BF16)

    def put(index, sums):
        left[index] = sums[:margin]
        own[index] = sums[margin : margin + middle]
        right[index] = sums[margin + middle :]

    single_f = single[...].astype(F32)
    for s in range(samples):
        query = (noised[s].astype(F32) + single_f).astype(BF16)
        pre = dot(query, w_atom[...])
        value = (query.astype(F32) + pre / (1.0 + jnp.exp(-pre))).astype(BF16)
        hidden[s] = value
        put(s, dot(one_hot, value))
    put(samples, dot(one_hot, jnp.ones((atoms, channels), BF16)))
    for s in range(samples):
        put(samples + 1 + s, dot(one_hot, d_out[s]))


def settle_kernel(own, from_left, from_right, pooled, d_token):
    margin = from_left.shape[1]
    samples = (own.shape[0] - 1) // 2
    middle = own.shape[1]

    def settled(index):
        return jnp.concatenate(
            [own[index, :margin] + from_left[index], own[index, margin:] + from_right[index]], axis=0
        )

    scale = 1.0 / jnp.maximum(settled(samples), 1.0)
    for s in range(samples):
        pooled[s * middle : (s + 1) * middle] = (settled(s) * scale).astype(BF16)
        d_token[s * middle : (s + 1) * middle] = settled(samples + 1 + s).astype(BF16)


def prep_kernel(inner, t_ref, w_up, w_all, t_cent, base, w_cent, w_kv):
    @pl.when(pl.program_id(0) == 0)
    def _():
        up = w_up[...].astype(F32)
        cent = (up - jnp.mean(up, axis=-1, keepdims=True)).astype(BF16)
        w_cent[...] = cent
        w_kv[...] = dot(cent, w_all[:, inner : 3 * inner]).astype(BF16)

    t = t_ref[...].astype(F32)
    cent = (t - jnp.mean(t, axis=-1, keepdims=True)).astype(BF16)
    t_cent[...] = cent
    base[...] = dot(cent, w_all[:, inner : 3 * inner])


def attend_kernel(
    heads,
    factor,
    place,
    pooled_all,
    t_cent,
    base,
    w_cent,
    w_kv,
    pooled,
    t_own,
    w_up,
    w_all,
    w_out,
    bias_hbm,
    d_token,
    proj,
    keep,
    send,
    t_blk,
    base_blk,
    bias,
    kv,
    tokens_in,
    queries,
    scores,
    probs,
    mixed_full,
    inv_sum,
    mixed,
    d_mixed,
    t_sem,
    base_sem,
    bias_sem,
):
    blocks, samples, tok, channels = pooled_all.shape
    pairs = blocks // 2
    block = 2 * tok
    total = blocks * tok
    width = t_own.shape[1]
    inner = w_out.shape[0]
    head_dim = inner // heads
    half = heads // 2
    rows = half * tok
    span = 256
    starts = (0, inner - span)
    rank = place[0]
    core = place[1]

    def fetch(b):
        slot = lax.rem(b, 2)
        where = pl.ds(pl.multiple_of(b * block, block), block)
        return (
            pltpu.make_async_copy(t_cent.at[where], t_blk.at[slot], t_sem.at[slot]),
            pltpu.make_async_copy(base.at[where], base_blk.at[slot], base_sem.at[slot]),
        )

    bias_copy = pltpu.make_async_copy(bias_hbm, bias, bias_sem)
    for copy in fetch(0):
        copy.start()
    bias_copy.start()

    t_f = t_own[...].astype(F32)
    for s in range(samples):
        own_rows = slice(s * tok, (s + 1) * tok)
        tokens_in[own_rows] = dot(pooled[own_rows], w_up[...]) + t_f
    normed, _ = normalize(tokens_in[...])
    queries[...] = (dot(normed.astype(BF16), w_all[:, :inner]) * (head_dim**-0.5)).astype(BF16)

    def kv_step(b, carry):
        slot = lax.rem(b, 2)

        @pl.when(b + 1 < pairs)
        def _():
            for copy in fetch(b + 1):
                copy.start()

        for copy in fetch(b):
            copy.wait()
        owner = [lax.rem(rank + 2 * b + part, blocks) for part in range(2)]
        p = jnp.concatenate([pooled_all[o, s] for s in range(samples) for o in owner], axis=0)
        x = dot(p, w_cent[...])
        y = dot(p, w_kv[...])
        tb = t_blk[slot].astype(F32)
        bb = base_blk[slot]
        for s in range(samples):
            part = slice(s * block, (s + 1) * block)
            centered = x[part] + tb
            inverse = lax.rsqrt(jnp.sum(centered * centered, axis=-1, keepdims=True) / width + EPSILON)
            result = ((y[part] + bb) * inverse).astype(BF16)
            for i, o in enumerate(owner):
                kv[s, pl.ds(pl.multiple_of(o * tok, tok), tok), :] = result[i * tok : (i + 1) * tok]
        return carry

    lax.fori_loop(0, pairs, kv_step, 0)
    bias_copy.wait()

    lane_head = lax.broadcasted_iota(jnp.int32, (rows, span), 1)
    row_head = lax.broadcasted_iota(jnp.int32, (rows, span), 0) // tok

    def head_mask(g):
        lo = (row_head + g * half) * head_dim - starts[g]
        return (lane_head >= lo) & (lane_head < lo + head_dim)

    def spread(values, g):
        tile = values[:, starts[g] : starts[g] + span].astype(F32)
        return jnp.where(head_mask(g), jnp.concatenate([tile] * half, axis=0), 0.0)

    chunk = 512

    def forward(s, carry):
        own_rows = pl.ds(pl.multiple_of(s * tok, tok), tok)
        pieces = []
        for g in range(2):
            q = spread(queries[own_rows, :], g).astype(BF16)
            lanes = slice(starts[g], starts[g] + span)
            value_lanes = slice(inner + starts[g], inner + starts[g] + span)
            top = jnp.full((rows, 128), -jnp.inf, F32)
            for j in range(0, total, chunk):
                part = dot_nt(q, kv[s, j : j + chunk, lanes])
                part = part + bias[g * rows : (g + 1) * rows, j : j + chunk].astype(F32)
                scores[g, :, j : j + chunk] = part
                for c in range(0, chunk, 128):
                    top = jnp.maximum(top, part[:, c : c + 128])
            top = jnp.max(top, axis=-1, keepdims=True)
            amount = jnp.zeros((rows, 128), F32)
            out = jnp.zeros((rows, span), F32)
            for j in range(0, total, chunk):
                e = jnp.exp(scores[g, :, j : j + chunk] - top)
                for c in range(0, chunk, 128):
                    amount = amount + e[:, c : c + 128]
                e = e.astype(BF16)
                probs[s, g, :, j : j + chunk] = e
                out = out + dot(e, kv[s, j : j + chunk, value_lanes])
            inverse = 1.0 / jnp.sum(amount, axis=-1, keepdims=True)
            out = jnp.where(head_mask(g), out * inverse, 0.0)
            mixed_full[s, g] = out
            inv_sum[s, g] = jnp.broadcast_to(inverse, (rows, 128))
            piece = out[:tok]
            for h in range(1, half):
                piece = piece + out[h * tok : (h + 1) * tok]
            pieces.append(piece)
        cut = starts[1]
        mixed[own_rows, :cut] = pieces[0][:, :cut].astype(BF16)
        mixed[own_rows, cut:span] = (pieces[0][:, cut:] + pieces[1][:, : span - cut]).astype(BF16)
        mixed[own_rows, span:] = pieces[1][:, span - cut :].astype(BF16)
        return carry

    lax.fori_loop(0, samples, forward, 0)

    w_down = w_all[:, 3 * inner :]
    normed_out, inverse_out = normalize(tokens_in[...] + dot(mixed[...], w_out[...]))
    proj[...] = dot(normed_out.astype(BF16), w_down).astype(BF16)
    d_normed = dot_nt(d_token[...], w_down)
    first = jnp.mean(d_normed, axis=-1, keepdims=True)
    second = jnp.mean(d_normed * normed_out, axis=-1, keepdims=True)
    d_tokens = inverse_out * (d_normed - first - normed_out * second)
    d_mixed[...] = dot_nt(d_tokens.astype(BF16), w_out[...]).astype(BF16)

    for g in range(2):
        value_lanes = slice(inner + starts[g], inner + starts[g] + span)
        wide = []
        delta = []
        scale = []
        for s in range(samples):
            w = spread(d_mixed[s * tok : (s + 1) * tok, :], g)
            wide.append(w.astype(BF16))
            delta.append(jnp.sum(w * mixed_full[s, g], axis=-1, keepdims=True))
            scale.append(inv_sum[s, g][:, :1] * factor)

        def backward(k, carry):
            cols = pl.ds(pl.multiple_of(k * 256, 256), 256)
            grad = None
            for s in range(samples):
                d_prob = dot_nt(wide[s], kv[s, cols, value_lanes])
                term = probs[s, g, :, cols].astype(F32) * ((d_prob - delta[s]) * scale[s])
                grad = term if grad is None else grad + term
            low = grad[:, :128]
            high = grad[:, 128:]
            keep[k, g * rows : (g + 1) * rows, :] = jnp.where(core == 0, low, high).astype(BF16)
            send[k, g * rows : (g + 1) * rows, :] = jnp.where(core == 0, high, low).astype(BF16)
            return carry

        lax.fori_loop(0, total // 256, backward, 0)


def decode_kernel(count, token, hidden, proj, from_left, from_right, out):
    samples, atoms, channels = hidden.shape
    tok = proj.shape[1]
    wide = tok + 2 * from_left.shape[1]
    line = lax.broadcasted_iota(jnp.int32, (atoms, wide), 1)
    one_hot = jnp.where(line == token[...], 1.0, 0.0).astype(BF16)
    alive = lax.broadcasted_iota(jnp.int32, (atoms, channels), 0) < count[0]
    for s in range(samples):
        table = jnp.concatenate([from_left[s], proj[s], from_right[s]], axis=0)
        value = hidden[s].astype(F32) + dot(one_hot, table)
        out[s] = jnp.where(alive, value, 0.0).astype(BF16)


def local(
    atom_noised,
    atom_single,
    atom_token,
    atom_count,
    token_single,
    pair_bias,
    w_atom,
    w_up,
    w_query,
    w_key,
    w_value,
    w_out,
    w_down,
    d_atom_out,
):
    samples, atoms, channels = atom_noised.shape
    tok, width = token_single.shape
    margin = tok // 2
    heads, _, total = pair_bias.shape
    n_rows = lax.axis_size("rows")
    n_samp = lax.axis_size("samp")
    inner = w_query.shape[1]
    rank = lax.axis_index("rows")
    group = lax.axis_index("samp")
    chips = n_samp // 2

    fetched = []
    for part in range(2):
        perm = [
            ((r + 2 * s + part) % n_rows * n_samp + s, r * n_samp + s)
            for r in range(n_rows)
            for s in range(n_samp)
        ]
        fetched.append(lax.ppermute(token_single, ("rows", "samp"), perm))

    local_token = atom_token - (rank * tok - margin)
    shape = jax.ShapeDtypeStruct
    sums = 2 * samples + 1
    hidden, own, left, right = pl.pallas_call(
        pool_kernel,
        out_shape=(
            shape((samples, atoms, channels), BF16),
            shape((sums, tok, channels), F32),
            shape((sums, margin, channels), F32),
            shape((sums, margin, channels), F32),
        ),
        in_specs=[SCALAR] + [WHOLE] * 5,
        out_specs=(WHOLE,) * 4,
        compiler_params=params(),
        name="pool",
    )(atom_count, local_token[None, :], atom_noised, atom_single, w_atom, d_atom_out)
    up = [(i, i + 1) for i in range(n_rows - 1)]
    down = [(i + 1, i) for i in range(n_rows - 1)]
    from_left = lax.ppermute(right, "rows", up)
    from_right = lax.ppermute(left, "rows", down)
    pooled, d_token = pl.pallas_call(
        settle_kernel,
        out_shape=(shape((samples * tok, channels), BF16), shape((samples * tok, channels), BF16)),
        in_specs=[WHOLE] * 3,
        out_specs=(WHOLE,) * 2,
        compiler_params=params(),
        name="settle",
    )(own, from_left, from_right)
    pooled_all = lax.all_gather(pooled, "rows", axis=0, tiled=True)
    pooled_all = pooled_all.reshape(n_rows, samples, tok, channels)

    w_all = lax.all_gather(
        jnp.concatenate([w_query, w_key, w_value, w_down], axis=1), "samp", axis=0, tiled=True
    )
    w_two = lax.all_gather(jnp.concatenate([w_up, w_out], axis=0), "samp", axis=0, tiled=False)
    w_up_all = w_two[:, : w_up.shape[0]].reshape(-1, width)
    w_out_all = w_two[:, w_up.shape[0] :].reshape(-1, width)
    t_all = lax.all_gather(jnp.concatenate(fetched, axis=0), "samp", axis=0, tiled=True)

    block = 256
    t_cent, base, w_cent, w_kv = pl.pallas_call(
        functools.partial(prep_kernel, inner),
        grid=(total // block,),
        out_shape=(
            shape((total, width), BF16),
            shape((total, 2 * inner), F32),
            shape((channels, width), BF16),
            shape((channels, 2 * inner), BF16),
        ),
        in_specs=[
            pl.BlockSpec((block, width), lambda i: (i, 0)),
            pl.BlockSpec((channels, width), lambda i: (0, 0)),
            pl.BlockSpec(w_all.shape, lambda i: (0, 0)),
        ],
        out_specs=(
            pl.BlockSpec((block, width), lambda i: (i, 0)),
            pl.BlockSpec((block, 2 * inner), lambda i: (i, 0)),
            pl.BlockSpec((channels, width), lambda i: (0, 0)),
            pl.BlockSpec((channels, 2 * inner), lambda i: (0, 0)),
        ),
        compiler_params=params(),
        name="prep",
    )(t_all, w_up_all, w_all)

    place = jnp.stack([rank, group % 2]).astype(jnp.int32)
    factor = total / (samples * n_samp)
    rows = heads // 2 * tok
    proj, keep, send = pl.pallas_call(
        functools.partial(attend_kernel, heads, factor),
        out_shape=(
            shape((samples * tok, channels), BF16),
            shape((chips, heads * tok, 128), BF16),
            shape((chips, heads * tok, 128), BF16),
        ),
        in_specs=[SCALAR, WHOLE, ANY, ANY] + [WHOLE] * 7 + [ANY, WHOLE],
        out_specs=(WHOLE,) * 3,
        scratch_shapes=[
            pltpu.VMEM((2, 2 * tok, width), BF16),
            pltpu.VMEM((2, 2 * tok, 2 * inner), F32),
            pltpu.VMEM((heads * tok, total), BF16),
            pltpu.VMEM((samples, total, 2 * inner), BF16),
            pltpu.VMEM((samples * tok, width), F32),
            pltpu.VMEM((samples * tok, inner), BF16),
            pltpu.VMEM((2, rows, total), F32),
            pltpu.VMEM((samples, 2, rows, total), BF16),
            pltpu.VMEM((samples, 2, rows, 256), F32),
            pltpu.VMEM((samples, 2, rows, 128), F32),
            pltpu.VMEM((samples * tok, inner), BF16),
            pltpu.VMEM((samples * tok, inner), BF16),
            pltpu.SemaphoreType.DMA((2,)),
            pltpu.SemaphoreType.DMA((2,)),
            pltpu.SemaphoreType.DMA,
        ],
        compiler_params=params(),
        name="attend",
    )(
        place,
        pooled_all,
        t_cent,
        base,
        w_cent,
        w_kv,
        pooled,
        token_single,
        w_up_all,
        w_all,
        w_out_all,
        pair_bias.reshape(heads * tok, total),
        d_token,
    )

    swap = [(s, s ^ 1) for s in range(n_samp)]
    other = lax.ppermute(send, "samp", swap)
    both = (keep.astype(F32) + other.astype(F32)).astype(BF16)
    sets = [[2 * m + c for m in range(chips)] for c in range(2)]
    shares = lax.all_to_all(both, "samp", 0, 0, axis_index_groups=sets, tiled=True)
    bias_grad = jnp.sum(shares.astype(F32), axis=0).reshape(heads, tok, 128)

    proj = proj.reshape(samples, tok, channels)
    proj_left = lax.ppermute(proj[:, margin:], "rows", up)
    proj_right = lax.ppermute(proj[:, :margin], "rows", down)
    atom_out = pl.pallas_call(
        decode_kernel,
        out_shape=shape((samples, atoms, channels), BF16),
        in_specs=[SCALAR] + [WHOLE] * 5,
        out_specs=WHOLE,
        compiler_params=params(),
        name="decode",
    )(atom_count, local_token[:, None], hidden, proj, proj_left, proj_right)
    return (atom_out, bias_grad)


def solution(mesh):
    placed = (
        P("samp", "rows", None),
        P("rows", None),
        P("rows"),
        P("rows"),
        P("rows", None),
        P(None, "rows", None),
        P(),
        P("samp", None),
        P("samp", None),
        P("samp", None),
        P("samp", None),
        P("samp", None),
        P("samp", None),
        P("samp", "rows", None),
    )
    return jax.shard_map(
        local,
        mesh=mesh,
        in_specs=placed,
        out_specs=(P("samp", "rows", None), P(None, "rows", "samp")),
        check_vma=False,
    )
```

time: 564 us -> 329 us (0.58)
  the two profiles are of different devices: /device:TPU:32 before, /device:TPU:37 now
where the time goes in v1:
time: 329 us; the launch traced here: 328 us
  waiting for transfers between devices  176 us (53%)
  starting transfers between devices  53.4 us (16%)
  Pallas kernels  48.9 us (15%)
  blocking collectives  23.9 us (7%)
  between operations  14.5 us (4%)
  other arithmetic  7.44 us (2%)
  local copies, waits for them, and re-layouts  3.68 us (1%)
    all_gather x1, waiting for transfers between devices, local(): pooled_all = lax.all_gather(pooled, 'rows', axis=0, tiled=True)  131 us
    pallas_call x1, Pallas kernels, local(): pl.pallas_call(functools.partial(attend_kernel, heads, factor), out_shape...  32.5 us
    all_gather x1, blocking collectives, local(): lax.all_gather(jnp.concatenate([w_up, w_out], axis=0), 'samp', axis=0, ti...  23.9 us
    ppermute x2, starting transfers between devices, local(): fetched.append(lax.ppermute(token_single, ('rows', 'samp'), perm))  21.6 us
    all_gather x1, waiting for transfers between devices, local(): lax.all_gather(jnp.concatenate(fetched, axis=0), 'samp', axis=0, tiled=True)  15 us
    ppermute x2, waiting for transfers between devices, local(): fetched.append(lax.ppermute(token_single, ('rows', 'samp'), perm))  14.5 us
    ppermute x1, starting transfers between devices, local(): other = lax.ppermute(send, 'samp', swap)  12 us
    pallas_call x1, Pallas kernels, local(): pl.pallas_call(functools.partial(prep_kernel, inner), grid=(total // bloc...  9.89 us
  transfers between devices with their start and end apart: 11, of which 8 were waited for; matrix products, arithmetic and copies ran while one was open for 2% of the time, Pallas kernels for 5%

profile of v1, /device:TPU:37, one launch (start us, length us, event | category | flops | bytes accessed | tf_op | source)
XLA Modules:
  0.0 327.9 jit_solution(14033692267039260372)
XLA Ops:
  7.2 1.5 pad_maximum_fusion.1
  8.8 14.1 %collective-permute-start.2 = (bf16[64,768]{1,0:T(8,128)(2,1)}, bf16[64,768]{1,0:T(8,128)(2,1)S(1)}, u32[]{:S(2)}, u32[]{:S(2)}) collective-permute-start(bf16[64,768]{1,0:T(8,128)(2,1)} %t_own.1), channel_id=1, source_target_pairs={{0,0},{33,1},{66,2},{99,3},{132,4},{165,5},{198,6},{231,7},{264,8}... | collective-permute-start | bytes 294920 | tf_op jit(solution)/shard_map/ppermute | solution.py:329
  22.9 7.6 %collective-permute-start.3 = (bf16[64,768]{1,0:T(8,128)(2,1)}, bf16[64,768]{1,0:T(8,128)(2,1)S(1)}, u32[]{:S(2)}, u32[]{:S(2)}) collective-permute-start(bf16[64,768]{1,0:T(8,128)(2,1)} %t_own.1), channel_id=1, source_target_pairs={{16,0},{49,1},{82,2},{115,3},{148,4},{181,5},{214,6},{247,7},{280,... | collective-permute-start | bytes 294920 | tf_op jit(solution)/shard_map/ppermute | solution.py:329
  30.5 14.5 %collective-permute-done.3 = bf16[64,768]{1,0:T(8,128)(2,1)S(1)} collective-permute-done((bf16[64,768]{1,0:T(8,128)(2,1)}, bf16[64,768]{1,0:T(8,128)(2,1)S(1)}, u32[]{:S(2)}, u32[]{:S(2)}) %collective-permute-start.3) | collective-permute-done | bytes 98336 | tf_op jit(solution)/shard_map/ppermute | solution.py:329
  46.4 1.2 broadcast_subtract_fusion
  47.6 2.7 pool.1
  50.3 5.4 %collective-permute-start = (f32[7,32,128]{2,1,0:T(8,128)}, f32[7,32,128]{2,1,0:T(8,128)S(1)}, u32[]{:S(2)}, u32[]{:S(2)}) collective-permute-start(f32[7,32,128]{2,1,0:T(8,128)} %get-tuple-element.17), channel_id=1, source_target_pairs={{0,16},{16,32},{32,48},{48,64},{64,80},{80,96},{96,112},{112,128},... | collective-permute-start | bytes 344072 | tf_op jit(solution)/shard_map/ppermute | solution.py:349
  55.6 2.3 collective-permute-start.1
  58.8 5.4 %collective-permute-done.1.from_right = f32[7,32,128]{2,1,0:T(8,128)S(1)} collective-permute-done((f32[7,32,128]{2,1,0:T(8,128)}, f32[7,32,128]{2,1,0:T(8,128)S(1)}, u32[]{:S(2)}, u32[]{:S(2)}) %collective-permute-start.1) | collective-permute-done | bytes 114720 | tf_op jit(solution)/shard_map/ppermute | solution.py:350
  64.9 1.7 settle.1
  66.7 23.9 %all-gather = bf16[512,768]{1,0:T(8,128)(2,1)S(1)} all-gather(bf16[32,768]{1,0:T(8,128)(2,1)S(1)} %pad_maximum_fusion.2), channel_id=2, replica_groups=mesh['rows'=32,'samp'=16] {'samp'}, dimensions={0}, use_global_device_ids=true | all-gather | bytes 835584 | tf_op jit(solution)/shard_map/all_gather | solution.py:365
  92.8 15.0 %all-gather.7.cloned.1.call-done.t_ref = bf16[2048,768]{1,0:T(8,128)(2,1)} async-done(((bf16[128,768]{1,0:T(8,128)(2,1)}), bf16[2048,768]{1,0:T(8,128)(2,1)}) %all-gather.7.cloned.1.call-update) | async-done | bytes 3145744 | tf_op jit(solution)/shard_map/all_gather | solution.py:368
  107.8 9.9 %prep.1 = (bf16[2048,768]{1,0:T(8,128)(2,1)}, f32[2048,768]{1,0:T(8,128)}, bf16[128,768]{1,0:T(8,128)(2,1)}, bf16[128,768]{1,0:T(8,128)(2,1)}) custom-call(bf16[2048,768]{1,0:T(8,128)(2,1)} %all-gather.7.cloned.1.call-done.t_ref, bf16[128,768]{1,0:T(8,128)(2,1)} %slice_bitcast_fusion.w_up, bf16[768,1280]{1,0:T(8,128)(2,1)} %all-gather.9.cloned.1.call-done.w_all), custom_call_target="tpu_custom_call" | custom-call | tf_op jit(solution)/shard_map/prep/pallas_call | solution.py:371
  117.7 130.9 %all-gather.5.cloned.1.call-done = bf16[6144,128]{1,0:T(8,128)(2,1)} async-done(((bf16[192,128]{1,0:T(8,128)(2,1)}), bf16[6144,128]{1,0:T(8,128)(2,1)}) %all-gather.5.cloned.1.call-update) | async-done | bytes 1572880 | tf_op jit(solution)/shard_map/all_gather | solution.py:359
  248.6 32.5 %attend.1 = (bf16[192,128]{1,0:T(8,128)(2,1)}, bf16[8,512,128]{2,1,0:T(8,128)(2,1)}, bf16[8,512,128]{2,1,0:T(8,128)(2,1)}) custom-call(s32[2]{0:T(128)} %pad_add_fusion.place, bf16[32,3,64,128]{3,2,1,0:T(8,128)(2,1)} %bitcast.16, bf16[2048,768]{1,0:T(8,128)(2,1)} %get-tuple-element.20.t_cent, f32[2048,768]{1,0:T(8,128)} %get-tuple-element.21.base, ...), custom_call_target="tpu_custom_call" | custom-call | tf_op jit(solution)/shard_map/attend/pallas_call | solution.py:398
  281.1 12.0 %collective-permute-start.6 = (bf16[8,512,128]{2,1,0:T(8,128)(2,1)}, bf16[8,512,128]{2,1,0:T(8,128)(2,1)S(1)}, u32[]{:S(2)}, u32[]{:S(2)}) collective-permute-start(bf16[8,512,128]{2,1,0:T(8,128)(2,1)} %get-tuple-element.27), channel_id=1, source_target_pairs={{0,1},{1,0},{2,3},{3,2},{4,5},{5,4},{6,7},{7,6},{8,9},{9,8},{10,11... | collective-permute-start | bytes 3145736 | tf_op jit(solution)/shard_map/ppermute | solution.py:443
  293.1 2.5 collective-permute-done.6
  295.5 2.5 add_convert_fusion
  298.1 4.3 %all-to-all-start = ((bf16[8,512,128]{2,1,0:T(8,128)(2,1)}), bf16[8,512,128]{2,1,0:T(8,128)(2,1)S(1)}, u32[]{:S(2)}, u32[]{:S(2)}) async-start(bf16[8,512,128]{2,1,0:T(8,128)(2,1)} %add_convert_fusion), calls=%async_computation | async-start | bytes 2097152 | tf_op jit(solution)/shard_map/all_to_all | solution.py:446
  302.3 3.7 %collective-permute-start.4 = (bf16[3,32,128]{2,1,0:T(8,128)(2,1)S(1)}, bf16[3,32,128]{2,1,0:T(8,128)(2,1)S(1)}, u32[]{:S(2)}, u32[]{:S(2)}) collective-permute-start(bf16[3,32,128]{2,1,0:T(8,128)(2,1)S(1)} %get-tuple-element.29), channel_id=1, source_target_pairs={{0,16},{16,32},{32,48},{48,64},{64,80},{80,96},{96,112},{112,128},... | collective-permute-start | bytes 73736 | tf_op jit(solution)/shard_map/ppermute | solution.py:450
  306.0 4.0 %collective-permute-start.5 = (bf16[3,32,128]{2,1,0:T(8,128)(2,1)S(1)}, bf16[3,32,128]{2,1,0:T(8,128)(2,1)S(1)}, u32[]{:S(2)}, u32[]{:S(2)}) collective-permute-start(bf16[3,32,128]{2,1,0:T(8,128)(2,1)S(1)} %get-tuple-element.28), channel_id=1, source_target_pairs={{16,0},{32,16},{48,32},{64,48},{80,64},{96,80},{112,96},{128,112},... | collective-permute-start | bytes 73736 | tf_op jit(solution)/shard_map/ppermute | solution.py:451
  310.9 4.3 %collective-permute-done.4.from_left = bf16[3,32,128]{2,1,0:T(8,128)(2,1)S(1)} collective-permute-done((bf16[3,32,128]{2,1,0:T(8,128)(2,1)S(1)}, bf16[3,32,128]{2,1,0:T(8,128)(2,1)S(1)}, u32[]{:S(2)}, u32[]{:S(2)}) %collective-permute-start.4) | collective-permute-done | bytes 24608 | tf_op jit(solution)/shard_map/ppermute | solution.py:450
  315.2 2.5 collective-permute-done.5.from_right
  318.3 2.2 decode.1
  (34 shorter events, 6.9 us)
Async XLA Ops:
  7.2 59.5 %copy-start.7 = (bf16[8,768]{1,0:T(8,128)(2,1)S(1)}, bf16[8,768]{1,0:T(8,128)(2,1)}, u32[]{:S(2)}) copy-start(bf16[8,768]{1,0:T(8,128)(2,1)} %param.21) | copy-start | bytes 36868
  7.2 59.5 %copy-start.3 = (bf16[24,768]{1,0:T(8,128)(2,1)S(1)}, bf16[24,768]{1,0:T(8,128)(2,1)}, u32[]{:S(2)}) copy-start(bf16[24,768]{1,0:T(8,128)(2,1)} %param.25) | copy-start | bytes 110596
  7.2 85.6 %all-gather.9.cloned.1.call-start = ((), (), s32[]{:S(2)}) async-start(), calls=%async_computation.3 | async-start | bytes 2088960 | tf_op jit(solution)/shard_map/all_gather | solution.py:362
  8.7 99.1 %all-gather.7.cloned.1.call-start = ((), (), s32[]{:S(2)}) async-start(), calls=%async_computation.2 | async-start | bytes 3342336 | tf_op jit(solution)/shard_map/all_gather | solution.py:368
  8.8 21.7 %collective-permute-start.2 = (bf16[64,768]{1,0:T(8,128)(2,1)}, bf16[64,768]{1,0:T(8,128)(2,1)S(1)}, u32[]{:S(2)}, u32[]{:S(2)}) collective-permute-start(bf16[64,768]{1,0:T(8,128)(2,1)} %t_own.1), channel_id=1, source_target_pairs={{0,0},{33,1},{66,2},{99,3},{132,4},{165,5},{198,6},{231,7},{264,8}... | collective-permute-start | bytes 294920 | tf_op jit(solution)/shard_map/ppermute | solution.py:329
  22.9 22.0 %collective-permute-start.3 = (bf16[64,768]{1,0:T(8,128)(2,1)}, bf16[64,768]{1,0:T(8,128)(2,1)S(1)}, u32[]{:S(2)}, u32[]{:S(2)}) collective-permute-start(bf16[64,768]{1,0:T(8,128)(2,1)} %t_own.1), channel_id=1, source_target_pairs={{16,0},{49,1},{82,2},{115,3},{148,4},{181,5},{214,6},{247,7},{280,... | collective-permute-start | bytes 294920 | tf_op jit(solution)/shard_map/ppermute | solution.py:329
  45.6 202.9 %all-gather.5.cloned.1.call-start = ((), (), s32[]{:S(2)}) async-start(), calls=%async_computation.1 | async-start | bytes 1622016 | tf_op jit(solution)/shard_map/all_gather | solution.py:359
  50.3 8.5 %collective-permute-start = (f32[7,32,128]{2,1,0:T(8,128)}, f32[7,32,128]{2,1,0:T(8,128)S(1)}, u32[]{:S(2)}, u32[]{:S(2)}) collective-permute-start(f32[7,32,128]{2,1,0:T(8,128)} %get-tuple-element.17), channel_id=1, source_target_pairs={{0,16},{16,32},{32,48},{48,64},{64,80},{80,96},{96,112},{112,128},... | collective-permute-start | bytes 344072 | tf_op jit(solution)/shard_map/ppermute | solution.py:349
  55.6 8.6 %collective-permute-start.1 = (f32[7,32,128]{2,1,0:T(8,128)}, f32[7,32,128]{2,1,0:T(8,128)S(1)}, u32[]{:S(2)}, u32[]{:S(2)}) collective-permute-start(f32[7,32,128]{2,1,0:T(8,128)} %get-tuple-element.18), channel_id=1, source_target_pairs={{16,0},{32,16},{48,32},{64,48},{80,64},{96,80},{112,96},{128,112},... | collective-permute-start | bytes 344072 | tf_op jit(solution)/shard_map/ppermute | solution.py:350
  58.8 5.4 %copy-start.1 = (f32[7,32,128]{2,1,0:T(8,128)}, f32[7,32,128]{2,1,0:T(8,128)S(1)}, u32[]{:S(2)}) copy-start(f32[7,32,128]{2,1,0:T(8,128)S(1)} %collective-permute-done.from_left) | copy-start | bytes 344068
  64.2 0.6 copy-start.2
  281.1 14.5 %collective-permute-start.6 = (bf16[8,512,128]{2,1,0:T(8,128)(2,1)}, bf16[8,512,128]{2,1,0:T(8,128)(2,1)S(1)}, u32[]{:S(2)}, u32[]{:S(2)}) collective-permute-start(bf16[8,512,128]{2,1,0:T(8,128)(2,1)} %get-tuple-element.27), channel_id=1, source_target_pairs={{0,1},{1,0},{2,3},{3,2},{4,5},{5,4},{6,7},{7,6},{8,9},{9,8},{10,11... | collective-permute-start | bytes 3145736 | tf_op jit(solution)/shard_map/ppermute | solution.py:443
  295.5 6.8 %copy-start = (bf16[192,128]{1,0:T(8,128)(2,1)S(1)}, bf16[192,128]{1,0:T(8,128)(2,1)}, u32[]{:S(2)}) copy-start(bf16[192,128]{1,0:T(8,128)(2,1)} %get-tuple-element.25) | copy-start | bytes 147460
  295.5 14.5 %copy-start.6 = (s32[512]{0:T(512)S(1)}, s32[512]{0:T(512)}, u32[]{:S(2)}) copy-start(s32[512]{0:T(512)} %broadcast_subtract_fusion) | copy-start | bytes 6148
  298.1 22.4 %all-to-all-start = ((bf16[8,512,128]{2,1,0:T(8,128)(2,1)}), bf16[8,512,128]{2,1,0:T(8,128)(2,1)S(1)}, u32[]{:S(2)}, u32[]{:S(2)}) async-start(bf16[8,512,128]{2,1,0:T(8,128)(2,1)} %add_convert_fusion), calls=%async_computation | async-start | bytes 2097152 | tf_op jit(solution)/shard_map/all_to_all | solution.py:446
  302.3 12.9 %collective-permute-start.4 = (bf16[3,32,128]{2,1,0:T(8,128)(2,1)S(1)}, bf16[3,32,128]{2,1,0:T(8,128)(2,1)S(1)}, u32[]{:S(2)}, u32[]{:S(2)}) collective-permute-start(bf16[3,32,128]{2,1,0:T(8,128)(2,1)S(1)} %get-tuple-element.29), channel_id=1, source_target_pairs={{0,16},{16,32},{32,48},{48,64},{64,80},{80,96},{96,112},{112,128},... | collective-permute-start | bytes 73736 | tf_op jit(solution)/shard_map/ppermute | solution.py:450
  306.0 11.7 %collective-permute-start.5 = (bf16[3,32,128]{2,1,0:T(8,128)(2,1)S(1)}, bf16[3,32,128]{2,1,0:T(8,128)(2,1)S(1)}, u32[]{:S(2)}, u32[]{:S(2)}) collective-permute-start(bf16[3,32,128]{2,1,0:T(8,128)(2,1)S(1)} %get-tuple-element.28), channel_id=1, source_target_pairs={{16,0},{32,16},{48,32},{64,48},{80,64},{96,80},{112,96},{128,112},... | collective-permute-start | bytes 73736 | tf_op jit(solution)/shard_map/ppermute | solution.py:451
  315.2 2.5 copy-start.4
  317.7 0.6 copy-start.5
Sparse Core Ops, SparseCore 0:
  10.2 46.2 all-gather.8
  59.1 48.6 all-gather.6
  110.9 137.6 all-gather.4

commit v2 on v1

--- a/solution.py
+++ b/solution.py
@@ -79,116 +79,200 @@
         d_token[s * middle : (s + 1) * middle] = settled(samples + 1 + s).astype(BF16)
 
 
-def prep_kernel(inner, t_ref, w_up, w_all, t_cent, base, w_cent, w_kv):
-    @pl.when(pl.program_id(0) == 0)
+def prep_kernel(splits, t_mine, t_other, w_up, w_got, base, extra, w_mix):
+    step = pl.program_id(0)
+    inner = w_got.shape[2] // 2
+    depth = w_got.shape[0] * w_got.shape[1] * 3 // 8
+    width = w_up.shape[1]
+    channels = w_up.shape[0]
+    cut = w_got.shape[1] * 3 // 8
+    w_key = w_got[:, :cut, inner:].reshape(depth, inner)
+    w_value = w_got[:, cut : 2 * cut, :inner].reshape(depth, inner)
+    up = w_up[...].astype(F32)
+    up = (up - jnp.mean(up, axis=-1, keepdims=True)).astype(BF16)
+
+    @pl.when(step == 0)
     def _():
-        up = w_up[...].astype(F32)
-        cent = (up - jnp.mean(up, axis=-1, keepdims=True)).astype(BF16)
-        w_cent[...] = cent
-        w_kv[...] = dot(cent, w_all[:, inner : 3 * inner]).astype(BF16)
-
-    t = t_ref[...].astype(F32)
-    cent = (t - jnp.mean(t, axis=-1, keepdims=True)).astype(BF16)
-    t_cent[...] = cent
-    base[...] = dot(cent, w_all[:, inner : 3 * inner])
+        w_mix[:, :inner] = dot(up, w_key).astype(BF16)
+        w_mix[:, inner : 2 * inner] = dot(up, w_value).astype(BF16)
+        gram = dot_nt(up, up) * (1.0 / width)
+        high = gram.astype(BF16)
+        w_mix[:, 2 * inner : 2 * inner + channels] = high
+        w_mix[:, 2 * inner + channels :] = (gram - high.astype(F32)).astype(BF16)
+
+    def work(t_ref):
+        t = t_ref[...].astype(F32)
+        cent = (t - jnp.mean(t, axis=-1, keepdims=True)).astype(BF16)
+        base[:, :inner] = dot(cent, w_key).astype(BF16)
+        base[:, inner:] = dot(cent, w_value).astype(BF16)
+        extra[:, :channels] = dot_nt(cent, up) * (2.0 / width)
+        wide = cent.astype(F32)
+        square = jnp.sum(wide * wide, axis=-1, keepdims=True) * (1.0 / width)
+        extra[:, channels:] = jnp.broadcast_to(square, (t.shape[0], channels))
+
+    @pl.when(step < splits)
+    def _():
+        work(t_mine)
+
+    @pl.when(step >= splits)
+    def _():
+        work(t_other)
+
+
+def key_value(tables, bases, extras, w_mix):
+    lines, channels = tables[0].shape
+    tok, deep = bases[0].shape
+    repeat = lines // tok
+    y_all = dot(jnp.concatenate(tables, axis=0), w_mix)
+    results = []
+    for i, (p, base, extra) in enumerate(zip(tables, bases, extras)):
+        y = y_all[i * lines : (i + 1) * lines]
+        gram = y[:, deep : deep + channels] + y[:, deep + channels :]
+        cross = jnp.concatenate([extra[:, :channels]] * repeat, axis=0)
+        square = jnp.concatenate([extra[:, channels : channels + 1]] * repeat, axis=0)
+        variance = jnp.sum(p.astype(F32) * (gram + cross), axis=-1, keepdims=True) + square
+        inverse = lax.rsqrt(jnp.maximum(variance, 0.0) + EPSILON)
+        tiled = jnp.concatenate([base.astype(F32)] * repeat, axis=0)
+        results.append(((y[:, :deep] + tiled) * inverse).astype(BF16))
+    return results
+
+
+def source(position, core, half):
+    own = position < half
+    return jnp.where(own, 2 * position + core, 2 * (position - half) + 1 - core)
+
+
+def half_kernel(
+    head_dim,
+    place,
+    pooled_z,
+    base,
+    extra,
+    w_mix,
+    pooled,
+    t_own,
+    w_up,
+    w_got,
+    d_token,
+    kv,
+    tokens_in,
+    queries,
+    d_normed,
+):
+    blocks, lines, channels = pooled_z.shape
+    samples, _, tok, _ = kv.shape
+    inner = w_got.shape[2] // 2
+    cut = w_got.shape[1] * 3 // 8
+    depth = w_got.shape[0] * cut
+    w_query = w_got[:, :cut, :inner].reshape(depth, inner)
+    w_down = w_got[:, cut : 2 * cut, inner : inner + channels].reshape(depth, channels)
+    t_f = t_own[...].astype(F32)
+    for s in range(samples):
+        own_rows = slice(s * tok, (s + 1) * tok)
+        tokens_in[own_rows] = dot(pooled[own_rows], w_up[...]) + t_f
+    normed, _ = normalize(tokens_in[...])
+    queries[...] = (dot(normed.astype(BF16), w_query) * (head_dim**-0.5)).astype(BF16)
+    d_normed[...] = dot_nt(d_token[...], w_down)
+
+    def step(i, carry):
+        which = (2 * i, 2 * i + 1)
+        at = [lax.rem(place[0] + source(b, place[2], blocks // 2), blocks) for b in which]
+        results = key_value(
+            [pooled_z[z] for z in at], [base[b, 0] for b in which], [extra[b, 0] for b in which], w_mix[...]
+        )
+        for z, result in zip(at, results):
+            for s in range(samples):
+                kv[s, z] = result[s * tok : (s + 1) * tok]
+        return carry
+
+    lax.fori_loop(0, blocks // 2, step, 0)
 
 
 def attend_kernel(
     heads,
     factor,
     place,
-    pooled_all,
-    t_cent,
-    base,
-    w_cent,
-    w_kv,
-    pooled,
-    t_own,
-    w_up,
-    w_all,
+    pooled_y,
+    w_mix,
+    base_hbm,
+    extra_hbm,
+    kv_hbm,
+    tokens_in,
+    queries,
+    d_normed,
+    w_down,
     w_out,
     bias_hbm,
-    d_token,
     proj,
     keep,
     send,
-    t_blk,
-    base_blk,
+    base,
+    extra,
+    kv,
     bias,
-    kv,
-    tokens_in,
-    queries,
     scores,
     probs,
     mixed_full,
     inv_sum,
     mixed,
     d_mixed,
-    t_sem,
-    base_sem,
-    bias_sem,
+    sems,
 ):
-    blocks, samples, tok, channels = pooled_all.shape
-    pairs = blocks // 2
-    block = 2 * tok
-    total = blocks * tok
-    width = t_own.shape[1]
-    inner = w_out.shape[0]
+    blocks, lines, channels = pooled_y.shape
+    samples, _, _, tok, deep = kv.shape
+    total = 2 * blocks * tok
+    inner = deep // 2
     head_dim = inner // heads
     half = heads // 2
     rows = half * tok
     span = 256
     starts = (0, inner - span)
-    rank = place[0]
-    core = place[1]
-
-    def fetch(b):
-        slot = lax.rem(b, 2)
-        where = pl.ds(pl.multiple_of(b * block, block), block)
-        return (
-            pltpu.make_async_copy(t_cent.at[where], t_blk.at[slot], t_sem.at[slot]),
-            pltpu.make_async_copy(base.at[where], base_blk.at[slot], base_sem.at[slot]),
+    first_z = place[0]
+    high = place[1]
+    core = place[2]
+    pieces_in = min(4, blocks // 2)
+    run = blocks // pieces_in
+
+    copies = []
+    for piece in range(pieces_in):
+        part = pl.ds(piece * run, run)
+        copies.append(
+            (
+                pltpu.make_async_copy(base_hbm.at[part, 1], base.at[part], sems.at[2 * piece]),
+                pltpu.make_async_copy(extra_hbm.at[part, 1], extra.at[part], sems.at[2 * piece + 1]),
+            )
         )
-
-    bias_copy = pltpu.make_async_copy(bias_hbm, bias, bias_sem)
-    for copy in fetch(0):
+    bias_copy = pltpu.make_async_copy(bias_hbm, bias, sems.at[2 * pieces_in])
+    kv_copies = [
+        pltpu.make_async_copy(kv_hbm.at[s], kv.at[s, :, high], sems.at[2 * pieces_in + 1 + s])
+        for s in range(samples)
+    ]
+    for pair in copies:
+        for copy in pair:
+            copy.start()
+    bias_copy.start()
+    for copy in kv_copies:
         copy.start()
-    bias_copy.start()
-
-    t_f = t_own[...].astype(F32)
-    for s in range(samples):
-        own_rows = slice(s * tok, (s + 1) * tok)
-        tokens_in[own_rows] = dot(pooled[own_rows], w_up[...]) + t_f
-    normed, _ = normalize(tokens_in[...])
-    queries[...] = (dot(normed.astype(BF16), w_all[:, :inner]) * (head_dim**-0.5)).astype(BF16)
-
-    def kv_step(b, carry):
-        slot = lax.rem(b, 2)
-
-        @pl.when(b + 1 < pairs)
-        def _():
-            for copy in fetch(b + 1):
-                copy.start()
-
-        for copy in fetch(b):
+
+    for piece in range(pieces_in):
+        for copy in copies[piece]:
             copy.wait()
-        owner = [lax.rem(rank + 2 * b + part, blocks) for part in range(2)]
-        p = jnp.concatenate([pooled_all[o, s] for s in range(samples) for o in owner], axis=0)
-        x = dot(p, w_cent[...])
-        y = dot(p, w_kv[...])
-        tb = t_blk[slot].astype(F32)
-        bb = base_blk[slot]
-        for s in range(samples):
-            part = slice(s * block, (s + 1) * block)
-            centered = x[part] + tb
-            inverse = lax.rsqrt(jnp.sum(centered * centered, axis=-1, keepdims=True) / width + EPSILON)
-            result = ((y[part] + bb) * inverse).astype(BF16)
-            for i, o in enumerate(owner):
-                kv[s, pl.ds(pl.multiple_of(o * tok, tok), tok), :] = result[i * tok : (i + 1) * tok]
-        return carry
-
-    lax.fori_loop(0, pairs, kv_step, 0)
+
+        def step(i, carry):
+            which = (2 * i, 2 * i + 1)
+            at = [lax.rem(first_z + source(b, core, blocks // 2) + high, blocks) for b in which]
+            results = key_value(
+                [pooled_y[z] for z in at], [base[b] for b in which], [extra[b] for b in which], w_mix[...]
+            )
+            for z, result in zip(at, results):
+                for s in range(samples):
+                    kv[s, z, 1 - high] = result[s * tok : (s + 1) * tok]
+            return carry
+
+        lax.fori_loop(piece * run // 2, (piece + 1) * run // 2, step, 0)
     bias_copy.wait()
+    for copy in kv_copies:
+        copy.wait()
 
     lane_head = lax.broadcasted_iota(jnp.int32, (rows, span), 1)
     row_head = lax.broadcasted_iota(jnp.int32, (rows, span), 0) // tok
@@ -202,6 +286,9 @@
         return jnp.where(head_mask(g), jnp.concatenate([tile] * half, axis=0), 0.0)
 
     chunk = 512
+
+    def keys(s, start, count, lanes):
+        return kv[s, pl.ds(start // (2 * tok), count // (2 * tok)), :, :, lanes].reshape(count, span)
 
     def forward(s, carry):
         own_rows = pl.ds(pl.multiple_of(s * tok, tok), tok)
@@ -212,7 +299,7 @@
             value_lanes = slice(inner + starts[g], inner + starts[g] + span)
             top = jnp.full((rows, 128), -jnp.inf, F32)
             for j in range(0, total, chunk):
-                part = dot_nt(q, kv[s, j : j + chunk, lanes])
+                part = dot_nt(q, keys(s, j, chunk, lanes))
                 part = part + bias[g * rows : (g + 1) * rows, j : j + chunk].astype(F32)
                 scores[g, :, j : j + chunk] = part
                 for c in range(0, chunk, 128):
@@ -226,7 +313,7 @@
                     amount = amount + e[:, c : c + 128]
                 e = e.astype(BF16)
                 probs[s, g, :, j : j + chunk] = e
-                out = out + dot(e, kv[s, j : j + chunk, value_lanes])
+                out = out + dot(e, keys(s, j, chunk, value_lanes))
             inverse = 1.0 / jnp.sum(amount, axis=-1, keepdims=True)
             out = jnp.where(head_mask(g), out * inverse, 0.0)
             mixed_full[s, g] = out
@@ -243,13 +330,12 @@
 
     lax.fori_loop(0, samples, forward, 0)
 
-    w_down = w_all[:, 3 * inner :]
     normed_out, inverse_out = normalize(tokens_in[...] + dot(mixed[...], w_out[...]))
-    proj[...] = dot(normed_out.astype(BF16), w_down).astype(BF16)
-    d_normed = dot_nt(d_token[...], w_down)
-    first = jnp.mean(d_normed, axis=-1, keepdims=True)
-    second = jnp.mean(d_normed * normed_out, axis=-1, keepdims=True)
-    d_tokens = inverse_out * (d_normed - first - normed_out * second)
+    proj[...] = dot(normed_out.astype(BF16), w_down[...]).astype(BF16)
+    d_norm = d_normed[...]
+    first = jnp.mean(d_norm, axis=-1, keepdims=True)
+    second = jnp.mean(d_norm * normed_out, axis=-1, keepdims=True)
+    d_tokens = inverse_out * (d_norm - first - normed_out * second)
     d_mixed[...] = dot_nt(d_tokens.astype(BF16), w_out[...]).astype(BF16)
 
     for g in range(2):
@@ -267,7 +353,7 @@
             cols = pl.ds(pl.multiple_of(k * 256, 256), 256)
             grad = None
             for s in range(samples):
-                d_prob = dot_nt(wide[s], kv[s, cols, value_lanes])
+                d_prob = dot_nt(wide[s], keys(s, k * 256, 256, value_lanes))
                 term = probs[s, g, :, cols].astype(F32) * ((d_prob - delta[s]) * scale[s])
                 grad = term if grad is None else grad + term
             low = grad[:, :128]
@@ -319,6 +405,25 @@
     group = lax.axis_index("samp")
     chips = n_samp // 2
 
+    sets = [[2 * m + c for m in range(chips)] for c in range(2)]
+    swap = [(s, s ^ 1) for s in range(n_samp)]
+
+    spare = jnp.zeros((w_value.shape[0], width - inner - channels), BF16)
+    w_own = jnp.concatenate(
+        [
+            jnp.concatenate([w_query, w_key], axis=1),
+            jnp.concatenate([w_value, w_down, spare], axis=1),
+            w_out,
+            w_up,
+        ],
+        axis=0,
+    )
+    w_got = lax.all_gather(w_own, "samp", axis=0, tiled=False)
+    cut = w_query.shape[0]
+    w_out_all = w_got[:, 2 * cut : 2 * cut + w_out.shape[0]].reshape(-1, width)
+    w_up_all = w_got[:, 2 * cut + w_out.shape[0] :].reshape(-1, width)
+    w_down_all = w_got[:, cut : 2 * cut, inner : inner + channels].reshape(-1, channels)
+
     fetched = []
     for part in range(2):
         perm = [
@@ -327,6 +432,11 @@
             for s in range(n_samp)
         ]
         fetched.append(lax.ppermute(token_single, ("rows", "samp"), perm))
+    fetched = jnp.concatenate(fetched, axis=0)
+    t_mine = lax.all_to_all(
+        jnp.broadcast_to(fetched[None], (chips,) + fetched.shape), "samp", 0, 0, axis_index_groups=sets, tiled=True
+    )
+    t_other = lax.ppermute(t_mine, "samp", swap)
 
     local_token = atom_token - (rank * tok - margin)
     shape = jax.ShapeDtypeStruct
@@ -356,43 +466,54 @@
         compiler_params=params(),
         name="settle",
     )(own, from_left, from_right)
-    pooled_all = lax.all_gather(pooled, "rows", axis=0, tiled=True)
-    pooled_all = pooled_all.reshape(n_rows, samples, tok, channels)
-
-    w_all = lax.all_gather(
-        jnp.concatenate([w_query, w_key, w_value, w_down], axis=1), "samp", axis=0, tiled=True
-    )
-    w_two = lax.all_gather(jnp.concatenate([w_up, w_out], axis=0), "samp", axis=0, tiled=False)
-    w_up_all = w_two[:, : w_up.shape[0]].reshape(-1, width)
-    w_out_all = w_two[:, w_up.shape[0] :].reshape(-1, width)
-    t_all = lax.all_gather(jnp.concatenate(fetched, axis=0), "samp", axis=0, tiled=True)
-
-    block = 256
-    t_cent, base, w_cent, w_kv = pl.pallas_call(
-        functools.partial(prep_kernel, inner),
-        grid=(total // block,),
+    z_sets = [[2 * z + y for z in range(n_rows // 2)] for y in range(2)]
+    pooled_z = lax.all_gather(pooled, "rows", axis=0, tiled=False, axis_index_groups=z_sets)
+    pooled_y = lax.ppermute(pooled_z, "rows", [(r, r ^ 1) for r in range(n_rows)])
+
+    block = total // 4
+    flat = (chips * 2 * tok, width)
+    base, extra, w_mix = pl.pallas_call(
+        functools.partial(prep_kernel, 2),
+        grid=(4,),
         out_shape=(
-            shape((total, width), BF16),
-            shape((total, 2 * inner), F32),
-            shape((channels, width), BF16),
-            shape((channels, 2 * inner), BF16),
+            shape((total, 2 * inner), BF16),
+            shape((total, 2 * channels), F32),
+            shape((channels, 2 * inner + 2 * channels), BF16),
         ),
         in_specs=[
-            pl.BlockSpec((block, width), lambda i: (i, 0)),
+            pl.BlockSpec((block, width), lambda i: (jnp.minimum(i, 1), 0)),
+            pl.BlockSpec((block, width), lambda i: (jnp.maximum(i - 2, 0), 0)),
             pl.BlockSpec((channels, width), lambda i: (0, 0)),
-            pl.BlockSpec(w_all.shape, lambda i: (0, 0)),
+            pl.BlockSpec(w_got.shape, lambda i: (0, 0, 0)),
         ],
         out_specs=(
-            pl.BlockSpec((block, width), lambda i: (i, 0)),
             pl.BlockSpec((block, 2 * inner), lambda i: (i, 0)),
-            pl.BlockSpec((channels, width), lambda i: (0, 0)),
-            pl.BlockSpec((channels, 2 * inner), lambda i: (0, 0)),
+            pl.BlockSpec((block, 2 * channels), lambda i: (i, 0)),
+            pl.BlockSpec((channels, 2 * inner + 2 * channels), lambda i: (0, 0)),
         ),
         compiler_params=params(),
         name="prep",
-    )(t_all, w_up_all, w_all)
-
-    place = jnp.stack([rank, group % 2]).astype(jnp.int32)
+    )(t_mine.reshape(flat), t_other.reshape(flat), w_up_all, w_got)
+    blocks = n_rows // 2
+    base = base.reshape(blocks, 2, tok, 2 * inner)
+    extra = extra.reshape(blocks, 2, tok, 2 * channels)
+
+    place = jnp.stack([rank // 2, rank % 2, group % 2]).astype(jnp.int32)
+    kv_half, tokens_in, queries, d_normed = pl.pallas_call(
+        functools.partial(half_kernel, inner // heads),
+        out_shape=(
+            shape((samples, blocks, tok, 2 * inner), BF16),
+            shape((samples * tok, width), F32),
+            shape((samples * tok, inner), BF16),
+            shape((samples * tok, width), F32),
+        ),
+        in_specs=[SCALAR] + [WHOLE] * 9,
+        out_specs=(WHOLE,) * 4,
+        compiler_params=params(),
+        cost_estimate=pl.CostEstimate(flops=6 * 10**9, bytes_accessed=16 * 10**6, transcendentals=0),
+        name="half",
+    )(place, pooled_z, base, extra, w_mix, pooled, token_single, w_up_all, w_got, d_token)
+
     factor = total / (samples * n_samp)
     rows = heads // 2 * tok
     proj, keep, send = pl.pallas_call(
@@ -402,47 +523,40 @@
             shape((chips, heads * tok, 128), BF16),
             shape((chips, heads * tok, 128), BF16),
         ),
-        in_specs=[SCALAR, WHOLE, ANY, ANY] + [WHOLE] * 7 + [ANY, WHOLE],
+        in_specs=[SCALAR, WHOLE, WHOLE, ANY, ANY, ANY] + [WHOLE] * 5 + [ANY],
         out_specs=(WHOLE,) * 3,
         scratch_shapes=[
-            pltpu.VMEM((2, 2 * tok, width), BF16),
-            pltpu.VMEM((2, 2 * tok, 2 * inner), F32),
+            pltpu.VMEM((blocks, tok, 2 * inner), BF16),
+            pltpu.VMEM((blocks, tok, 2 * channels), F32),
+            pltpu.VMEM((samples, blocks, 2, tok, 2 * inner), BF16),
             pltpu.VMEM((heads * tok, total), BF16),
-            pltpu.VMEM((samples, total, 2 * inner), BF16),
-            pltpu.VMEM((samples * tok, width), F32),
-            pltpu.VMEM((samples * tok, inner), BF16),
             pltpu.VMEM((2, rows, total), F32),
             pltpu.VMEM((samples, 2, rows, total), BF16),
             pltpu.VMEM((samples, 2, rows, 256), F32),
             pltpu.VMEM((samples, 2, rows, 128), F32),
             pltpu.VMEM((samples * tok, inner), BF16),
             pltpu.VMEM((samples * tok, inner), BF16),
-            pltpu.SemaphoreType.DMA((2,)),
-            pltpu.SemaphoreType.DMA((2,)),
-            pltpu.SemaphoreType.DMA,
+            pltpu.SemaphoreType.DMA((9 + samples,)),
         ],
         compiler_params=params(),
         name="attend",
     )(
         place,
-        pooled_all,
-        t_cent,
+        pooled_y,
+        w_mix,
         base,
-        w_cent,
-        w_kv,
-        pooled,
-        token_single,
-        w_up_all,
-        w_all,
+        extra,
+        kv_half,
+        tokens_in,
+        queries,
+        d_normed,
+        w_down_all,
         w_out_all,
         pair_bias.reshape(heads * tok, total),
-        d_token,
     )
 
-    swap = [(s, s ^ 1) for s in range(n_samp)]
     other = lax.ppermute(send, "samp", swap)
     both = (keep.astype(F32) + other.astype(F32)).astype(BF16)
-    sets = [[2 * m + c for m in range(chips)] for c in range(2)]
     shares = lax.all_to_all(both, "samp", 0, 0, axis_index_groups=sets, tiled=True)
     bias_grad = jnp.sum(shares.astype(F32), axis=0).reshape(heads, tok, 128)
 

time: 329 us -> 229 us (0.70)
  the two profiles are of different devices: /device:TPU:37 before, /device:TPU:29 now
where the time goes in v2:
time: 229 us; the launch traced here: 228 us
  blocking collectives  61.2 us (27%)
  starting transfers between devices  56.1 us (24%)
  Pallas kernels  52.8 us (23%)
  waiting for transfers between devices  28.4 us (12%)
  between operations  14.9 us (7%)
  local copies, waits for them, and re-layouts  8.57 us (4%)
  other arithmetic  6.16 us (3%)
    all_gather x1, blocking collectives, local(): lax.all_gather(pooled, 'rows', axis=0, tiled=False, axis_index_groups=z_s...  31.5 us
    all_to_all x1, blocking collectives, local(): lax.all_to_all(jnp.broadcast_to(fetched[None], (chips,) + fetched.shape),...  29.7 us
    pallas_call x1, Pallas kernels, local(): pl.pallas_call(functools.partial(attend_kernel, heads, factor), out_shape...  24.2 us
    ppermute x2, starting transfers between devices, local(): fetched.append(lax.ppermute(token_single, ('rows', 'samp'), perm))  19.2 us
    ppermute x2, waiting for transfers between devices, local(): fetched.append(lax.ppermute(token_single, ('rows', 'samp'), perm))  12.7 us
    pallas_call x1, Pallas kernels, local(): pl.pallas_call(functools.partial(half_kernel, inner // heads), out_shape=...  11.5 us
    pallas_call x1, Pallas kernels, local(): pl.pallas_call(functools.partial(prep_kernel, 2), grid=(4,), out_shape=(s...  10.6 us
    ppermute x1, starting transfers between devices, local(): other = lax.ppermute(send, 'samp', swap)  9.86 us
  transfers between devices with their start and end apart: 11, of which 5 were waited for; matrix products, arithmetic and copies ran while one was open for 3% of the time, Pallas kernels for 13%

profile of v2, /device:TPU:29, one launch (start us, length us, event | category | flops | bytes accessed | tf_op | source)
XLA Modules:
  0.0 228.1 jit_solution(9660337045768702531)
XLA Ops:
  8.8 10.2 %collective-permute-start.3 = (bf16[64,768]{1,0:T(8,128)(2,1)}, bf16[64,768]{1,0:T(8,128)(2,1)S(1)}, u32[]{:S(2)}, u32[]{:S(2)}) collective-permute-start(bf16[64,768]{1,0:T(8,128)(2,1)} %t_own.1), channel_id=1, source_target_pairs={{0,0},{33,1},{66,2},{99,3},{132,4},{165,5},{198,6},{231,7},{264,8}... | collective-permute-start | bytes 294920 | tf_op jit(solution)/shard_map/ppermute | solution.py:434
  19.0 9.0 %collective-permute-start.4 = (bf16[64,768]{1,0:T(8,128)(2,1)}, bf16[64,768]{1,0:T(8,128)(2,1)S(1)}, u32[]{:S(2)}, u32[]{:S(2)}) collective-permute-start(bf16[64,768]{1,0:T(8,128)(2,1)} %t_own.1), channel_id=1, source_target_pairs={{16,0},{49,1},{82,2},{115,3},{148,4},{181,5},{214,6},{247,7},{280,... | collective-permute-start | bytes 294920 | tf_op jit(solution)/shard_map/ppermute | solution.py:434
  28.0 12.7 %collective-permute-done.4 = bf16[64,768]{1,0:T(8,128)(2,1)S(1)} collective-permute-done((bf16[64,768]{1,0:T(8,128)(2,1)}, bf16[64,768]{1,0:T(8,128)(2,1)S(1)}, u32[]{:S(2)}, u32[]{:S(2)}) %collective-permute-start.4) | collective-permute-done | bytes 98336 | tf_op jit(solution)/shard_map/ppermute | solution.py:434
  40.8 29.7 %all_to_all.10 = bf16[8,128,768]{2,1,0:T(8,128)(2,1)S(1)} all-to-all(bf16[8,128,768]{2,1,0:T(8,128)(2,1)S(1)} %broadcast_in_dim.17), channel_id=1, replica_groups={{0,2,4,6,8,10,12,14},{1,3,5,7,9,11,13,15},{16,18,20,22,24,26,28,30},{17..., dimensions={0} | all-to-all | bytes 3145728 | tf_op jit(solution)/shard_map/all_to_all | solution.py:436
  70.6 5.4 %collective-permute-start.5 = (bf16[8,128,768]{2,1,0:T(8,128)(2,1)S(1)}, bf16[8,128,768]{2,1,0:T(8,128)(2,1)S(1)}, u32[]{:S(2)}, u32[]{:S(2)}) collective-permute-start(bf16[8,128,768]{2,1,0:T(8,128)(2,1)S(1)} %all_to_all.10), channel_id=1, source_target_pairs={{0,1},{1,0},{2,3},{3,2},{4,5},{5,4},{6,7},{7,6},{8,9},{9,8},{10,11... | collective-permute-start | bytes 4718600 | tf_op jit(solution)/shard_map/ppermute | solution.py:439
  77.2 2.7 %pool.1 = (bf16[3,512,128]{2,1,0:T(8,128)(2,1)}, f32[7,64,128]{2,1,0:T(8,128)}, f32[7,32,128]{2,1,0:T(8,128)}, f32[7,32,128]{2,1,0:T(8,128)}) custom-call(s32[1]{0:T(128)S(6)} %copy.17.count, s32[1,512]{1,0:T(1,128)} %bitcast.35, bf16[3,512,128]{2,1,0:T(8,128)(2,1)} %noised.1, bf16[512,128]{1,0:T(8,128)(2,1)} %single.1, bf16[128,128]{1,0:T(8,128)(2,1)} %w_atom.1, ...), custom_call_target="tpu_custom_call" | custom-call | tf_op jit(solution)/shard_map/pool/pallas_call | solution.py:444
  79.8 1.9 collective-permute-start
  81.7 4.9 %collective-permute-start.1 = (f32[7,32,128]{2,1,0:T(8,128)}, f32[7,32,128]{2,1,0:T(8,128)S(1)}, u32[]{:S(2)}, u32[]{:S(2)}) collective-permute-start(f32[7,32,128]{2,1,0:T(8,128)} %get-tuple-element.21), channel_id=1, source_target_pairs={{16,0},{32,16},{48,32},{64,48},{80,64},{96,80},{112,96},{128,112},... | collective-permute-start | bytes 344072 | tf_op jit(solution)/shard_map/ppermute | solution.py:460
  88.2 2.8 %collective-permute-done.1.from_right = f32[7,32,128]{2,1,0:T(8,128)S(1)} collective-permute-done((f32[7,32,128]{2,1,0:T(8,128)}, f32[7,32,128]{2,1,0:T(8,128)S(1)}, u32[]{:S(2)}, u32[]{:S(2)}) %collective-permute-start.1) | collective-permute-done | bytes 114720 | tf_op jit(solution)/shard_map/ppermute | solution.py:460
  91.7 1.7 settle.1
  93.4 31.5 %all-gather = bf16[3072,128]{1,0:T(8,128)(2,1)} all-gather(bf16[192,128]{1,0:T(8,128)(2,1)} %get-tuple-element.22.pooled), channel_id=2, replica_groups={{0,32,64,96,128,160,192,224,256,288,320,352,384,416,448,480},{16,48,80,..., dimensions={0}, use_global_device_ids=true | all-gather | bytes 835584 | tf_op jit(solution)/shard_map/all_gather | solution.py:470
  124.8 2.4 %collective-permute-start.2 = (bf16[16,192,128]{2,1,0:T(8,128)(2,1)}, bf16[16,192,128]{2,1,0:T(8,128)(2,1)}, u32[]{:S(2)}, u32[]{:S(2)}) collective-permute-start(bf16[16,192,128]{2,1,0:T(8,128)(2,1)} %bitcast.5.pooled_z), channel_id=1, source_target_pairs={{0,16},{16,0},{32,48},{48,32},{64,80},{80,64},{96,112},{112,96},{1... | collective-permute-start | bytes 2359304 | tf_op jit(solution)/shard_map/ppermute | solution.py:471
  127.2 1.9 slice.22
  133.6 10.6 %prep.1 = (bf16[2048,768]{1,0:T(8,128)(2,1)}, f32[2048,256]{1,0:T(8,128)}, bf16[128,1024]{1,0:T(8,128)(2,1)}) custom-call(bf16[1024,768]{1,0:T(8,128)(2,1)} %bitcast.18, bf16[1024,768]{1,0:T(8,128)(2,1)} %bitcast.30, bf16[128,768]{1,0:T(8,128)(2,1)} %slice_bitcast_fusion.w_up, bf16[16,128,768]{2,1,0:T(8,128)(2,1)} %bitcast.22), custom_call_target="tpu_custom_call" | custom-call | tf_op jit(solution)/shard_map/prep/pallas_call | solution.py:475
  144.1 11.5 %half.1 = (bf16[3,16,64,768]{3,2,1,0:T(8,128)(2,1)}, f32[192,768]{1,0:T(8,128)}, bf16[192,384]{1,0:T(8,128)(2,1)}, f32[192,768]{1,0:T(8,128)}) custom-call(s32[3]{0:T(128)} %pad_add_fusion.place, bf16[16,192,128]{2,1,0:T(8,128)(2,1)} %bitcast.5.pooled_z, bf16[16,2,64,768]{3,2,1,0:T(8,128)(2,1)} %bitcast.24, f32[16,2,64,256]{3,2,1,0:T(8,128)} %bitcast.28, ...), custom_call_target="tpu_custom_call" | custom-call | flops 6000000000 | bytes 16000000 | tf_op jit(solution)/shard_map/half/pallas_call | solution.py:502
  155.7 24.2 %attend.1 = (bf16[192,128]{1,0:T(8,128)(2,1)}, bf16[8,512,128]{2,1,0:T(8,128)(2,1)}, bf16[8,512,128]{2,1,0:T(8,128)(2,1)}) custom-call(s32[3]{0:T(128)} %pad_add_fusion.place, bf16[16,192,128]{2,1,0:T(8,128)(2,1)} %collective-permute-done.2.pooled_y, bf16[128,1024]{1,0:T(8,128)(2,1)} %get-tuple-element.23.w_mix, bf16[16,2,64,768]{3,2,1,0:T(8,128)(2,1)} %bitcast.25, ...), custom_call_target="tpu_custom_call" | custom-call | tf_op jit(solution)/shard_map/attend/pallas_call | solution.py:519
  179.9 9.9 %collective-permute-start.8 = (bf16[8,512,128]{2,1,0:T(8,128)(2,1)}, bf16[8,512,128]{2,1,0:T(8,128)(2,1)S(1)}, u32[]{:S(2)}, u32[]{:S(2)}) collective-permute-start(bf16[8,512,128]{2,1,0:T(8,128)(2,1)} %get-tuple-element.33), channel_id=1, source_target_pairs={{0,1},{1,0},{2,3},{3,2},{4,5},{5,4},{6,7},{7,6},{8,9},{9,8},{10,11... | collective-permute-start | bytes 3145736 | tf_op jit(solution)/shard_map/ppermute | solution.py:558
  189.7 2.5 %collective-permute-done.8 = bf16[8,512,128]{2,1,0:T(8,128)(2,1)S(1)} collective-permute-done((bf16[8,512,128]{2,1,0:T(8,128)(2,1)}, bf16[8,512,128]{2,1,0:T(8,128)(2,1)S(1)}, u32[]{:S(2)}, u32[]{:S(2)}) %collective-permute-start.8) | collective-permute-done | bytes 1048608 | tf_op jit(solution)/shard_map/ppermute | solution.py:558
  192.2 2.5 %add_convert_fusion = bf16[8,512,128]{2,1,0:T(8,128)(2,1)} fusion(bf16[8,512,128]{2,1,0:T(8,128)(2,1)S(1)} %collective-permute-done.8, bf16[8,512,128]{2,1,0:T(8,128)(2,1)} %get-tuple-element.32), kind=kLoop, calls=%fused_computation.1 | loop fusion | flops 2097152 | bytes 3145728 | tf_op jit(solution)/shard_map/convert_element_type | solution.py:559
  194.7 5.4 %all-to-all-start.1 = ((bf16[8,512,128]{2,1,0:T(8,128)(2,1)}), bf16[8,512,128]{2,1,0:T(8,128)(2,1)S(1)}, u32[]{:S(2)}, u32[]{:S(2)}) async-start(bf16[8,512,128]{2,1,0:T(8,128)(2,1)} %add_convert_fusion), calls=%async_computation.1 | async-start | bytes 2097152 | tf_op jit(solution)/shard_map/all_to_all | solution.py:560
  200.1 4.0 %collective-permute-start.6 = (bf16[3,32,128]{2,1,0:T(8,128)(2,1)S(1)}, bf16[3,32,128]{2,1,0:T(8,128)(2,1)S(1)}, u32[]{:S(2)}, u32[]{:S(2)}) collective-permute-start(bf16[3,32,128]{2,1,0:T(8,128)(2,1)S(1)} %get-tuple-element.35), channel_id=1, source_target_pairs={{0,16},{16,32},{32,48},{48,64},{64,80},{80,96},{96,112},{112,128},... | collective-permute-start | bytes 73736 | tf_op jit(solution)/shard_map/ppermute | solution.py:564
  204.1 3.1 %collective-permute-start.7 = (bf16[3,32,128]{2,1,0:T(8,128)(2,1)S(1)}, bf16[3,32,128]{2,1,0:T(8,128)(2,1)S(1)}, u32[]{:S(2)}, u32[]{:S(2)}) collective-permute-start(bf16[3,32,128]{2,1,0:T(8,128)(2,1)S(1)} %get-tuple-element.34), channel_id=1, source_target_pairs={{16,0},{32,16},{48,32},{64,48},{80,64},{96,80},{112,96},{128,112},... | collective-permute-start | bytes 73736 | tf_op jit(solution)/shard_map/ppermute | solution.py:565
  208.1 9.5 %collective-permute-done.6.from_left = bf16[3,32,128]{2,1,0:T(8,128)(2,1)S(1)} collective-permute-done((bf16[3,32,128]{2,1,0:T(8,128)(2,1)S(1)}, bf16[3,32,128]{2,1,0:T(8,128)(2,1)S(1)}, u32[]{:S(2)}, u32[]{:S(2)}) %collective-permute-start.6) | collective-permute-done | bytes 24608 | tf_op jit(solution)/shard_map/ppermute | solution.py:564
  218.2 2.2 decode.1
  (38 shorter events, 11.2 us)
Async XLA Ops:
  7.2 120.0 %all-gather.4.cloned.1.call-start = ((), (), s32[]{:S(2)}) async-start(), calls=%async_computation.2 | async-start | bytes 3342336 | tf_op jit(solution)/shard_map/all_gather | solution.py:421
  8.8 19.2 %collective-permute-start.3 = (bf16[64,768]{1,0:T(8,128)(2,1)}, bf16[64,768]{1,0:T(8,128)(2,1)S(1)}, u32[]{:S(2)}, u32[]{:S(2)}) collective-permute-start(bf16[64,768]{1,0:T(8,128)(2,1)} %t_own.1), channel_id=1, source_target_pairs={{0,0},{33,1},{66,2},{99,3},{132,4},{165,5},{198,6},{231,7},{264,8}... | collective-permute-start | bytes 294920 | tf_op jit(solution)/shard_map/ppermute | solution.py:434
  19.0 21.7 %collective-permute-start.4 = (bf16[64,768]{1,0:T(8,128)(2,1)}, bf16[64,768]{1,0:T(8,128)(2,1)S(1)}, u32[]{:S(2)}, u32[]{:S(2)}) collective-permute-start(bf16[64,768]{1,0:T(8,128)(2,1)} %t_own.1), channel_id=1, source_target_pairs={{16,0},{49,1},{82,2},{115,3},{148,4},{181,5},{214,6},{247,7},{280,... | collective-permute-start | bytes 294920 | tf_op jit(solution)/shard_map/ppermute | solution.py:434
  40.7 35.9 %copy-start.8 = (s32[512]{0:T(512)S(1)}, s32[512]{0:T(512)}, u32[]{:S(2)}) copy-start(s32[512]{0:T(512)} %param.16) | copy-start | bytes 6148
  70.6 61.8 %copy-start = (bf16[8,128,768]{2,1,0:T(8,128)(2,1)}, bf16[8,128,768]{2,1,0:T(8,128)(2,1)S(1)}, u32[]{:S(2)}) copy-start(bf16[8,128,768]{2,1,0:T(8,128)(2,1)S(1)} %all_to_all.10) | copy-start | bytes 4718596
  70.6 61.8 %collective-permute-start.5 = (bf16[8,128,768]{2,1,0:T(8,128)(2,1)S(1)}, bf16[8,128,768]{2,1,0:T(8,128)(2,1)S(1)}, u32[]{:S(2)}, u32[]{:S(2)}) collective-permute-start(bf16[8,128,768]{2,1,0:T(8,128)(2,1)S(1)} %all_to_all.10), channel_id=1, source_target_pairs={{0,1},{1,0},{2,3},{3,2},{4,5},{5,4},{6,7},{7,6},{8,9},{9,8},{10,11... | collective-permute-start | bytes 4718600 | tf_op jit(solution)/shard_map/ppermute | solution.py:439
  79.8 8.4 %collective-permute-start = (f32[7,32,128]{2,1,0:T(8,128)}, f32[7,32,128]{2,1,0:T(8,128)S(1)}, u32[]{:S(2)}, u32[]{:S(2)}) collective-permute-start(f32[7,32,128]{2,1,0:T(8,128)} %get-tuple-element.20), channel_id=1, source_target_pairs={{0,16},{16,32},{32,48},{48,64},{64,80},{80,96},{96,112},{112,128},... | collective-permute-start | bytes 344072 | tf_op jit(solution)/shard_map/ppermute | solution.py:459
  81.7 9.3 %collective-permute-start.1 = (f32[7,32,128]{2,1,0:T(8,128)}, f32[7,32,128]{2,1,0:T(8,128)S(1)}, u32[]{:S(2)}, u32[]{:S(2)}) collective-permute-start(f32[7,32,128]{2,1,0:T(8,128)} %get-tuple-element.21), channel_id=1, source_target_pairs={{16,0},{32,16},{48,32},{64,48},{80,64},{96,80},{112,96},{128,112},... | collective-permute-start | bytes 344072 | tf_op jit(solution)/shard_map/ppermute | solution.py:460
  88.2 2.8 %copy-start.3 = (f32[7,32,128]{2,1,0:T(8,128)}, f32[7,32,128]{2,1,0:T(8,128)S(1)}, u32[]{:S(2)}) copy-start(f32[7,32,128]{2,1,0:T(8,128)S(1)} %collective-permute-done.from_left) | copy-start | bytes 344068
  91.0 0.6 copy-start.4
  124.8 30.8 %collective-permute-start.2 = (bf16[16,192,128]{2,1,0:T(8,128)(2,1)}, bf16[16,192,128]{2,1,0:T(8,128)(2,1)}, u32[]{:S(2)}, u32[]{:S(2)}) collective-permute-start(bf16[16,192,128]{2,1,0:T(8,128)(2,1)} %bitcast.5.pooled_z), channel_id=1, source_target_pairs={{0,16},{16,0},{32,48},{48,32},{64,80},{80,64},{96,112},{112,96},{1... | collective-permute-start | bytes 2359304 | tf_op jit(solution)/shard_map/ppermute | solution.py:471
  132.4 1.1 copy-start.1
  179.9 12.3 %collective-permute-start.8 = (bf16[8,512,128]{2,1,0:T(8,128)(2,1)}, bf16[8,512,128]{2,1,0:T(8,128)(2,1)S(1)}, u32[]{:S(2)}, u32[]{:S(2)}) collective-permute-start(bf16[8,512,128]{2,1,0:T(8,128)(2,1)} %get-tuple-element.33), channel_id=1, source_target_pairs={{0,1},{1,0},{2,3},{3,2},{4,5},{5,4},{6,7},{7,6},{8,9},{9,8},{10,11... | collective-permute-start | bytes 3145736 | tf_op jit(solution)/shard_map/ppermute | solution.py:558
  192.2 7.9 %copy-start.2 = (bf16[192,128]{1,0:T(8,128)(2,1)S(1)}, bf16[192,128]{1,0:T(8,128)(2,1)}, u32[]{:S(2)}) copy-start(bf16[192,128]{1,0:T(8,128)(2,1)} %get-tuple-element.31) | copy-start | bytes 147460
  192.2 15.0 %copy-start.7 = (s32[512]{0:T(512)S(1)}, s32[512]{0:T(512)}, u32[]{:S(2)}) copy-start(s32[512]{0:T(512)} %broadcast_subtract_fusion) | copy-start | bytes 6148
  194.7 25.7 %all-to-all-start.1 = ((bf16[8,512,128]{2,1,0:T(8,128)(2,1)}), bf16[8,512,128]{2,1,0:T(8,128)(2,1)S(1)}, u32[]{:S(2)}, u32[]{:S(2)}) async-start(bf16[8,512,128]{2,1,0:T(8,128)(2,1)} %add_convert_fusion), calls=%async_computation.1 | async-start | bytes 2097152 | tf_op jit(solution)/shard_map/all_to_all | solution.py:560
  200.1 17.5 %collective-permute-start.6 = (bf16[3,32,128]{2,1,0:T(8,128)(2,1)S(1)}, bf16[3,32,128]{2,1,0:T(8,128)(2,1)S(1)}, u32[]{:S(2)}, u32[]{:S(2)}) collective-permute-start(bf16[3,32,128]{2,1,0:T(8,128)(2,1)S(1)} %get-tuple-element.35), channel_id=1, source_target_pairs={{0,16},{16,32},{32,48},{48,64},{64,80},{80,96},{96,112},{112,128},... | collective-permute-start | bytes 73736 | tf_op jit(solution)/shard_map/ppermute | solution.py:564
  204.1 13.5 %collective-permute-start.7 = (bf16[3,32,128]{2,1,0:T(8,128)(2,1)S(1)}, bf16[3,32,128]{2,1,0:T(8,128)(2,1)S(1)}, u32[]{:S(2)}, u32[]{:S(2)}) collective-permute-start(bf16[3,32,128]{2,1,0:T(8,128)(2,1)S(1)} %get-tuple-element.34), channel_id=1, source_target_pairs={{16,0},{32,16},{48,32},{64,48},{80,64},{96,80},{112,96},{128,112},... | collective-permute-start | bytes 73736 | tf_op jit(solution)/shard_map/ppermute | solution.py:565
  217.6 0.6 copy-start.5
  217.6 0.6 copy-start.6
Sparse Core Ops, SparseCore 0:
  10.7 46.6 all-gather.3

commit v3 on v2

--- a/solution.py
+++ b/solution.py
@@ -79,44 +79,130 @@
         d_token[s * middle : (s + 1) * middle] = settled(samples + 1 + s).astype(BF16)
 
 
-def prep_kernel(splits, t_mine, t_other, w_up, w_got, base, extra, w_mix):
-    step = pl.program_id(0)
-    inner = w_got.shape[2] // 2
-    depth = w_got.shape[0] * w_got.shape[1] * 3 // 8
-    width = w_up.shape[1]
-    channels = w_up.shape[0]
-    cut = w_got.shape[1] * 3 // 8
-    w_key = w_got[:, :cut, inner:].reshape(depth, inner)
-    w_value = w_got[:, cut : 2 * cut, :inner].reshape(depth, inner)
-    up = w_up[...].astype(F32)
-    up = (up - jnp.mean(up, axis=-1, keepdims=True)).astype(BF16)
-
-    @pl.when(step == 0)
-    def _():
-        w_mix[:, :inner] = dot(up, w_key).astype(BF16)
-        w_mix[:, inner : 2 * inner] = dot(up, w_value).astype(BF16)
-        gram = dot_nt(up, up) * (1.0 / width)
-        high = gram.astype(BF16)
-        w_mix[:, 2 * inner : 2 * inner + channels] = high
-        w_mix[:, 2 * inner + channels :] = (gram - high.astype(F32)).astype(BF16)
-
-    def work(t_ref):
-        t = t_ref[...].astype(F32)
-        cent = (t - jnp.mean(t, axis=-1, keepdims=True)).astype(BF16)
-        base[:, :inner] = dot(cent, w_key).astype(BF16)
-        base[:, inner:] = dot(cent, w_value).astype(BF16)
-        extra[:, :channels] = dot_nt(cent, up) * (2.0 / width)
-        wide = cent.astype(F32)
-        square = jnp.sum(wide * wide, axis=-1, keepdims=True) * (1.0 / width)
-        extra[:, channels:] = jnp.broadcast_to(square, (t.shape[0], channels))
-
-    @pl.when(step < splits)
-    def _():
-        work(t_mine)
-
-    @pl.when(step >= splits)
-    def _():
-        work(t_other)
+def select(rows, cols, size, padded, offset):
+    line = lax.broadcasted_iota(jnp.int32, (rows, cols), 0)
+    column = lax.broadcasted_iota(jnp.int32, (rows, cols), 1)
+    group = line // size
+    return jnp.where(column == group * padded + offset + (line - group * size), 1.0, 0.0).astype(BF16)
+
+
+def pack_kernel(near, far, w_query, w_key, w_value, w_down, w_out, w_up, out):
+    tok, width = near.shape
+    cut, inner = w_query.shape
+    end = inner + w_down.shape[1]
+    out[:tok] = near[...]
+    out[tok : 2 * tok] = far[...]
+    first = slice(2 * tok, 2 * tok + cut)
+    second = slice(2 * tok + cut, 2 * tok + 2 * cut)
+    out[first, :inner] = w_query[...]
+    out[first, inner:] = w_key[...]
+    out[second, :inner] = w_value[...]
+    out[second, inner:end] = w_down[...]
+    out[second, end:] = jnp.zeros((cut, width - end), BF16)
+    both = jnp.concatenate([w_out[...].astype(F32), w_up[...].astype(F32)], axis=0)
+    out[2 * tok + 2 * cut :] = both.astype(BF16)
+
+
+def prep_kernel(
+    head_dim,
+    place,
+    got_mine,
+    got_other,
+    pooled,
+    d_token,
+    t_own,
+    base_hbm,
+    extra_hbm,
+    w_mix,
+    tokens_in,
+    queries,
+    d_normed,
+    weights,
+    t_all,
+    w_big,
+    base,
+    extra,
+    in_sems,
+    out_sems,
+):
+    chips, height, width = got_mine.shape
+    tok = t_own.shape[0]
+    block = 2 * tok
+    channels = pooled.shape[1]
+    samples = pooled.shape[0] // tok
+    inner = queries.shape[1]
+    core = place[2]
+    cut = width // (2 * chips)
+    tail = weights.shape[2] - 2 * cut
+    up_rows = channels // (2 * chips)
+    run = chips // 2
+
+    weight_copies = [
+        pltpu.make_async_copy(got_mine.at[:, block:], weights.at[:, core], in_sems.at[0]),
+        pltpu.make_async_copy(got_other.at[:, block:], weights.at[:, 1 - core], in_sems.at[1]),
+    ]
+    t_copies = []
+    for i in range(4):
+        got = got_mine if i < 2 else got_other
+        part = pl.ds((i % 2) * run, run)
+        t_copies.append(
+            pltpu.make_async_copy(got.at[part, :block], t_all.at[pl.ds(i * run, run)], in_sems.at[2 + i])
+        )
+    for copy in weight_copies + t_copies:
+        copy.start()
+    for copy in weight_copies:
+        copy.wait()
+
+    rest = weights[:, :, 2 * cut :, :].reshape(2 * chips * tail, width)
+    up_raw = dot(select(channels, 2 * chips * tail, up_rows, tail, tail - up_rows), rest)
+    up = (up_raw - jnp.mean(up_raw, axis=-1, keepdims=True)).astype(BF16)
+    w_big[:, :inner] = weights[:, :, :cut, inner:].reshape(width, inner)
+    w_big[:, inner : 2 * inner] = weights[:, :, cut : 2 * cut, :inner].reshape(width, inner)
+    w_big[:, 2 * inner :] = up.astype(F32).T.astype(BF16)
+    mix = dot(up, w_big[...])
+    w_mix[:, : 2 * inner] = mix[:, : 2 * inner].astype(BF16)
+    gram = mix[:, 2 * inner :] * (1.0 / width)
+    high = gram.astype(BF16)
+    w_mix[:, 2 * inner : 2 * inner + channels] = high
+    w_mix[:, 2 * inner + channels :] = (gram - high.astype(F32)).astype(BF16)
+
+    outs = []
+    for i in range(4):
+        t_copies[i].wait()
+
+        def step(k, carry):
+            at = i * run + 2 * k
+            t = t_all[pl.ds(at, 2)].reshape(2 * block, width).astype(F32)
+            cent = (t - jnp.mean(t, axis=-1, keepdims=True)).astype(BF16)
+            both = dot(cent, w_big[...])
+            base[pl.ds(at, 2)] = both[:, : 2 * inner].astype(BF16).reshape(2, block, 2 * inner)
+            wide = cent.astype(F32)
+            square = jnp.sum(wide * wide, axis=-1, keepdims=True) * (1.0 / width)
+            extra[pl.ds(at, 2), :, :channels] = (both[:, 2 * inner :] * (2.0 / width)).reshape(2, block, channels)
+            extra[pl.ds(at, 2), :, channels:] = jnp.broadcast_to(square, (2 * block, channels)).reshape(
+                2, block, channels
+            )
+            return carry
+
+        lax.fori_loop(0, run // 2, step, 0)
+        part = pl.ds(i * run, run)
+        outs.append(pltpu.make_async_copy(base.at[part], base_hbm.at[part], out_sems.at[2 * i]))
+        outs.append(pltpu.make_async_copy(extra.at[part], extra_hbm.at[part], out_sems.at[2 * i + 1]))
+        outs[-2].start()
+        outs[-1].start()
+
+    w_query = weights[:, :, :cut, :inner].reshape(width, inner)
+    w_down = weights[:, :, cut : 2 * cut, inner : inner + channels].reshape(width, channels)
+    t_f = t_own[...].astype(F32)
+    up_exact = up_raw.astype(BF16)
+    for s in range(samples):
+        own_rows = slice(s * tok, (s + 1) * tok)
+        tokens_in[own_rows] = dot(pooled[own_rows], up_exact) + t_f
+    normed, _ = normalize(tokens_in[...])
+    queries[...] = (dot(normed.astype(BF16), w_query) * (head_dim**-0.5)).astype(BF16)
+    d_normed[...] = dot_nt(d_token[...], w_down)
+    for copy in outs:
+        copy.wait()
 
 
 def key_value(tables, bases, extras, w_mix):
@@ -142,66 +228,20 @@
     return jnp.where(own, 2 * position + core, 2 * (position - half) + 1 - core)
 
 
-def half_kernel(
-    head_dim,
-    place,
-    pooled_z,
-    base,
-    extra,
-    w_mix,
-    pooled,
-    t_own,
-    w_up,
-    w_got,
-    d_token,
-    kv,
-    tokens_in,
-    queries,
-    d_normed,
-):
-    blocks, lines, channels = pooled_z.shape
-    samples, _, tok, _ = kv.shape
-    inner = w_got.shape[2] // 2
-    cut = w_got.shape[1] * 3 // 8
-    depth = w_got.shape[0] * cut
-    w_query = w_got[:, :cut, :inner].reshape(depth, inner)
-    w_down = w_got[:, cut : 2 * cut, inner : inner + channels].reshape(depth, channels)
-    t_f = t_own[...].astype(F32)
-    for s in range(samples):
-        own_rows = slice(s * tok, (s + 1) * tok)
-        tokens_in[own_rows] = dot(pooled[own_rows], w_up[...]) + t_f
-    normed, _ = normalize(tokens_in[...])
-    queries[...] = (dot(normed.astype(BF16), w_query) * (head_dim**-0.5)).astype(BF16)
-    d_normed[...] = dot_nt(d_token[...], w_down)
-
-    def step(i, carry):
-        which = (2 * i, 2 * i + 1)
-        at = [lax.rem(place[0] + source(b, place[2], blocks // 2), blocks) for b in which]
-        results = key_value(
-            [pooled_z[z] for z in at], [base[b, 0] for b in which], [extra[b, 0] for b in which], w_mix[...]
-        )
-        for z, result in zip(at, results):
-            for s in range(samples):
-                kv[s, z] = result[s * tok : (s + 1) * tok]
-        return carry
-
-    lax.fori_loop(0, blocks // 2, step, 0)
-
-
 def attend_kernel(
     heads,
     factor,
     place,
+    pooled_z,
     pooled_y,
     w_mix,
     base_hbm,
     extra_hbm,
-    kv_hbm,
-    tokens_in,
+    tokens_hbm,
     queries,
-    d_normed,
-    w_down,
-    w_out,
+    d_normed_hbm,
+    got_mine,
+    got_other,
     bias_hbm,
     proj,
     keep,
@@ -210,6 +250,10 @@
     extra,
     kv,
     bias,
+    tokens_in,
+    d_normed,
+    w_rest,
+    w_down,
     scores,
     probs,
     mixed_full,
@@ -220,6 +264,7 @@
 ):
     blocks, lines, channels = pooled_y.shape
     samples, _, _, tok, deep = kv.shape
+    chips, height, width = got_mine.shape
     total = 2 * blocks * tok
     inner = deep // 2
     head_dim = inner // heads
@@ -230,49 +275,58 @@
     first_z = place[0]
     high = place[1]
     core = place[2]
+    tail = w_rest.shape[2]
+    cut = w_down.shape[2]
     pieces_in = min(4, blocks // 2)
     run = blocks // pieces_in
+
+    def copy(src, dst, index):
+        made = pltpu.make_async_copy(src, dst, sems.at[index])
+        made.start()
+        return made
 
     copies = []
     for piece in range(pieces_in):
         part = pl.ds(piece * run, run)
         copies.append(
             (
-                pltpu.make_async_copy(base_hbm.at[part, 1], base.at[part], sems.at[2 * piece]),
-                pltpu.make_async_copy(extra_hbm.at[part, 1], extra.at[part], sems.at[2 * piece + 1]),
+                copy(base_hbm.at[part], base.at[part], 2 * piece),
+                copy(extra_hbm.at[part], extra.at[part], 2 * piece + 1),
             )
         )
-    bias_copy = pltpu.make_async_copy(bias_hbm, bias, sems.at[2 * pieces_in])
-    kv_copies = [
-        pltpu.make_async_copy(kv_hbm.at[s], kv.at[s, :, high], sems.at[2 * pieces_in + 1 + s])
-        for s in range(samples)
+    down_rows = slice(height - tail - cut, height - tail)
+    down_lanes = slice(inner, inner + channels)
+    late = [
+        copy(bias_hbm, bias, 8),
+        copy(tokens_hbm, tokens_in, 9),
+        copy(d_normed_hbm, d_normed, 10),
+        copy(got_mine.at[:, height - tail :], w_rest.at[:, core], 11),
+        copy(got_other.at[:, height - tail :], w_rest.at[:, 1 - core], 12),
+        copy(got_mine.at[:, down_rows, down_lanes], w_down.at[:, core], 13),
+        copy(got_other.at[:, down_rows, down_lanes], w_down.at[:, 1 - core], 14),
     ]
-    for pair in copies:
-        for copy in pair:
-            copy.start()
-    bias_copy.start()
-    for copy in kv_copies:
-        copy.start()
 
     for piece in range(pieces_in):
-        for copy in copies[piece]:
-            copy.wait()
-
-        def step(i, carry):
-            which = (2 * i, 2 * i + 1)
-            at = [lax.rem(first_z + source(b, core, blocks // 2) + high, blocks) for b in which]
+        for made in copies[piece]:
+            made.wait()
+
+        def step(b, carry):
+            near = lax.rem(first_z + source(b, core, blocks // 2), blocks)
+            far = lax.rem(near + high, blocks)
             results = key_value(
-                [pooled_y[z] for z in at], [base[b] for b in which], [extra[b] for b in which], w_mix[...]
+                [pooled_z[near], pooled_y[far]],
+                [base[b, :tok], base[b, tok:]],
+                [extra[b, :tok], extra[b, tok:]],
+                w_mix[...],
             )
-            for z, result in zip(at, results):
-                for s in range(samples):
-                    kv[s, z, 1 - high] = result[s * tok : (s + 1) * tok]
+            for s in range(samples):
+                kv[s, near, high] = results[0][s * tok : (s + 1) * tok]
+                kv[s, far, 1 - high] = results[1][s * tok : (s + 1) * tok]
             return carry
 
-        lax.fori_loop(piece * run // 2, (piece + 1) * run // 2, step, 0)
-    bias_copy.wait()
-    for copy in kv_copies:
-        copy.wait()
+        lax.fori_loop(piece * run, (piece + 1) * run, step, 0)
+    for made in late:
+        made.wait()
 
     lane_head = lax.broadcasted_iota(jnp.int32, (rows, span), 1)
     row_head = lax.broadcasted_iota(jnp.int32, (rows, span), 0) // tok
@@ -330,13 +384,18 @@
 
     lax.fori_loop(0, samples, forward, 0)
 
-    normed_out, inverse_out = normalize(tokens_in[...] + dot(mixed[...], w_out[...]))
-    proj[...] = dot(normed_out.astype(BF16), w_down[...]).astype(BF16)
+    rest = w_rest[...].reshape(2 * chips * tail, width)
+    down = w_down[...].reshape(width, channels)
+    pick = select(inner, 2 * chips * tail, inner // (2 * chips), tail, 0)
+    mixed_wide = dot(mixed[...], pick).astype(BF16)
+    normed_out, inverse_out = normalize(tokens_in[...] + dot(mixed_wide, rest))
+    proj[...] = dot(normed_out.astype(BF16), down).astype(BF16)
     d_norm = d_normed[...]
     first = jnp.mean(d_norm, axis=-1, keepdims=True)
     second = jnp.mean(d_norm * normed_out, axis=-1, keepdims=True)
     d_tokens = inverse_out * (d_norm - first - normed_out * second)
-    d_mixed[...] = dot_nt(d_tokens.astype(BF16), w_out[...]).astype(BF16)
+    d_mixed_wide = dot_nt(d_tokens.astype(BF16), rest).astype(BF16)
+    d_mixed[...] = dot_nt(d_mixed_wide, pick).astype(BF16)
 
     for g in range(2):
         value_lanes = slice(inner + starts[g], inner + starts[g] + span)
@@ -405,24 +464,9 @@
     group = lax.axis_index("samp")
     chips = n_samp // 2
 
+    blocks = n_rows // 2
     sets = [[2 * m + c for m in range(chips)] for c in range(2)]
     swap = [(s, s ^ 1) for s in range(n_samp)]
-
-    spare = jnp.zeros((w_value.shape[0], width - inner - channels), BF16)
-    w_own = jnp.concatenate(
-        [
-            jnp.concatenate([w_query, w_key], axis=1),
-            jnp.concatenate([w_value, w_down, spare], axis=1),
-            w_out,
-            w_up,
-        ],
-        axis=0,
-    )
-    w_got = lax.all_gather(w_own, "samp", axis=0, tiled=False)
-    cut = w_query.shape[0]
-    w_out_all = w_got[:, 2 * cut : 2 * cut + w_out.shape[0]].reshape(-1, width)
-    w_up_all = w_got[:, 2 * cut + w_out.shape[0] :].reshape(-1, width)
-    w_down_all = w_got[:, cut : 2 * cut, inner : inner + channels].reshape(-1, channels)
 
     fetched = []
     for part in range(2):
@@ -432,11 +476,6 @@
             for s in range(n_samp)
         ]
         fetched.append(lax.ppermute(token_single, ("rows", "samp"), perm))
-    fetched = jnp.concatenate(fetched, axis=0)
-    t_mine = lax.all_to_all(
-        jnp.broadcast_to(fetched[None], (chips,) + fetched.shape), "samp", 0, 0, axis_index_groups=sets, tiled=True
-    )
-    t_other = lax.ppermute(t_mine, "samp", swap)
 
     local_token = atom_token - (rank * tok - margin)
     shape = jax.ShapeDtypeStruct
@@ -456,6 +495,8 @@
     )(atom_count, local_token[None, :], atom_noised, atom_single, w_atom, d_atom_out)
     up = [(i, i + 1) for i in range(n_rows - 1)]
     down = [(i + 1, i) for i in range(n_rows - 1)]
+
+
     from_left = lax.ppermute(right, "rows", up)
     from_right = lax.ppermute(left, "rows", down)
     pooled, d_token = pl.pallas_call(
@@ -466,53 +507,52 @@
         compiler_params=params(),
         name="settle",
     )(own, from_left, from_right)
+    fetched[0], fetched[1], _ = lax.optimization_barrier((fetched[0], fetched[1], left))
+    tail = w_out.shape[0] + w_up.shape[0]
+    shard = pl.pallas_call(
+        pack_kernel,
+        out_shape=shape((2 * tok + 2 * w_query.shape[0] + tail, width), BF16),
+        in_specs=[WHOLE] * 8,
+        out_specs=WHOLE,
+        compiler_params=params(),
+        name="pack",
+    )(fetched[0], fetched[1], w_query, w_key, w_value, w_down, w_out, w_up)
+    pooled, shard = lax.optimization_barrier((pooled, shard))
+    got_mine = lax.all_gather(shard, "samp", axis=0, tiled=False, axis_index_groups=sets)
     z_sets = [[2 * z + y for z in range(n_rows // 2)] for y in range(2)]
     pooled_z = lax.all_gather(pooled, "rows", axis=0, tiled=False, axis_index_groups=z_sets)
     pooled_y = lax.ppermute(pooled_z, "rows", [(r, r ^ 1) for r in range(n_rows)])
 
-    block = total // 4
-    flat = (chips * 2 * tok, width)
-    base, extra, w_mix = pl.pallas_call(
-        functools.partial(prep_kernel, 2),
-        grid=(4,),
+    got_mine, _ = lax.optimization_barrier((got_mine, pooled_z))
+    got_other = lax.ppermute(got_mine, "samp", swap)
+
+    place = jnp.stack([rank // 2, rank % 2, group % 2]).astype(jnp.int32)
+    weight_rows = shard.shape[0] - 2 * tok
+    base, extra, w_mix, tokens_in, queries, d_normed = pl.pallas_call(
+        functools.partial(prep_kernel, inner // heads),
         out_shape=(
-            shape((total, 2 * inner), BF16),
-            shape((total, 2 * channels), F32),
+            shape((blocks, 2 * tok, 2 * inner), BF16),
+            shape((blocks, 2 * tok, 2 * channels), F32),
             shape((channels, 2 * inner + 2 * channels), BF16),
-        ),
-        in_specs=[
-            pl.BlockSpec((block, width), lambda i: (jnp.minimum(i, 1), 0)),
-            pl.BlockSpec((block, width), lambda i: (jnp.maximum(i - 2, 0), 0)),
-            pl.BlockSpec((channels, width), lambda i: (0, 0)),
-            pl.BlockSpec(w_got.shape, lambda i: (0, 0, 0)),
-        ],
-        out_specs=(
-            pl.BlockSpec((block, 2 * inner), lambda i: (i, 0)),
-            pl.BlockSpec((block, 2 * channels), lambda i: (i, 0)),
-            pl.BlockSpec((channels, 2 * inner + 2 * channels), lambda i: (0, 0)),
-        ),
-        compiler_params=params(),
-        name="prep",
-    )(t_mine.reshape(flat), t_other.reshape(flat), w_up_all, w_got)
-    blocks = n_rows // 2
-    base = base.reshape(blocks, 2, tok, 2 * inner)
-    extra = extra.reshape(blocks, 2, tok, 2 * channels)
-
-    place = jnp.stack([rank // 2, rank % 2, group % 2]).astype(jnp.int32)
-    kv_half, tokens_in, queries, d_normed = pl.pallas_call(
-        functools.partial(half_kernel, inner // heads),
-        out_shape=(
-            shape((samples, blocks, tok, 2 * inner), BF16),
             shape((samples * tok, width), F32),
             shape((samples * tok, inner), BF16),
             shape((samples * tok, width), F32),
         ),
-        in_specs=[SCALAR] + [WHOLE] * 9,
-        out_specs=(WHOLE,) * 4,
+        in_specs=[SCALAR, ANY, ANY] + [WHOLE] * 3,
+        out_specs=(ANY, ANY) + (WHOLE,) * 4,
+        scratch_shapes=[
+            pltpu.VMEM((chips, 2, weight_rows, width), BF16),
+            pltpu.VMEM((blocks, 2 * tok, width), BF16),
+            pltpu.VMEM((width, 2 * inner + channels), BF16),
+            pltpu.VMEM((blocks, 2 * tok, 2 * inner), BF16),
+            pltpu.VMEM((blocks, 2 * tok, 2 * channels), F32),
+            pltpu.SemaphoreType.DMA((6,)),
+            pltpu.SemaphoreType.DMA((8,)),
+        ],
         compiler_params=params(),
         cost_estimate=pl.CostEstimate(flops=6 * 10**9, bytes_accessed=16 * 10**6, transcendentals=0),
-        name="half",
-    )(place, pooled_z, base, extra, w_mix, pooled, token_single, w_up_all, w_got, d_token)
+        name="prep",
+    )(place, got_mine, got_other, pooled, d_token, token_single)
 
     factor = total / (samples * n_samp)
     rows = heads // 2 * tok
@@ -523,35 +563,39 @@
             shape((chips, heads * tok, 128), BF16),
             shape((chips, heads * tok, 128), BF16),
         ),
-        in_specs=[SCALAR, WHOLE, WHOLE, ANY, ANY, ANY] + [WHOLE] * 5 + [ANY],
+        in_specs=[SCALAR, WHOLE, WHOLE, WHOLE, ANY, ANY, ANY, WHOLE, ANY, ANY, ANY, ANY],
         out_specs=(WHOLE,) * 3,
         scratch_shapes=[
-            pltpu.VMEM((blocks, tok, 2 * inner), BF16),
-            pltpu.VMEM((blocks, tok, 2 * channels), F32),
+            pltpu.VMEM((blocks, 2 * tok, 2 * inner), BF16),
+            pltpu.VMEM((blocks, 2 * tok, 2 * channels), F32),
             pltpu.VMEM((samples, blocks, 2, tok, 2 * inner), BF16),
             pltpu.VMEM((heads * tok, total), BF16),
+            pltpu.VMEM((samples * tok, width), F32),
+            pltpu.VMEM((samples * tok, width), F32),
+            pltpu.VMEM((chips, 2, tail, width), BF16),
+            pltpu.VMEM((chips, 2, w_down.shape[0], channels), BF16),
             pltpu.VMEM((2, rows, total), F32),
             pltpu.VMEM((samples, 2, rows, total), BF16),
             pltpu.VMEM((samples, 2, rows, 256), F32),
             pltpu.VMEM((samples, 2, rows, 128), F32),
             pltpu.VMEM((samples * tok, inner), BF16),
             pltpu.VMEM((samples * tok, inner), BF16),
-            pltpu.SemaphoreType.DMA((9 + samples,)),
+            pltpu.SemaphoreType.DMA((15,)),
         ],
         compiler_params=params(),
         name="attend",
     )(
         place,
+        pooled_z,
         pooled_y,
         w_mix,
         base,
         extra,
-        kv_half,
         tokens_in,
         queries,
         d_normed,
-        w_down_all,
-        w_out_all,
+        got_mine,
+        got_other,
         pair_bias.reshape(heads * tok, total),
     )
 

time: 229 us -> 239 us (1.044)
  the two profiles are of different devices: /device:TPU:29 before, /device:TPU:37 now
where the time goes in v3:
time: 239 us; the launch traced here: 238 us
  waiting for transfers between devices  81.7 us (34%)
  starting transfers between devices  52.5 us (22%)
  Pallas kernels  48.8 us (20%)
  blocking collectives  31.1 us (13%)
  between operations  14.9 us (6%)
  other arithmetic  5.24 us (2%)
  local copies, waits for them, and re-layouts  3.69 us (2%)
    all_gather x1, waiting for transfers between devices, local(): lax.all_gather(shard, 'samp', axis=0, tiled=False, axis_index_groups=sets)  49.1 us
    all_gather x1, blocking collectives, local(): lax.all_gather(pooled, 'rows', axis=0, tiled=False, axis_index_groups=z_s...  31.1 us
    pallas_call x1, Pallas kernels, local(): pl.pallas_call(functools.partial(attend_kernel, heads, factor), out_shape...  29.4 us
    ppermute x2, starting transfers between devices, local(): fetched.append(lax.ppermute(token_single, ('rows', 'samp'), perm))  22.5 us
    ppermute x2, waiting for transfers between devices, local(): fetched.append(lax.ppermute(token_single, ('rows', 'samp'), perm))  16.5 us
    pallas_call x1, Pallas kernels, local(): pl.pallas_call(functools.partial(prep_kernel, inner // heads), out_shape=...  11.2 us
    ppermute x1, waiting for transfers between devices, local(): lax.ppermute(pooled_z, 'rows', [(r, r ^ 1) for r in range(n_rows)])  5.78 us
    all_to_all x1, starting transfers between devices, local(): lax.all_to_all(both, 'samp', 0, 0, axis_index_groups=sets, tiled=True)  5.03 us
  transfers between devices with their start and end apart: 11, of which 7 were waited for; matrix products, arithmetic and copies ran while one was open for 1% of the time, Pallas kernels for 6%

profile of v3, /device:TPU:37, one launch (start us, length us, event | category | flops | bytes accessed | tf_op | source)
XLA Modules:
  0.0 237.9 jit_solution(9592738904969104252)
XLA Ops:
  9.1 2.6 %pool.1 = (bf16[3,512,128]{2,1,0:T(8,128)(2,1)}, f32[7,64,128]{2,1,0:T(8,128)}, f32[7,32,128]{2,1,0:T(8,128)}, f32[7,32,128]{2,1,0:T(8,128)}) custom-call(s32[1]{0:T(128)S(6)} %copy.17.count, s32[1,512]{1,0:T(1,128)} %bitcast.19, bf16[3,512,128]{2,1,0:T(8,128)(2,1)} %noised.1, bf16[512,128]{1,0:T(8,128)(2,1)} %single.1, bf16[128,128]{1,0:T(8,128)(2,1)} %w_atom.1, ...), custom_call_target="tpu_custom_call" | custom-call | tf_op jit(solution)/shard_map/pool/pallas_call | solution.py:483
  11.8 4.4 %collective-permute-start.1 = (f32[7,32,128]{2,1,0:T(8,128)}, f32[7,32,128]{2,1,0:T(8,128)S(1)}, u32[]{:S(2)}, u32[]{:S(2)}) collective-permute-start(f32[7,32,128]{2,1,0:T(8,128)} %get-tuple-element.25), channel_id=1, source_target_pairs={{16,0},{32,16},{48,32},{64,48},{80,64},{96,80},{112,96},{128,112},... | collective-permute-start | bytes 344072 | tf_op jit(solution)/shard_map/ppermute | solution.py:501
  16.1 2.4 %collective-permute-start = (f32[7,32,128]{2,1,0:T(8,128)}, f32[7,32,128]{2,1,0:T(8,128)S(1)}, u32[]{:S(2)}, u32[]{:S(2)}) collective-permute-start(f32[7,32,128]{2,1,0:T(8,128)} %get-tuple-element.24), channel_id=1, source_target_pairs={{0,16},{16,32},{32,48},{48,64},{64,80},{80,96},{96,112},{112,128},... | collective-permute-start | bytes 344072 | tf_op jit(solution)/shard_map/ppermute | solution.py:500
  18.5 14.1 %collective-permute-start.2 = (bf16[64,768]{1,0:T(8,128)(2,1)}, bf16[64,768]{1,0:T(8,128)(2,1)S(1)}, u32[]{:S(2)}, u32[]{:S(2)}) collective-permute-start(bf16[64,768]{1,0:T(8,128)(2,1)} %t_own.1), channel_id=1, source_target_pairs={{0,0},{33,1},{66,2},{99,3},{132,4},{165,5},{198,6},{231,7},{264,8}... | collective-permute-start | bytes 294920 | tf_op jit(solution)/shard_map/ppermute | solution.py:478
  32.6 8.5 %collective-permute-start.3 = (bf16[64,768]{1,0:T(8,128)(2,1)}, bf16[64,768]{1,0:T(8,128)(2,1)S(1)}, u32[]{:S(2)}, u32[]{:S(2)}) collective-permute-start(bf16[64,768]{1,0:T(8,128)(2,1)} %t_own.1), channel_id=1, source_target_pairs={{16,0},{49,1},{82,2},{115,3},{148,4},{181,5},{214,6},{247,7},{280,... | collective-permute-start | bytes 294920 | tf_op jit(solution)/shard_map/ppermute | solution.py:478
  41.1 16.5 %collective-permute-done.3.far = bf16[64,768]{1,0:T(8,128)(2,1)S(1)} collective-permute-done((bf16[64,768]{1,0:T(8,128)(2,1)}, bf16[64,768]{1,0:T(8,128)(2,1)S(1)}, u32[]{:S(2)}, u32[]{:S(2)}) %collective-permute-start.3) | collective-permute-done | bytes 98336 | tf_op jit(solution)/shard_map/ppermute | solution.py:478
  58.3 1.8 pack.1
  60.7 1.7 settle.1
  62.5 31.1 %all-gather = bf16[3072,128]{1,0:T(8,128)(2,1)S(1)} all-gather(bf16[192,128]{1,0:T(8,128)(2,1)} %get-tuple-element.29.pooled), channel_id=2, replica_groups={{0,32,64,96,128,160,192,224,256,288,320,352,384,416,448,480},{16,48,80,..., dimensions={0}, use_global_device_ids=true | all-gather | bytes 835584 | tf_op jit(solution)/shard_map/all_gather | solution.py:523
  93.5 49.1 %all-gather.4.cloned.1.call-done = bf16[2048,768]{1,0:T(8,128)(2,1)} async-done(((bf16[256,768]{1,0:T(8,128)(2,1)}), bf16[2048,768]{1,0:T(8,128)(2,1)}) %all-gather.4.cloned.1.call-update) | async-done | bytes 3145744 | tf_op jit(solution)/shard_map/all_gather | solution.py:521
  142.6 3.4 %collective-permute-start.5 = (bf16[8,256,768]{2,1,0:T(8,128)(2,1)}, bf16[8,256,768]{2,1,0:T(8,128)(2,1)}, u32[]{:S(2)}, u32[]{:S(2)}) collective-permute-start(bf16[8,256,768]{2,1,0:T(8,128)(2,1)} %bitcast.12), channel_id=1, source_target_pairs={{0,1},{1,0},{2,3},{3,2},{4,5},{5,4},{6,7},{7,6},{8,9},{9,8},{10,11... | collective-permute-start | bytes 9437192 | tf_op jit(solution)/shard_map/ppermute | solution.py:527
  146.0 4.3 %collective-permute-start.4 = (bf16[16,192,128]{2,1,0:T(8,128)(2,1)S(1)}, bf16[16,192,128]{2,1,0:T(8,128)(2,1)S(1)}, u32[]{:S(2)}, u32[]{:S(2)}) collective-permute-start(bf16[16,192,128]{2,1,0:T(8,128)(2,1)S(1)} %bitcast.10), channel_id=1, source_target_pairs={{0,16},{16,0},{32,48},{48,32},{64,80},{80,64},{96,112},{112,96},{1... | collective-permute-start | bytes 2359304 | tf_op jit(solution)/shard_map/ppermute | solution.py:524
  151.6 11.2 %prep.1 = (bf16[16,128,768]{2,1,0:T(8,128)(2,1)}, f32[16,128,256]{2,1,0:T(8,128)}, bf16[128,1024]{1,0:T(8,128)(2,1)}, f32[192,768]{1,0:T(8,128)}, bf16[192,384]{1,0:T(8,128)(2,1)}, /*index=5*/f32[192,768]{1,0:T(8,128)}) custom-call(s32[3]{0:T(128)} %pad_add_fusion.place, bf16[8,256,768]{2,1,0:T(8,128)(2,1)} %bitcast.13, ...), custom_call_target="tpu_custom_call" | custom-call | flops 6000000000 | bytes 16000000 | tf_op jit(solution)/shard_map/prep/pallas_call | solution.py:531
  162.8 5.8 %collective-permute-done.4.pooled_y = bf16[16,192,128]{2,1,0:T(8,128)(2,1)S(1)} collective-permute-done((bf16[16,192,128]{2,1,0:T(8,128)(2,1)S(1)}, bf16[16,192,128]{2,1,0:T(8,128)(2,1)S(1)}, u32[]{:S(2)}, u32[]{:S(2)}) %collective-permute-start.4) | collective-permute-done | bytes 786464 | tf_op jit(solution)/shard_map/ppermute | solution.py:524
  169.5 29.4 %attend.1 = (bf16[192,128]{1,0:T(8,128)(2,1)}, bf16[8,512,128]{2,1,0:T(8,128)(2,1)}, bf16[8,512,128]{2,1,0:T(8,128)(2,1)}) custom-call(s32[3]{0:T(128)} %pad_add_fusion.place, bf16[16,192,128]{2,1,0:T(8,128)(2,1)} %bitcast.11, bf16[16,192,128]{2,1,0:T(8,128)(2,1)} %copy-done.1, bf16[128,1024]{1,0:T(8,128)(2,1)} %get-tuple-element.33.w_mix, ...), custom_call_target="tpu_custom_call" | custom-call | tf_op jit(solution)/shard_map/attend/pallas_call | solution.py:559
  198.9 2.7 %collective-permute-start.8 = (bf16[8,512,128]{2,1,0:T(8,128)(2,1)}, bf16[8,512,128]{2,1,0:T(8,128)(2,1)S(1)}, u32[]{:S(2)}, u32[]{:S(2)}) collective-permute-start(bf16[8,512,128]{2,1,0:T(8,128)(2,1)} %get-tuple-element.41), channel_id=1, source_target_pairs={{0,1},{1,0},{2,3},{3,2},{4,5},{5,4},{6,7},{7,6},{8,9},{9,8},{10,11... | collective-permute-start | bytes 3145736 | tf_op jit(solution)/shard_map/ppermute | solution.py:602
  201.6 2.5 %collective-permute-done.8 = bf16[8,512,128]{2,1,0:T(8,128)(2,1)S(1)} collective-permute-done((bf16[8,512,128]{2,1,0:T(8,128)(2,1)}, bf16[8,512,128]{2,1,0:T(8,128)(2,1)S(1)}, u32[]{:S(2)}, u32[]{:S(2)}) %collective-permute-start.8) | collective-permute-done | bytes 1048608 | tf_op jit(solution)/shard_map/ppermute | solution.py:602
  204.1 2.5 %add_convert_fusion = bf16[8,512,128]{2,1,0:T(8,128)(2,1)} fusion(bf16[8,512,128]{2,1,0:T(8,128)(2,1)S(1)} %collective-permute-done.8, bf16[8,512,128]{2,1,0:T(8,128)(2,1)} %get-tuple-element.40), kind=kLoop, calls=%fused_computation.1 | loop fusion | flops 2097152 | bytes 3145728 | tf_op jit(solution)/shard_map/convert_element_type | solution.py:603
  206.6 5.0 %all-to-all-start = ((bf16[8,512,128]{2,1,0:T(8,128)(2,1)}), bf16[8,512,128]{2,1,0:T(8,128)(2,1)S(1)}, u32[]{:S(2)}, u32[]{:S(2)}) async-start(bf16[8,512,128]{2,1,0:T(8,128)(2,1)} %add_convert_fusion), calls=%async_computation | async-start | bytes 2097152 | tf_op jit(solution)/shard_map/all_to_all | solution.py:604
  211.6 4.1 %collective-permute-start.6 = (bf16[3,32,128]{2,1,0:T(8,128)(2,1)S(1)}, bf16[3,32,128]{2,1,0:T(8,128)(2,1)S(1)}, u32[]{:S(2)}, u32[]{:S(2)}) collective-permute-start(bf16[3,32,128]{2,1,0:T(8,128)(2,1)S(1)} %get-tuple-element.43), channel_id=1, source_target_pairs={{0,16},{16,32},{32,48},{48,64},{64,80},{80,96},{96,112},{112,128},... | collective-permute-start | bytes 73736 | tf_op jit(solution)/shard_map/ppermute | solution.py:608
  215.7 3.6 %collective-permute-start.7 = (bf16[3,32,128]{2,1,0:T(8,128)(2,1)S(1)}, bf16[3,32,128]{2,1,0:T(8,128)(2,1)S(1)}, u32[]{:S(2)}, u32[]{:S(2)}) collective-permute-start(bf16[3,32,128]{2,1,0:T(8,128)(2,1)S(1)} %get-tuple-element.42), channel_id=1, source_target_pairs={{16,0},{32,16},{48,32},{64,48},{80,64},{96,80},{112,96},{128,112},... | collective-permute-start | bytes 73736 | tf_op jit(solution)/shard_map/ppermute | solution.py:609
  220.2 4.3 %collective-permute-done.6.from_left = bf16[3,32,128]{2,1,0:T(8,128)(2,1)S(1)} collective-permute-done((bf16[3,32,128]{2,1,0:T(8,128)(2,1)S(1)}, bf16[3,32,128]{2,1,0:T(8,128)(2,1)S(1)}, u32[]{:S(2)}, u32[]{:S(2)}) %collective-permute-start.6) | collective-permute-done | bytes 24608 | tf_op jit(solution)/shard_map/ppermute | solution.py:608
  224.5 2.9 %collective-permute-done.7.from_right = bf16[3,32,128]{2,1,0:T(8,128)(2,1)S(1)} collective-permute-done((bf16[3,32,128]{2,1,0:T(8,128)(2,1)S(1)}, bf16[3,32,128]{2,1,0:T(8,128)(2,1)S(1)}, u32[]{:S(2)}, u32[]{:S(2)}) %collective-permute-start.7) | collective-permute-done | bytes 24608 | tf_op jit(solution)/shard_map/ppermute | solution.py:609
  228.0 2.2 decode.1
  (32 shorter events, 7.1 us)
Async XLA Ops:
  7.2 135.5 %all-gather.4.cloned.1.call-start = ((), (), s32[]{:S(2)}) async-start(), calls=%async_computation.1 | async-start | bytes 3538944 | tf_op jit(solution)/shard_map/all_gather | solution.py:521
  11.8 48.3 %collective-permute-start.1 = (f32[7,32,128]{2,1,0:T(8,128)}, f32[7,32,128]{2,1,0:T(8,128)S(1)}, u32[]{:S(2)}, u32[]{:S(2)}) collective-permute-start(f32[7,32,128]{2,1,0:T(8,128)} %get-tuple-element.25), channel_id=1, source_target_pairs={{16,0},{32,16},{48,32},{64,48},{80,64},{96,80},{112,96},{128,112},... | collective-permute-start | bytes 344072 | tf_op jit(solution)/shard_map/ppermute | solution.py:501
  16.1 43.9 %collective-permute-start = (f32[7,32,128]{2,1,0:T(8,128)}, f32[7,32,128]{2,1,0:T(8,128)S(1)}, u32[]{:S(2)}, u32[]{:S(2)}) collective-permute-start(f32[7,32,128]{2,1,0:T(8,128)} %get-tuple-element.24), channel_id=1, source_target_pairs={{0,16},{16,32},{32,48},{48,64},{64,80},{80,96},{96,112},{112,128},... | collective-permute-start | bytes 344072 | tf_op jit(solution)/shard_map/ppermute | solution.py:500
  18.5 22.6 %collective-permute-start.2 = (bf16[64,768]{1,0:T(8,128)(2,1)}, bf16[64,768]{1,0:T(8,128)(2,1)S(1)}, u32[]{:S(2)}, u32[]{:S(2)}) collective-permute-start(bf16[64,768]{1,0:T(8,128)(2,1)} %t_own.1), channel_id=1, source_target_pairs={{0,0},{33,1},{66,2},{99,3},{132,4},{165,5},{198,6},{231,7},{264,8}... | collective-permute-start | bytes 294920 | tf_op jit(solution)/shard_map/ppermute | solution.py:478
  32.6 25.0 %collective-permute-start.3 = (bf16[64,768]{1,0:T(8,128)(2,1)}, bf16[64,768]{1,0:T(8,128)(2,1)S(1)}, u32[]{:S(2)}, u32[]{:S(2)}) collective-permute-start(bf16[64,768]{1,0:T(8,128)(2,1)} %t_own.1), channel_id=1, source_target_pairs={{16,0},{49,1},{82,2},{115,3},{148,4},{181,5},{214,6},{247,7},{280,... | collective-permute-start | bytes 294920 | tf_op jit(solution)/shard_map/ppermute | solution.py:478
  41.1 16.5 %copy-start.5 = (bf16[64,768]{1,0:T(8,128)(2,1)}, bf16[64,768]{1,0:T(8,128)(2,1)S(1)}, u32[]{:S(2)}) copy-start(bf16[64,768]{1,0:T(8,128)(2,1)S(1)} %collective-permute-done.2.near) | copy-start | bytes 294916
  57.6 0.6 copy-start.6
  60.0 0.7 copy-start.3
  60.0 0.7 copy-start.4
  93.5 69.3 %copy-start = (bf16[3072,128]{1,0:T(8,128)(2,1)}, bf16[3072,128]{1,0:T(8,128)(2,1)S(1)}, u32[]{:S(2)}) copy-start(bf16[3072,128]{1,0:T(8,128)(2,1)S(1)} %all-gather) | copy-start | bytes 2359300
  142.6 9.0 %collective-permute-start.5 = (bf16[8,256,768]{2,1,0:T(8,128)(2,1)}, bf16[8,256,768]{2,1,0:T(8,128)(2,1)}, u32[]{:S(2)}, u32[]{:S(2)}) collective-permute-start(bf16[8,256,768]{2,1,0:T(8,128)(2,1)} %bitcast.12), channel_id=1, source_target_pairs={{0,1},{1,0},{2,3},{3,2},{4,5},{5,4},{6,7},{7,6},{8,9},{9,8},{10,11... | collective-permute-start | bytes 9437192 | tf_op jit(solution)/shard_map/ppermute | solution.py:527
  146.0 22.6 %collective-permute-start.4 = (bf16[16,192,128]{2,1,0:T(8,128)(2,1)S(1)}, bf16[16,192,128]{2,1,0:T(8,128)(2,1)S(1)}, u32[]{:S(2)}, u32[]{:S(2)}) collective-permute-start(bf16[16,192,128]{2,1,0:T(8,128)(2,1)S(1)} %bitcast.10), channel_id=1, source_target_pairs={{0,16},{16,0},{32,48},{48,32},{64,80},{80,64},{96,112},{112,96},{1... | collective-permute-start | bytes 2359304 | tf_op jit(solution)/shard_map/ppermute | solution.py:524
  168.6 0.9 copy-start.1
  198.9 5.2 %collective-permute-start.8 = (bf16[8,512,128]{2,1,0:T(8,128)(2,1)}, bf16[8,512,128]{2,1,0:T(8,128)(2,1)S(1)}, u32[]{:S(2)}, u32[]{:S(2)}) collective-permute-start(bf16[8,512,128]{2,1,0:T(8,128)(2,1)} %get-tuple-element.41), channel_id=1, source_target_pairs={{0,1},{1,0},{2,3},{3,2},{4,5},{5,4},{6,7},{7,6},{8,9},{9,8},{10,11... | collective-permute-start | bytes 3145736 | tf_op jit(solution)/shard_map/ppermute | solution.py:602
  204.1 7.6 %copy-start.2 = (bf16[192,128]{1,0:T(8,128)(2,1)S(1)}, bf16[192,128]{1,0:T(8,128)(2,1)}, u32[]{:S(2)}) copy-start(bf16[192,128]{1,0:T(8,128)(2,1)} %get-tuple-element.39) | copy-start | bytes 147460
  204.1 15.3 %copy-start.9 = (s32[512]{0:T(512)S(1)}, s32[512]{0:T(512)}, u32[]{:S(2)}) copy-start(s32[512]{0:T(512)} %broadcast_subtract_fusion) | copy-start | bytes 6148
  206.6 23.6 %all-to-all-start = ((bf16[8,512,128]{2,1,0:T(8,128)(2,1)}), bf16[8,512,128]{2,1,0:T(8,128)(2,1)S(1)}, u32[]{:S(2)}, u32[]{:S(2)}) async-start(bf16[8,512,128]{2,1,0:T(8,128)(2,1)} %add_convert_fusion), calls=%async_computation | async-start | bytes 2097152 | tf_op jit(solution)/shard_map/all_to_all | solution.py:604
  211.6 12.9 %collective-permute-start.6 = (bf16[3,32,128]{2,1,0:T(8,128)(2,1)S(1)}, bf16[3,32,128]{2,1,0:T(8,128)(2,1)S(1)}, u32[]{:S(2)}, u32[]{:S(2)}) collective-permute-start(bf16[3,32,128]{2,1,0:T(8,128)(2,1)S(1)} %get-tuple-element.43), channel_id=1, source_target_pairs={{0,16},{16,32},{32,48},{48,64},{64,80},{80,96},{96,112},{112,128},... | collective-permute-start | bytes 73736 | tf_op jit(solution)/shard_map/ppermute | solution.py:608
  215.7 11.7 %collective-permute-start.7 = (bf16[3,32,128]{2,1,0:T(8,128)(2,1)S(1)}, bf16[3,32,128]{2,1,0:T(8,128)(2,1)S(1)}, u32[]{:S(2)}, u32[]{:S(2)}) collective-permute-start(bf16[3,32,128]{2,1,0:T(8,128)(2,1)S(1)} %get-tuple-element.42), channel_id=1, source_target_pairs={{16,0},{32,16},{48,32},{64,48},{80,64},{96,80},{112,96},{128,112},... | collective-permute-start | bytes 73736 | tf_op jit(solution)/shard_map/ppermute | solution.py:609
  224.5 2.9 %copy-start.7 = (bf16[3,32,128]{2,1,0:T(8,128)(2,1)}, bf16[3,32,128]{2,1,0:T(8,128)(2,1)S(1)}, u32[]{:S(2)}) copy-start(bf16[3,32,128]{2,1,0:T(8,128)(2,1)S(1)} %collective-permute-done.6.from_left) | copy-start | bytes 73732
  227.4 0.6 copy-start.8
Sparse Core Ops, SparseCore 0:
  62.6 80.0 all-gather.3

commit v4 on v3

--- a/solution.py
+++ b/solution.py
@@ -105,9 +105,7 @@
 
 def prep_kernel(
     head_dim,
-    place,
-    got_mine,
-    got_other,
+    got,
     pooled,
     d_token,
     t_own,
@@ -125,39 +123,32 @@
     in_sems,
     out_sems,
 ):
-    chips, height, width = got_mine.shape
+    members, height, width = got.shape
     tok = t_own.shape[0]
     block = 2 * tok
     channels = pooled.shape[1]
     samples = pooled.shape[0] // tok
     inner = queries.shape[1]
-    core = place[2]
-    cut = width // (2 * chips)
-    tail = weights.shape[2] - 2 * cut
-    up_rows = channels // (2 * chips)
-    run = chips // 2
-
-    weight_copies = [
-        pltpu.make_async_copy(got_mine.at[:, block:], weights.at[:, core], in_sems.at[0]),
-        pltpu.make_async_copy(got_other.at[:, block:], weights.at[:, 1 - core], in_sems.at[1]),
-    ]
+    cut = width // members
+    tail = weights.shape[1] - 2 * cut
+    up_rows = channels // members
+    run = members // 4
+
+    weight_copies = [pltpu.make_async_copy(got.at[:, block:], weights, in_sems.at[0])]
     t_copies = []
     for i in range(4):
-        got = got_mine if i < 2 else got_other
-        part = pl.ds((i % 2) * run, run)
-        t_copies.append(
-            pltpu.make_async_copy(got.at[part, :block], t_all.at[pl.ds(i * run, run)], in_sems.at[2 + i])
-        )
+        part = pl.ds(i * run, run)
+        t_copies.append(pltpu.make_async_copy(got.at[part, :block], t_all.at[part], in_sems.at[1 + i]))
     for copy in weight_copies + t_copies:
         copy.start()
     for copy in weight_copies:
         copy.wait()
 
-    rest = weights[:, :, 2 * cut :, :].reshape(2 * chips * tail, width)
-    up_raw = dot(select(channels, 2 * chips * tail, up_rows, tail, tail - up_rows), rest)
+    rest = weights[:, 2 * cut :, :].reshape(members * tail, width)
+    up_raw = dot(select(channels, members * tail, up_rows, tail, tail - up_rows), rest)
     up = (up_raw - jnp.mean(up_raw, axis=-1, keepdims=True)).astype(BF16)
-    w_big[:, :inner] = weights[:, :, :cut, inner:].reshape(width, inner)
-    w_big[:, inner : 2 * inner] = weights[:, :, cut : 2 * cut, :inner].reshape(width, inner)
+    w_big[:, :inner] = weights[:, :cut, inner:].reshape(width, inner)
+    w_big[:, inner : 2 * inner] = weights[:, cut : 2 * cut, :inner].reshape(width, inner)
     w_big[:, 2 * inner :] = up.astype(F32).T.astype(BF16)
     mix = dot(up, w_big[...])
     w_mix[:, : 2 * inner] = mix[:, : 2 * inner].astype(BF16)
@@ -191,8 +182,8 @@
         outs[-2].start()
         outs[-1].start()
 
-    w_query = weights[:, :, :cut, :inner].reshape(width, inner)
-    w_down = weights[:, :, cut : 2 * cut, inner : inner + channels].reshape(width, channels)
+    w_query = weights[:, :cut, :inner].reshape(width, inner)
+    w_down = weights[:, cut : 2 * cut, inner : inner + channels].reshape(width, channels)
     t_f = t_own[...].astype(F32)
     up_exact = up_raw.astype(BF16)
     for s in range(samples):
@@ -223,11 +214,6 @@
     return results
 
 
-def source(position, core, half):
-    own = position < half
-    return jnp.where(own, 2 * position + core, 2 * (position - half) + 1 - core)
-
-
 def attend_kernel(
     heads,
     factor,
@@ -240,8 +226,7 @@
     tokens_hbm,
     queries,
     d_normed_hbm,
-    got_mine,
-    got_other,
+    got,
     bias_hbm,
     proj,
     keep,
@@ -264,7 +249,7 @@
 ):
     blocks, lines, channels = pooled_y.shape
     samples, _, _, tok, deep = kv.shape
-    chips, height, width = got_mine.shape
+    members, height, width = got.shape
     total = 2 * blocks * tok
     inner = deep // 2
     head_dim = inner // heads
@@ -275,8 +260,8 @@
     first_z = place[0]
     high = place[1]
     core = place[2]
-    tail = w_rest.shape[2]
-    cut = w_down.shape[2]
+    tail = w_rest.shape[1]
+    cut = w_down.shape[1]
     pieces_in = min(4, blocks // 2)
     run = blocks // pieces_in
 
@@ -300,10 +285,8 @@
         copy(bias_hbm, bias, 8),
         copy(tokens_hbm, tokens_in, 9),
         copy(d_normed_hbm, d_normed, 10),
-        copy(got_mine.at[:, height - tail :], w_rest.at[:, core], 11),
-        copy(got_other.at[:, height - tail :], w_rest.at[:, 1 - core], 12),
-        copy(got_mine.at[:, down_rows, down_lanes], w_down.at[:, core], 13),
-        copy(got_other.at[:, down_rows, down_lanes], w_down.at[:, 1 - core], 14),
+        copy(got.at[:, height - tail :], w_rest, 11),
+        copy(got.at[:, down_rows, down_lanes], w_down, 12),
     ]
 
     for piece in range(pieces_in):
@@ -311,7 +294,7 @@
             made.wait()
 
         def step(b, carry):
-            near = lax.rem(first_z + source(b, core, blocks // 2), blocks)
+            near = lax.rem(first_z + b, blocks)
             far = lax.rem(near + high, blocks)
             results = key_value(
                 [pooled_z[near], pooled_y[far]],
@@ -384,9 +367,9 @@
 
     lax.fori_loop(0, samples, forward, 0)
 
-    rest = w_rest[...].reshape(2 * chips * tail, width)
+    rest = w_rest[...].reshape(members * tail, width)
     down = w_down[...].reshape(width, channels)
-    pick = select(inner, 2 * chips * tail, inner // (2 * chips), tail, 0)
+    pick = select(inner, members * tail, inner // members, tail, 0)
     mixed_wide = dot(mixed[...], pick).astype(BF16)
     normed_out, inverse_out = normalize(tokens_in[...] + dot(mixed_wide, rest))
     proj[...] = dot(normed_out.astype(BF16), down).astype(BF16)
@@ -496,6 +479,17 @@
     up = [(i, i + 1) for i in range(n_rows - 1)]
     down = [(i + 1, i) for i in range(n_rows - 1)]
 
+    tail = w_out.shape[0] + w_up.shape[0]
+    shard = pl.pallas_call(
+        pack_kernel,
+        out_shape=shape((2 * tok + 2 * w_query.shape[0] + tail, width), BF16),
+        in_specs=[WHOLE] * 8,
+        out_specs=WHOLE,
+        compiler_params=params(),
+        name="pack",
+    )(fetched[0], fetched[1], w_query, w_key, w_value, w_down, w_out, w_up)
+    got = lax.all_gather(shard, "samp", axis=0, tiled=False)
+    left, right, _ = lax.optimization_barrier((left, right, shard))
 
     from_left = lax.ppermute(right, "rows", up)
     from_right = lax.ppermute(left, "rows", down)
@@ -507,24 +501,11 @@
         compiler_params=params(),
         name="settle",
     )(own, from_left, from_right)
-    fetched[0], fetched[1], _ = lax.optimization_barrier((fetched[0], fetched[1], left))
-    tail = w_out.shape[0] + w_up.shape[0]
-    shard = pl.pallas_call(
-        pack_kernel,
-        out_shape=shape((2 * tok + 2 * w_query.shape[0] + tail, width), BF16),
-        in_specs=[WHOLE] * 8,
-        out_specs=WHOLE,
-        compiler_params=params(),
-        name="pack",
-    )(fetched[0], fetched[1], w_query, w_key, w_value, w_down, w_out, w_up)
-    pooled, shard = lax.optimization_barrier((pooled, shard))
-    got_mine = lax.all_gather(shard, "samp", axis=0, tiled=False, axis_index_groups=sets)
     z_sets = [[2 * z + y for z in range(n_rows // 2)] for y in range(2)]
     pooled_z = lax.all_gather(pooled, "rows", axis=0, tiled=False, axis_index_groups=z_sets)
     pooled_y = lax.ppermute(pooled_z, "rows", [(r, r ^ 1) for r in range(n_rows)])
 
-    got_mine, _ = lax.optimization_barrier((got_mine, pooled_z))
-    got_other = lax.ppermute(got_mine, "samp", swap)
+    got, pooled_y = lax.optimization_barrier((got, pooled_y))
 
     place = jnp.stack([rank // 2, rank % 2, group % 2]).astype(jnp.int32)
     weight_rows = shard.shape[0] - 2 * tok
@@ -538,21 +519,21 @@
             shape((samples * tok, inner), BF16),
             shape((samples * tok, width), F32),
         ),
-        in_specs=[SCALAR, ANY, ANY] + [WHOLE] * 3,
+        in_specs=[ANY] + [WHOLE] * 3,
         out_specs=(ANY, ANY) + (WHOLE,) * 4,
         scratch_shapes=[
-            pltpu.VMEM((chips, 2, weight_rows, width), BF16),
+            pltpu.VMEM((n_samp, weight_rows, width), BF16),
             pltpu.VMEM((blocks, 2 * tok, width), BF16),
             pltpu.VMEM((width, 2 * inner + channels), BF16),
             pltpu.VMEM((blocks, 2 * tok, 2 * inner), BF16),
             pltpu.VMEM((blocks, 2 * tok, 2 * channels), F32),
-            pltpu.SemaphoreType.DMA((6,)),
+            pltpu.SemaphoreType.DMA((5,)),
             pltpu.SemaphoreType.DMA((8,)),
         ],
         compiler_params=params(),
         cost_estimate=pl.CostEstimate(flops=6 * 10**9, bytes_accessed=16 * 10**6, transcendentals=0),
         name="prep",
-    )(place, got_mine, got_other, pooled, d_token, token_single)
+    )(got, pooled, d_token, token_single)
 
     factor = total / (samples * n_samp)
     rows = heads // 2 * tok
@@ -563,7 +544,7 @@
             shape((chips, heads * tok, 128), BF16),
             shape((chips, heads * tok, 128), BF16),
         ),
-        in_specs=[SCALAR, WHOLE, WHOLE, WHOLE, ANY, ANY, ANY, WHOLE, ANY, ANY, ANY, ANY],
+        in_specs=[SCALAR, WHOLE, WHOLE, WHOLE, ANY, ANY, ANY, WHOLE, ANY, ANY, ANY],
         out_specs=(WHOLE,) * 3,
         scratch_shapes=[
             pltpu.VMEM((blocks, 2 * tok, 2 * inner), BF16),
@@ -572,15 +553,15 @@
             pltpu.VMEM((heads * tok, total), BF16),
             pltpu.VMEM((samples * tok, width), F32),
             pltpu.VMEM((samples * tok, width), F32),
-            pltpu.VMEM((chips, 2, tail, width), BF16),
-            pltpu.VMEM((chips, 2, w_down.shape[0], channels), BF16),
+            pltpu.VMEM((n_samp, tail, width), BF16),
+            pltpu.VMEM((n_samp, w_down.shape[0], channels), BF16),
             pltpu.VMEM((2, rows, total), F32),
             pltpu.VMEM((samples, 2, rows, total), BF16),
             pltpu.VMEM((samples, 2, rows, 256), F32),
             pltpu.VMEM((samples, 2, rows, 128), F32),
             pltpu.VMEM((samples * tok, inner), BF16),
             pltpu.VMEM((samples * tok, inner), BF16),
-            pltpu.SemaphoreType.DMA((15,)),
+            pltpu.SemaphoreType.DMA((13,)),
         ],
         compiler_params=params(),
         name="attend",
@@ -594,8 +575,7 @@
         tokens_in,
         queries,
         d_normed,
-        got_mine,
-        got_other,
+        got,
         pair_bias.reshape(heads * tok, total),
     )
 

time: 239 us -> 203 us (0.85)
  the two profiles are of different devices: /device:TPU:37 before, /device:TPU:5 now
where the time goes in v4:
time: 203 us
  starting transfers between devices  60.4 us (30%)
  Pallas kernels  49 us (24%)
  waiting for transfers between devices  37.1 us (18%)
  blocking collectives  33.4 us (16%)
  between operations  14.8 us (7%)
  other arithmetic  5.25 us (3%)
  local copies, waits for them, and re-layouts  2.76 us (1%)
    all_gather x1, blocking collectives, local(): lax.all_gather(pooled, 'rows', axis=0, tiled=False, axis_index_groups=z_s...  33.4 us
    pallas_call x1, Pallas kernels, local(): pl.pallas_call(functools.partial(attend_kernel, heads, factor), out_shape...  29.4 us
    ppermute x2, starting transfers between devices, local(): fetched.append(lax.ppermute(token_single, ('rows', 'samp'), perm))  22.5 us
    pallas_call x1, Pallas kernels, local(): pl.pallas_call(functools.partial(prep_kernel, inner // heads), out_shape=...  11.3 us
    ppermute x1, waiting for transfers between devices, local(): lax.ppermute(pooled_z, 'rows', [(r, r ^ 1) for r in range(n_rows)])  10.9 us
    ppermute x1, starting transfers between devices, local(): other = lax.ppermute(send, 'samp', swap)  9.94 us
    ppermute x1, starting transfers between devices, local(): from_left = lax.ppermute(right, 'rows', up)  9.74 us
    ppermute x2, waiting for transfers between devices, local(): fetched.append(lax.ppermute(token_single, ('rows', 'samp'), perm))  8.76 us
  transfers between devices with their start and end apart: 10, of which 7 were waited for; matrix products, arithmetic and copies ran while one was open for 1% of the time, Pallas kernels for 3%

profile of v4, /device:TPU:5, one launch (start us, length us, event | category | flops | bytes accessed | tf_op | source)
XLA Modules:
  0.0 202.8 jit_solution(15149486493289981094)
XLA Ops:
  7.2 12.9 %collective-permute-start = (bf16[64,768]{1,0:T(8,128)(2,1)}, bf16[64,768]{1,0:T(8,128)(2,1)S(1)}, u32[]{:S(2)}, u32[]{:S(2)}) collective-permute-start(bf16[64,768]{1,0:T(8,128)(2,1)} %t_own.1), channel_id=1, source_target_pairs={{0,0},{33,1},{66,2},{99,3},{132,4},{165,5},{198,6},{231,7},{264,8}... | collective-permute-start | bytes 294920 | tf_op jit(solution)/shard_map/ppermute | solution.py:461
  20.1 9.7 %collective-permute-start.1 = (bf16[64,768]{1,0:T(8,128)(2,1)}, bf16[64,768]{1,0:T(8,128)(2,1)S(1)}, u32[]{:S(2)}, u32[]{:S(2)}) collective-permute-start(bf16[64,768]{1,0:T(8,128)(2,1)} %t_own.1), channel_id=1, source_target_pairs={{16,0},{49,1},{82,2},{115,3},{148,4},{181,5},{214,6},{247,7},{280,... | collective-permute-start | bytes 294920 | tf_op jit(solution)/shard_map/ppermute | solution.py:461
  29.8 8.8 %collective-permute-done.1.far = bf16[64,768]{1,0:T(8,128)(2,1)S(1)} collective-permute-done((bf16[64,768]{1,0:T(8,128)(2,1)}, bf16[64,768]{1,0:T(8,128)(2,1)S(1)}, u32[]{:S(2)}, u32[]{:S(2)}) %collective-permute-start.1) | collective-permute-done | bytes 98336 | tf_op jit(solution)/shard_map/ppermute | solution.py:461
  39.2 1.8 pack.1
  41.6 1.3 broadcast_subtract_fusion
  42.9 2.7 %pool.1 = (bf16[3,512,128]{2,1,0:T(8,128)(2,1)}, f32[7,64,128]{2,1,0:T(8,128)}, f32[7,32,128]{2,1,0:T(8,128)}, f32[7,32,128]{2,1,0:T(8,128)}) custom-call(s32[1]{0:T(128)S(6)} %copy.17.count, s32[1,512]{1,0:T(1,128)} %bitcast.18, bf16[3,512,128]{2,1,0:T(8,128)(2,1)} %noised.1, bf16[512,128]{1,0:T(8,128)(2,1)} %single.1, bf16[128,128]{1,0:T(8,128)(2,1)} %w_atom.1, ...), custom_call_target="tpu_custom_call" | custom-call | tf_op jit(solution)/shard_map/pool/pallas_call | solution.py:466
  45.6 9.7 %collective-permute-start.2 = (f32[7,32,128]{2,1,0:T(8,128)}, f32[7,32,128]{2,1,0:T(8,128)S(1)}, u32[]{:S(2)}, u32[]{:S(2)}) collective-permute-start(f32[7,32,128]{2,1,0:T(8,128)} %get-tuple-element.25), channel_id=1, source_target_pairs={{0,16},{16,32},{32,48},{48,64},{64,80},{80,96},{96,112},{112,128},... | collective-permute-start | bytes 344072 | tf_op jit(solution)/shard_map/ppermute | solution.py:494
  55.3 1.3 collective-permute-start.3
  57.4 5.2 %collective-permute-done.3.from_right = f32[7,32,128]{2,1,0:T(8,128)S(1)} collective-permute-done((f32[7,32,128]{2,1,0:T(8,128)}, f32[7,32,128]{2,1,0:T(8,128)S(1)}, u32[]{:S(2)}, u32[]{:S(2)}) %collective-permute-start.3) | collective-permute-done | bytes 114720 | tf_op jit(solution)/shard_map/ppermute | solution.py:495
  63.2 1.7 settle.1
  64.9 33.4 %all-gather = bf16[3072,128]{1,0:T(8,128)(2,1)S(1)} all-gather(bf16[192,128]{1,0:T(8,128)(2,1)} %get-tuple-element.27.pooled), channel_id=2, replica_groups={{0,32,64,96,128,160,192,224,256,288,320,352,384,416,448,480},{16,48,80,..., dimensions={0}, use_global_device_ids=true | all-gather | bytes 835584 | tf_op jit(solution)/shard_map/all_gather | solution.py:505
  98.3 3.7 %collective-permute-start.4 = (bf16[16,192,128]{2,1,0:T(8,128)(2,1)S(1)}, bf16[16,192,128]{2,1,0:T(8,128)(2,1)S(1)}, u32[]{:S(2)}, u32[]{:S(2)}) collective-permute-start(bf16[16,192,128]{2,1,0:T(8,128)(2,1)S(1)} %bitcast.12), channel_id=1, source_target_pairs={{0,16},{16,0},{32,48},{48,32},{64,80},{80,64},{96,112},{112,96},{1... | collective-permute-start | bytes 2359304 | tf_op jit(solution)/shard_map/ppermute | solution.py:506
  102.7 10.9 %collective-permute-done.4.pooled_y = bf16[16,192,128]{2,1,0:T(8,128)(2,1)S(1)} collective-permute-done((bf16[16,192,128]{2,1,0:T(8,128)(2,1)S(1)}, bf16[16,192,128]{2,1,0:T(8,128)(2,1)S(1)}, u32[]{:S(2)}, u32[]{:S(2)}) %collective-permute-start.4) | collective-permute-done | bytes 786464 | tf_op jit(solution)/shard_map/ppermute | solution.py:506
  113.6 11.3 %prep.1 = (bf16[16,128,768]{2,1,0:T(8,128)(2,1)}, f32[16,128,256]{2,1,0:T(8,128)}, bf16[128,1024]{1,0:T(8,128)(2,1)}, f32[192,768]{1,0:T(8,128)}, bf16[192,384]{1,0:T(8,128)(2,1)}, /*index=5*/f32[192,768]{1,0:T(8,128)}) custom-call(bf16[16,256,768]{2,1,0:T(8,128)(2,1)} %bitcast.10, bf16[192,128]{1,0:T(8,128)(2,1)} %get-tuple-element.27.pooled, ...), custom_call_target="tpu_custom_call" | custom-call | flops 6000000000 | bytes 16000000 | tf_op jit(solution)/shard_map/prep/pallas_call | solution.py:512
  124.9 29.4 %attend.1 = (bf16[192,128]{1,0:T(8,128)(2,1)}, bf16[8,512,128]{2,1,0:T(8,128)(2,1)}, bf16[8,512,128]{2,1,0:T(8,128)(2,1)}) custom-call(s32[3]{0:T(128)} %pad_add_fusion.place, bf16[16,192,128]{2,1,0:T(8,128)(2,1)} %bitcast.13, bf16[16,192,128]{2,1,0:T(8,128)(2,1)} %copy-done.1, bf16[128,1024]{1,0:T(8,128)(2,1)} %get-tuple-element.31.w_mix, ...), custom_call_target="tpu_custom_call" | custom-call | tf_op jit(solution)/shard_map/attend/pallas_call | solution.py:540
  154.4 9.9 %collective-permute-start.7 = (bf16[8,512,128]{2,1,0:T(8,128)(2,1)}, bf16[8,512,128]{2,1,0:T(8,128)(2,1)S(1)}, u32[]{:S(2)}, u32[]{:S(2)}) collective-permute-start(bf16[8,512,128]{2,1,0:T(8,128)(2,1)} %get-tuple-element.39), channel_id=1, source_target_pairs={{0,1},{1,0},{2,3},{3,2},{4,5},{5,4},{6,7},{7,6},{8,9},{9,8},{10,11... | collective-permute-start | bytes 3145736 | tf_op jit(solution)/shard_map/ppermute | solution.py:582
  164.3 2.5 %collective-permute-done.7 = bf16[8,512,128]{2,1,0:T(8,128)(2,1)S(1)} collective-permute-done((bf16[8,512,128]{2,1,0:T(8,128)(2,1)}, bf16[8,512,128]{2,1,0:T(8,128)(2,1)S(1)}, u32[]{:S(2)}, u32[]{:S(2)}) %collective-permute-start.7) | collective-permute-done | bytes 1048608 | tf_op jit(solution)/shard_map/ppermute | solution.py:582
  166.8 2.5 %add_convert_fusion = bf16[8,512,128]{2,1,0:T(8,128)(2,1)} fusion(bf16[8,512,128]{2,1,0:T(8,128)(2,1)S(1)} %collective-permute-done.7, bf16[8,512,128]{2,1,0:T(8,128)(2,1)} %get-tuple-element.38), kind=kLoop, calls=%fused_computation.1 | loop fusion | flops 2097152 | bytes 3145728 | tf_op jit(solution)/shard_map/convert_element_type | solution.py:583
  169.3 6.1 %all-to-all-start = ((bf16[8,512,128]{2,1,0:T(8,128)(2,1)}), bf16[8,512,128]{2,1,0:T(8,128)(2,1)S(1)}, u32[]{:S(2)}, u32[]{:S(2)}) async-start(bf16[8,512,128]{2,1,0:T(8,128)(2,1)} %add_convert_fusion), calls=%async_computation | async-start | bytes 2097152 | tf_op jit(solution)/shard_map/all_to_all | solution.py:584
  175.4 5.8 %collective-permute-start.5 = (bf16[3,32,128]{2,1,0:T(8,128)(2,1)S(1)}, bf16[3,32,128]{2,1,0:T(8,128)(2,1)S(1)}, u32[]{:S(2)}, u32[]{:S(2)}) collective-permute-start(bf16[3,32,128]{2,1,0:T(8,128)(2,1)S(1)} %get-tuple-element.41), channel_id=1, source_target_pairs={{0,16},{16,32},{32,48},{48,64},{64,80},{80,96},{96,112},{112,128},... | collective-permute-start | bytes 73736 | tf_op jit(solution)/shard_map/ppermute | solution.py:588
  181.1 1.3 collective-permute-start.6
  183.3 5.0 %collective-permute-done.5.from_left = bf16[3,32,128]{2,1,0:T(8,128)(2,1)S(1)} collective-permute-done((bf16[3,32,128]{2,1,0:T(8,128)(2,1)S(1)}, bf16[3,32,128]{2,1,0:T(8,128)(2,1)S(1)}, u32[]{:S(2)}, u32[]{:S(2)}) %collective-permute-start.5) | collective-permute-done | bytes 24608 | tf_op jit(solution)/shard_map/ppermute | solution.py:588
  188.3 4.1 %collective-permute-done.6.from_right = bf16[3,32,128]{2,1,0:T(8,128)(2,1)S(1)} collective-permute-done((bf16[3,32,128]{2,1,0:T(8,128)(2,1)S(1)}, bf16[3,32,128]{2,1,0:T(8,128)(2,1)S(1)}, u32[]{:S(2)}, u32[]{:S(2)}) %collective-permute-start.6) | collective-permute-done | bytes 24608 | tf_op jit(solution)/shard_map/ppermute | solution.py:589
  192.9 2.2 %decode.1 = bf16[3,512,128]{2,1,0:T(8,128)(2,1)} custom-call(s32[1]{0:T(128)S(6)} %copy.17.count, s32[512,1]{1,0:T(8,128)} %copy.16.token, bf16[3,512,128]{2,1,0:T(8,128)(2,1)} %get-tuple-element.21.hidden, bf16[3,64,128]{2,1,0:T(8,128)(2,1)} %bitcast.16, bf16[3,32,128]{2,1,0:T(8,128)(2,1)} %copy-done.7, bf16[3,32,128]{2,1,0:T(8,128)(2,1)} %copy-done.8), custom_call_target="tpu_custom_call" | custom-call | tf_op jit(solution)/shard_map/decode/pallas_call | solution.py:590
  (30 shorter events, 5.1 us)
Async XLA Ops:
  7.2 106.4 %all-gather.4.cloned.1.call-start = ((), (), s32[]{:S(2)}) async-start(), calls=%async_computation.1 | async-start | bytes 6684672 | tf_op jit(solution)/shard_map/all_gather | solution.py:491
  7.2 22.6 %collective-permute-start = (bf16[64,768]{1,0:T(8,128)(2,1)}, bf16[64,768]{1,0:T(8,128)(2,1)S(1)}, u32[]{:S(2)}, u32[]{:S(2)}) collective-permute-start(bf16[64,768]{1,0:T(8,128)(2,1)} %t_own.1), channel_id=1, source_target_pairs={{0,0},{33,1},{66,2},{99,3},{132,4},{165,5},{198,6},{231,7},{264,8}... | collective-permute-start | bytes 294920 | tf_op jit(solution)/shard_map/ppermute | solution.py:461
  20.1 18.5 %collective-permute-start.1 = (bf16[64,768]{1,0:T(8,128)(2,1)}, bf16[64,768]{1,0:T(8,128)(2,1)S(1)}, u32[]{:S(2)}, u32[]{:S(2)}) collective-permute-start(bf16[64,768]{1,0:T(8,128)(2,1)} %t_own.1), channel_id=1, source_target_pairs={{16,0},{49,1},{82,2},{115,3},{148,4},{181,5},{214,6},{247,7},{280,... | collective-permute-start | bytes 294920 | tf_op jit(solution)/shard_map/ppermute | solution.py:461
  29.8 8.8 %copy-start.5 = (bf16[64,768]{1,0:T(8,128)(2,1)}, bf16[64,768]{1,0:T(8,128)(2,1)S(1)}, u32[]{:S(2)}) copy-start(bf16[64,768]{1,0:T(8,128)(2,1)S(1)} %collective-permute-done.near) | copy-start | bytes 294916
  38.6 0.6 copy-start.6
  45.6 11.8 %collective-permute-start.2 = (f32[7,32,128]{2,1,0:T(8,128)}, f32[7,32,128]{2,1,0:T(8,128)S(1)}, u32[]{:S(2)}, u32[]{:S(2)}) collective-permute-start(f32[7,32,128]{2,1,0:T(8,128)} %get-tuple-element.25), channel_id=1, source_target_pairs={{0,16},{16,32},{32,48},{48,64},{64,80},{80,96},{96,112},{112,128},... | collective-permute-start | bytes 344072 | tf_op jit(solution)/shard_map/ppermute | solution.py:494
  55.3 7.3 %collective-permute-start.3 = (f32[7,32,128]{2,1,0:T(8,128)}, f32[7,32,128]{2,1,0:T(8,128)S(1)}, u32[]{:S(2)}, u32[]{:S(2)}) collective-permute-start(f32[7,32,128]{2,1,0:T(8,128)} %get-tuple-element.26), channel_id=1, source_target_pairs={{16,0},{32,16},{48,32},{64,48},{80,64},{96,80},{112,96},{128,112},... | collective-permute-start | bytes 344072 | tf_op jit(solution)/shard_map/ppermute | solution.py:495
  57.4 5.2 %copy-start.3 = (f32[7,32,128]{2,1,0:T(8,128)}, f32[7,32,128]{2,1,0:T(8,128)S(1)}, u32[]{:S(2)}) copy-start(f32[7,32,128]{2,1,0:T(8,128)S(1)} %collective-permute-done.2.from_left) | copy-start | bytes 344068
  62.6 0.6 copy-start.4
  98.3 26.6 %copy-start = (bf16[3072,128]{1,0:T(8,128)(2,1)}, bf16[3072,128]{1,0:T(8,128)(2,1)S(1)}, u32[]{:S(2)}) copy-start(bf16[3072,128]{1,0:T(8,128)(2,1)S(1)} %all-gather) | copy-start | bytes 2359300
  98.3 15.3 %collective-permute-start.4 = (bf16[16,192,128]{2,1,0:T(8,128)(2,1)S(1)}, bf16[16,192,128]{2,1,0:T(8,128)(2,1)S(1)}, u32[]{:S(2)}, u32[]{:S(2)}) collective-permute-start(bf16[16,192,128]{2,1,0:T(8,128)(2,1)S(1)} %bitcast.12), channel_id=1, source_target_pairs={{0,16},{16,0},{32,48},{48,32},{64,80},{80,64},{96,112},{112,96},{1... | collective-permute-start | bytes 2359304 | tf_op jit(solution)/shard_map/ppermute | solution.py:506
  113.6 11.4 %copy-start.1 = (bf16[16,192,128]{2,1,0:T(8,128)(2,1)}, bf16[16,192,128]{2,1,0:T(8,128)(2,1)S(1)}, u32[]{:S(2)}) copy-start(bf16[16,192,128]{2,1,0:T(8,128)(2,1)S(1)} %collective-permute-done.4.pooled_y) | copy-start | bytes 2359300
  154.4 12.4 %collective-permute-start.7 = (bf16[8,512,128]{2,1,0:T(8,128)(2,1)}, bf16[8,512,128]{2,1,0:T(8,128)(2,1)S(1)}, u32[]{:S(2)}, u32[]{:S(2)}) collective-permute-start(bf16[8,512,128]{2,1,0:T(8,128)(2,1)} %get-tuple-element.39), channel_id=1, source_target_pairs={{0,1},{1,0},{2,3},{3,2},{4,5},{5,4},{6,7},{7,6},{8,9},{9,8},{10,11... | collective-permute-start | bytes 3145736 | tf_op jit(solution)/shard_map/ppermute | solution.py:582
  166.8 8.6 %copy-start.2 = (bf16[192,128]{1,0:T(8,128)(2,1)S(1)}, bf16[192,128]{1,0:T(8,128)(2,1)}, u32[]{:S(2)}) copy-start(bf16[192,128]{1,0:T(8,128)(2,1)} %get-tuple-element.37) | copy-start | bytes 147460
  166.8 15.6 %copy-start.9 = (s32[512]{0:T(512)S(1)}, s32[512]{0:T(512)}, u32[]{:S(2)}) copy-start(s32[512]{0:T(512)} %broadcast_subtract_fusion) | copy-start | bytes 6148
  169.3 25.8 %all-to-all-start = ((bf16[8,512,128]{2,1,0:T(8,128)(2,1)}), bf16[8,512,128]{2,1,0:T(8,128)(2,1)S(1)}, u32[]{:S(2)}, u32[]{:S(2)}) async-start(bf16[8,512,128]{2,1,0:T(8,128)(2,1)} %add_convert_fusion), calls=%async_computation | async-start | bytes 2097152 | tf_op jit(solution)/shard_map/all_to_all | solution.py:584
  175.4 12.9 %collective-permute-start.5 = (bf16[3,32,128]{2,1,0:T(8,128)(2,1)S(1)}, bf16[3,32,128]{2,1,0:T(8,128)(2,1)S(1)}, u32[]{:S(2)}, u32[]{:S(2)}) collective-permute-start(bf16[3,32,128]{2,1,0:T(8,128)(2,1)S(1)} %get-tuple-element.41), channel_id=1, source_target_pairs={{0,16},{16,32},{32,48},{48,64},{64,80},{80,96},{96,112},{112,128},... | collective-permute-start | bytes 73736 | tf_op jit(solution)/shard_map/ppermute | solution.py:588
  181.1 11.2 %collective-permute-start.6 = (bf16[3,32,128]{2,1,0:T(8,128)(2,1)S(1)}, bf16[3,32,128]{2,1,0:T(8,128)(2,1)S(1)}, u32[]{:S(2)}, u32[]{:S(2)}) collective-permute-start(bf16[3,32,128]{2,1,0:T(8,128)(2,1)S(1)} %get-tuple-element.40), channel_id=1, source_target_pairs={{16,0},{32,16},{48,32},{64,48},{80,64},{96,80},{112,96},{128,112},... | collective-permute-start | bytes 73736 | tf_op jit(solution)/shard_map/ppermute | solution.py:589
  188.2 4.1 %copy-start.7 = (bf16[3,32,128]{2,1,0:T(8,128)(2,1)}, bf16[3,32,128]{2,1,0:T(8,128)(2,1)S(1)}, u32[]{:S(2)}) copy-start(bf16[3,32,128]{2,1,0:T(8,128)(2,1)S(1)} %collective-permute-done.5.from_left) | copy-start | bytes 73732
  192.3 0.6 copy-start.8
Sparse Core Ops, SparseCore 0:
  41.1 71.4 all-gather.3

commit v5 on v4

--- a/solution.py
+++ b/solution.py
@@ -86,63 +86,28 @@
     return jnp.where(column == group * padded + offset + (line - group * size), 1.0, 0.0).astype(BF16)
 
 
-def pack_kernel(near, far, w_query, w_key, w_value, w_down, w_out, w_up, out):
-    tok, width = near.shape
+def pack_kernel(w_query, w_key, w_value, w_down, w_out, w_up, out):
     cut, inner = w_query.shape
+    width = out.shape[1]
     end = inner + w_down.shape[1]
-    out[:tok] = near[...]
-    out[tok : 2 * tok] = far[...]
-    first = slice(2 * tok, 2 * tok + cut)
-    second = slice(2 * tok + cut, 2 * tok + 2 * cut)
-    out[first, :inner] = w_query[...]
-    out[first, inner:] = w_key[...]
-    out[second, :inner] = w_value[...]
-    out[second, inner:end] = w_down[...]
-    out[second, end:] = jnp.zeros((cut, width - end), BF16)
+    out[:cut, :inner] = w_query[...]
+    out[:cut, inner:] = w_key[...]
+    out[cut : 2 * cut, :inner] = w_value[...]
+    out[cut : 2 * cut, inner:end] = w_down[...]
+    out[cut : 2 * cut, end:] = jnp.zeros((cut, width - end), BF16)
     both = jnp.concatenate([w_out[...].astype(F32), w_up[...].astype(F32)], axis=0)
-    out[2 * tok + 2 * cut :] = both.astype(BF16)
-
-
-def prep_kernel(
-    head_dim,
-    got,
-    pooled,
-    d_token,
-    t_own,
-    base_hbm,
-    extra_hbm,
-    w_mix,
-    tokens_in,
-    queries,
-    d_normed,
-    weights,
-    t_all,
-    w_big,
-    base,
-    extra,
-    in_sems,
-    out_sems,
-):
-    members, height, width = got.shape
+    out[2 * cut :] = both.astype(BF16)
+
+
+def prep_kernel(head_dim, weights, pooled, d_token, t_own, w_big, w_mix, tokens_in, queries, d_normed):
+    members, height, width = weights.shape
     tok = t_own.shape[0]
-    block = 2 * tok
     channels = pooled.shape[1]
     samples = pooled.shape[0] // tok
     inner = queries.shape[1]
     cut = width // members
-    tail = weights.shape[1] - 2 * cut
+    tail = height - 2 * cut
     up_rows = channels // members
-    run = members // 4
-
-    weight_copies = [pltpu.make_async_copy(got.at[:, block:], weights, in_sems.at[0])]
-    t_copies = []
-    for i in range(4):
-        part = pl.ds(i * run, run)
-        t_copies.append(pltpu.make_async_copy(got.at[part, :block], t_all.at[part], in_sems.at[1 + i]))
-    for copy in weight_copies + t_copies:
-        copy.start()
-    for copy in weight_copies:
-        copy.wait()
 
     rest = weights[:, 2 * cut :, :].reshape(members * tail, width)
     up_raw = dot(select(channels, members * tail, up_rows, tail, tail - up_rows), rest)
@@ -157,31 +122,6 @@
     w_mix[:, 2 * inner : 2 * inner + channels] = high
     w_mix[:, 2 * inner + channels :] = (gram - high.astype(F32)).astype(BF16)
 
-    outs = []
-    for i in range(4):
-        t_copies[i].wait()
-
-        def step(k, carry):
-            at = i * run + 2 * k
-            t = t_all[pl.ds(at, 2)].reshape(2 * block, width).astype(F32)
-            cent = (t - jnp.mean(t, axis=-1, keepdims=True)).astype(BF16)
-            both = dot(cent, w_big[...])
-            base[pl.ds(at, 2)] = both[:, : 2 * inner].astype(BF16).reshape(2, block, 2 * inner)
-            wide = cent.astype(F32)
-            square = jnp.sum(wide * wide, axis=-1, keepdims=True) * (1.0 / width)
-            extra[pl.ds(at, 2), :, :channels] = (both[:, 2 * inner :] * (2.0 / width)).reshape(2, block, channels)
-            extra[pl.ds(at, 2), :, channels:] = jnp.broadcast_to(square, (2 * block, channels)).reshape(
-                2, block, channels
-            )
-            return carry
-
-        lax.fori_loop(0, run // 2, step, 0)
-        part = pl.ds(i * run, run)
-        outs.append(pltpu.make_async_copy(base.at[part], base_hbm.at[part], out_sems.at[2 * i]))
-        outs.append(pltpu.make_async_copy(extra.at[part], extra_hbm.at[part], out_sems.at[2 * i + 1]))
-        outs[-2].start()
-        outs[-1].start()
-
     w_query = weights[:, :cut, :inner].reshape(width, inner)
     w_down = weights[:, cut : 2 * cut, inner : inner + channels].reshape(width, channels)
     t_f = t_own[...].astype(F32)
@@ -192,8 +132,6 @@
     normed, _ = normalize(tokens_in[...])
     queries[...] = (dot(normed.astype(BF16), w_query) * (head_dim**-0.5)).astype(BF16)
     d_normed[...] = dot_nt(d_token[...], w_down)
-    for copy in outs:
-        copy.wait()
 
 
 def key_value(tables, bases, extras, w_mix):
@@ -221,8 +159,8 @@
     pooled_z,
     pooled_y,
     w_mix,
-    base_hbm,
-    extra_hbm,
+    w_big_hbm,
+    got_t,
     tokens_hbm,
     queries,
     d_normed_hbm,
@@ -231,6 +169,8 @@
     proj,
     keep,
     send,
+    w_big,
+    t_all,
     base,
     extra,
     kv,
@@ -270,44 +210,50 @@
         made.start()
         return made
 
+    big_copy = copy(w_big_hbm, w_big, 8)
     copies = []
     for piece in range(pieces_in):
         part = pl.ds(piece * run, run)
-        copies.append(
-            (
-                copy(base_hbm.at[part], base.at[part], 2 * piece),
-                copy(extra_hbm.at[part], extra.at[part], 2 * piece + 1),
-            )
-        )
+        copies.append(copy(got_t.at[part], t_all.at[part], piece))
     down_rows = slice(height - tail - cut, height - tail)
     down_lanes = slice(inner, inner + channels)
     late = [
-        copy(bias_hbm, bias, 8),
+        copy(bias_hbm, bias, 7),
         copy(tokens_hbm, tokens_in, 9),
         copy(d_normed_hbm, d_normed, 10),
         copy(got.at[:, height - tail :], w_rest, 11),
         copy(got.at[:, down_rows, down_lanes], w_down, 12),
     ]
 
+    big_copy.wait()
+    block = 2 * tok
     for piece in range(pieces_in):
-        for made in copies[piece]:
-            made.wait()
-
-        def step(b, carry):
-            near = lax.rem(first_z + b, blocks)
-            far = lax.rem(near + high, blocks)
-            results = key_value(
-                [pooled_z[near], pooled_y[far]],
-                [base[b, :tok], base[b, tok:]],
-                [extra[b, :tok], extra[b, tok:]],
-                w_mix[...],
-            )
-            for s in range(samples):
-                kv[s, near, high] = results[0][s * tok : (s + 1) * tok]
-                kv[s, far, 1 - high] = results[1][s * tok : (s + 1) * tok]
-            return carry
-
-        lax.fori_loop(piece * run, (piece + 1) * run, step, 0)
+        copies[piece].wait()
+        part = slice(piece * run, (piece + 1) * run)
+        t = t_all[part].reshape(run * block, width).astype(F32)
+        cent = (t - jnp.mean(t, axis=-1, keepdims=True)).astype(BF16)
+        both = dot(cent, w_big[...])
+        base[part] = both[:, :deep].astype(BF16).reshape(run, block, deep)
+        wide = cent.astype(F32)
+        square = jnp.sum(wide * wide, axis=-1, keepdims=True) * (1.0 / width)
+        extra[part, :, :channels] = (both[:, deep:] * (2.0 / width)).reshape(run, block, channels)
+        extra[part, :, channels:] = jnp.broadcast_to(square, (run * block, channels)).reshape(run, block, channels)
+
+    def step(b, carry):
+        near = lax.rem(first_z + b, blocks)
+        far = lax.rem(near + high, blocks)
+        results = key_value(
+            [pooled_z[near], pooled_y[far]],
+            [base[b, :tok], base[b, tok:]],
+            [extra[b, :tok], extra[b, tok:]],
+            w_mix[...],
+        )
+        for s in range(samples):
+            kv[s, near, high] = results[0][s * tok : (s + 1) * tok]
+            kv[s, far, 1 - high] = results[1][s * tok : (s + 1) * tok]
+        return carry
+
+    lax.fori_loop(0, blocks, step, 0)
     for made in late:
         made.wait()
 
@@ -451,6 +397,19 @@
     sets = [[2 * m + c for m in range(chips)] for c in range(2)]
     swap = [(s, s ^ 1) for s in range(n_samp)]
 
+    shape = jax.ShapeDtypeStruct
+    tail = w_out.shape[0] + w_up.shape[0]
+    w_own = pl.pallas_call(
+        pack_kernel,
+        out_shape=shape((2 * w_query.shape[0] + tail, width), BF16),
+        in_specs=[WHOLE] * 6,
+        out_specs=WHOLE,
+        compiler_params=params(),
+        name="pack",
+    )(w_query, w_key, w_value, w_down, w_out, w_up)
+    w_own, atom_noised = lax.optimization_barrier((w_own, atom_noised))
+    got = lax.all_gather(w_own, "samp", axis=0, tiled=False)
+
     fetched = []
     for part in range(2):
         perm = [
@@ -461,7 +420,6 @@
         fetched.append(lax.ppermute(token_single, ("rows", "samp"), perm))
 
     local_token = atom_token - (rank * tok - margin)
-    shape = jax.ShapeDtypeStruct
     sums = 2 * samples + 1
     hidden, own, left, right = pl.pallas_call(
         pool_kernel,
@@ -479,18 +437,6 @@
     up = [(i, i + 1) for i in range(n_rows - 1)]
     down = [(i + 1, i) for i in range(n_rows - 1)]
 
-    tail = w_out.shape[0] + w_up.shape[0]
-    shard = pl.pallas_call(
-        pack_kernel,
-        out_shape=shape((2 * tok + 2 * w_query.shape[0] + tail, width), BF16),
-        in_specs=[WHOLE] * 8,
-        out_specs=WHOLE,
-        compiler_params=params(),
-        name="pack",
-    )(fetched[0], fetched[1], w_query, w_key, w_value, w_down, w_out, w_up)
-    got = lax.all_gather(shard, "samp", axis=0, tiled=False)
-    left, right, _ = lax.optimization_barrier((left, right, shard))
-
     from_left = lax.ppermute(right, "rows", up)
     from_right = lax.ppermute(left, "rows", down)
     pooled, d_token = pl.pallas_call(
@@ -501,37 +447,30 @@
         compiler_params=params(),
         name="settle",
     )(own, from_left, from_right)
+    fetched[0], fetched[1], pooled = lax.optimization_barrier((fetched[0], fetched[1], pooled))
+    t_own_pair = jnp.concatenate(fetched, axis=0)
+    pooled, t_own_pair = lax.optimization_barrier((pooled, t_own_pair))
+    got_t = lax.all_gather(t_own_pair, "samp", axis=0, tiled=False)
     z_sets = [[2 * z + y for z in range(n_rows // 2)] for y in range(2)]
     pooled_z = lax.all_gather(pooled, "rows", axis=0, tiled=False, axis_index_groups=z_sets)
     pooled_y = lax.ppermute(pooled_z, "rows", [(r, r ^ 1) for r in range(n_rows)])
 
-    got, pooled_y = lax.optimization_barrier((got, pooled_y))
+    got_t, pooled_y = lax.optimization_barrier((got_t, pooled_y))
 
     place = jnp.stack([rank // 2, rank % 2, group % 2]).astype(jnp.int32)
-    weight_rows = shard.shape[0] - 2 * tok
-    base, extra, w_mix, tokens_in, queries, d_normed = pl.pallas_call(
+    w_big, w_mix, tokens_in, queries, d_normed = pl.pallas_call(
         functools.partial(prep_kernel, inner // heads),
         out_shape=(
-            shape((blocks, 2 * tok, 2 * inner), BF16),
-            shape((blocks, 2 * tok, 2 * channels), F32),
+            shape((width, 2 * inner + channels), BF16),
             shape((channels, 2 * inner + 2 * channels), BF16),
             shape((samples * tok, width), F32),
             shape((samples * tok, inner), BF16),
             shape((samples * tok, width), F32),
         ),
-        in_specs=[ANY] + [WHOLE] * 3,
-        out_specs=(ANY, ANY) + (WHOLE,) * 4,
-        scratch_shapes=[
-            pltpu.VMEM((n_samp, weight_rows, width), BF16),
-            pltpu.VMEM((blocks, 2 * tok, width), BF16),
-            pltpu.VMEM((width, 2 * inner + channels), BF16),
-            pltpu.VMEM((blocks, 2 * tok, 2 * inner), BF16),
-            pltpu.VMEM((blocks, 2 * tok, 2 * channels), F32),
-            pltpu.SemaphoreType.DMA((5,)),
-            pltpu.SemaphoreType.DMA((8,)),
-        ],
+        in_specs=[WHOLE] * 4,
+        out_specs=(WHOLE,) * 5,
         compiler_params=params(),
-        cost_estimate=pl.CostEstimate(flops=6 * 10**9, bytes_accessed=16 * 10**6, transcendentals=0),
+        cost_estimate=pl.CostEstimate(flops=2 * 10**9, bytes_accessed=8 * 10**6, transcendentals=0),
         name="prep",
     )(got, pooled, d_token, token_single)
 
@@ -547,6 +486,8 @@
         in_specs=[SCALAR, WHOLE, WHOLE, WHOLE, ANY, ANY, ANY, WHOLE, ANY, ANY, ANY],
         out_specs=(WHOLE,) * 3,
         scratch_shapes=[
+            pltpu.VMEM((width, 2 * inner + channels), BF16),
+            pltpu.VMEM((blocks, 2 * tok, width), BF16),
             pltpu.VMEM((blocks, 2 * tok, 2 * inner), BF16),
             pltpu.VMEM((blocks, 2 * tok, 2 * channels), F32),
             pltpu.VMEM((samples, blocks, 2, tok, 2 * inner), BF16),
@@ -570,8 +511,8 @@
         pooled_z,
         pooled_y,
         w_mix,
-        base,
-        extra,
+        w_big,
+        got_t,
         tokens_in,
         queries,
         d_normed,

time: 203 us -> 189 us (0.931)
  the two profiles are of different devices: /device:TPU:5 before, /device:TPU:29 now
where the time goes in v5:
time: 189 us; the launch traced here: 188 us
  starting transfers between devices  51.2 us (27%)
  Pallas kernels  46.3 us (24%)
  waiting for transfers between devices  37.6 us (20%)
  blocking collectives  29.9 us (16%)
  between operations  14.9 us (8%)
  other arithmetic  5.97 us (3%)
  local copies, waits for them, and re-layouts  2.17 us (1%)
    pallas_call x1, Pallas kernels, local(): pl.pallas_call(functools.partial(attend_kernel, heads, factor), out_shape...  33.8 us
    all_gather x1, blocking collectives, local(): lax.all_gather(pooled, 'rows', axis=0, tiled=False, axis_index_groups=z_s...  29.9 us
    ppermute x2, starting transfers between devices, local(): fetched.append(lax.ppermute(token_single, ('rows', 'samp'), perm))  20.1 us
    all_to_all x1, starting transfers between devices, local(): lax.all_to_all(both, 'samp', 0, 0, axis_index_groups=sets, tiled=True)  11.3 us
    ppermute x2, waiting for transfers between devices, local(): fetched.append(lax.ppermute(token_single, ('rows', 'samp'), perm))  10.7 us
    all_gather x1, waiting for transfers between devices, local(): got_t = lax.all_gather(t_own_pair, 'samp', axis=0, tiled=False)  9.9 us
    ppermute x1, waiting for transfers between devices, local(): proj_left = lax.ppermute(proj[:, margin:], 'rows', up)  8.91 us
    ppermute x1, waiting for transfers between devices, local(): lax.ppermute(pooled_z, 'rows', [(r, r ^ 1) for r in range(n_rows)])  5.49 us
  transfers between devices with their start and end apart: 11, of which 5 were waited for; matrix products, arithmetic and copies ran while one was open for 2% of the time, Pallas kernels for 6%

profile of v5, /device:TPU:29, one launch (start us, length us, event | category | flops | bytes accessed | tf_op | source)
XLA Modules:
  0.0 187.9 jit_solution(5444171731451967236)
XLA Ops:
  7.2 1.5 pack.1
  9.5 1.3 broadcast_subtract_fusion
  10.7 2.6 %pool.1 = (bf16[3,512,128]{2,1,0:T(8,128)(2,1)}, f32[7,64,128]{2,1,0:T(8,128)}, f32[7,32,128]{2,1,0:T(8,128)}, f32[7,32,128]{2,1,0:T(8,128)}) custom-call(s32[1]{0:T(128)S(6)} %copy.17.count, s32[1,512]{1,0:T(1,128)} %bitcast.20, bf16[3,512,128]{2,1,0:T(8,128)(2,1)} %noised, bf16[512,128]{1,0:T(8,128)(2,1)} %single.1, bf16[128,128]{1,0:T(8,128)(2,1)} %w_atom.1, ...), custom_call_target="tpu_custom_call" | custom-call | tf_op jit(solution)/shard_map/pool/pallas_call | solution.py:424
  13.4 4.2 %collective-permute-start.2 = (f32[7,32,128]{2,1,0:T(8,128)}, f32[7,32,128]{2,1,0:T(8,128)S(1)}, u32[]{:S(2)}, u32[]{:S(2)}) collective-permute-start(f32[7,32,128]{2,1,0:T(8,128)} %get-tuple-element.28), channel_id=1, source_target_pairs={{0,16},{16,32},{32,48},{48,64},{64,80},{80,96},{96,112},{112,128},... | collective-permute-start | bytes 344072 | tf_op jit(solution)/shard_map/ppermute | solution.py:440
  17.6 2.6 %collective-permute-start.3 = (f32[7,32,128]{2,1,0:T(8,128)}, f32[7,32,128]{2,1,0:T(8,128)S(1)}, u32[]{:S(2)}, u32[]{:S(2)}) collective-permute-start(f32[7,32,128]{2,1,0:T(8,128)} %get-tuple-element.29), channel_id=1, source_target_pairs={{16,0},{32,16},{48,32},{64,48},{80,64},{96,80},{112,96},{128,112},... | collective-permute-start | bytes 344072 | tf_op jit(solution)/shard_map/ppermute | solution.py:441
  20.2 10.2 %collective-permute-start = (bf16[64,768]{1,0:T(8,128)(2,1)}, bf16[64,768]{1,0:T(8,128)(2,1)S(1)}, u32[]{:S(2)}, u32[]{:S(2)}) collective-permute-start(bf16[64,768]{1,0:T(8,128)(2,1)} %t_own.1), channel_id=1, source_target_pairs={{0,0},{33,1},{66,2},{99,3},{132,4},{165,5},{198,6},{231,7},{264,8}... | collective-permute-start | bytes 294920 | tf_op jit(solution)/shard_map/ppermute | solution.py:420
  30.3 9.9 %collective-permute-start.1 = (bf16[64,768]{1,0:T(8,128)(2,1)}, bf16[64,768]{1,0:T(8,128)(2,1)S(1)}, u32[]{:S(2)}, u32[]{:S(2)}) collective-permute-start(bf16[64,768]{1,0:T(8,128)(2,1)} %t_own.1), channel_id=1, source_target_pairs={{16,0},{49,1},{82,2},{115,3},{148,4},{181,5},{214,6},{247,7},{280,... | collective-permute-start | bytes 294920 | tf_op jit(solution)/shard_map/ppermute | solution.py:420
  41.0 1.7 settle.1
  42.7 10.7 %collective-permute-done.1 = bf16[64,768]{1,0:T(8,128)(2,1)S(1)} collective-permute-done((bf16[64,768]{1,0:T(8,128)(2,1)}, bf16[64,768]{1,0:T(8,128)(2,1)S(1)}, u32[]{:S(2)}, u32[]{:S(2)}) %collective-permute-start.1) | collective-permute-done | bytes 98336 | tf_op jit(solution)/shard_map/ppermute | solution.py:420
  54.2 29.9 %all-gather = bf16[3072,128]{1,0:T(8,128)(2,1)S(1)} all-gather(bf16[192,128]{1,0:T(8,128)(2,1)} %get-tuple-element.34.pooled), channel_id=2, replica_groups={{0,32,64,96,128,160,192,224,256,288,320,352,384,416,448,480},{16,48,80,..., dimensions={0}, use_global_device_ids=true | all-gather | bytes 835584 | tf_op jit(solution)/shard_map/all_gather | solution.py:455
  84.1 3.7 %collective-permute-start.4 = (bf16[16,192,128]{2,1,0:T(8,128)(2,1)S(1)}, bf16[16,192,128]{2,1,0:T(8,128)(2,1)S(1)}, u32[]{:S(2)}, u32[]{:S(2)}) collective-permute-start(bf16[16,192,128]{2,1,0:T(8,128)(2,1)S(1)} %bitcast.11), channel_id=1, source_target_pairs={{0,16},{16,0},{32,48},{48,32},{64,80},{80,64},{96,112},{112,96},{1... | collective-permute-start | bytes 2359304 | tf_op jit(solution)/shard_map/ppermute | solution.py:456
  88.5 4.4 %prep.1 = (bf16[768,896]{1,0:T(8,128)(2,1)}, bf16[128,1024]{1,0:T(8,128)(2,1)}, f32[192,768]{1,0:T(8,128)}, bf16[192,384]{1,0:T(8,128)(2,1)}, f32[192,768]{1,0:T(8,128)}) custom-call(bf16[16,128,768]{2,1,0:T(8,128)(2,1)} %bitcast.13, bf16[192,128]{1,0:T(8,128)(2,1)} %get-tuple-element.34.pooled, bf16[192,128]{1,0:T(8,128)(2,1)} %get-tuple-element.38.d_token, ...), custom_call_target="tpu_custom_call" | custom-call | flops 2000000000 | bytes 8000000 | tf_op jit(solution)/shard_map/prep/pallas_call | solution.py:461
  92.9 5.5 %collective-permute-done.4.pooled_y = bf16[16,192,128]{2,1,0:T(8,128)(2,1)S(1)} collective-permute-done((bf16[16,192,128]{2,1,0:T(8,128)(2,1)S(1)}, bf16[16,192,128]{2,1,0:T(8,128)(2,1)S(1)}, u32[]{:S(2)}, u32[]{:S(2)}) %collective-permute-start.4) | collective-permute-done | bytes 786464 | tf_op jit(solution)/shard_map/ppermute | solution.py:456
  98.4 9.9 %all-gather.6.cloned.1.call-done = bf16[2048,768]{1,0:T(8,128)(2,1)} async-done(((bf16[128,768]{1,0:T(8,128)(2,1)}), bf16[2048,768]{1,0:T(8,128)(2,1)}) %all-gather.6.cloned.1.call-update) | async-done | bytes 3145744 | tf_op jit(solution)/shard_map/all_gather | solution.py:453
  108.3 33.8 %attend.1 = (bf16[192,128]{1,0:T(8,128)(2,1)}, bf16[8,512,128]{2,1,0:T(8,128)(2,1)}, bf16[8,512,128]{2,1,0:T(8,128)(2,1)}) custom-call(s32[3]{0:T(128)} %pad_add_fusion.place, bf16[16,192,128]{2,1,0:T(8,128)(2,1)} %bitcast.12, bf16[16,192,128]{2,1,0:T(8,128)(2,1)} %copy-done.1, bf16[128,1024]{1,0:T(8,128)(2,1)} %get-tuple-element.39.w_mix, ...), custom_call_target="tpu_custom_call" | custom-call | tf_op jit(solution)/shard_map/attend/pallas_call | solution.py:479
  142.1 2.5 %collective-permute-start.7 = (bf16[8,512,128]{2,1,0:T(8,128)(2,1)}, bf16[8,512,128]{2,1,0:T(8,128)(2,1)S(1)}, u32[]{:S(2)}, u32[]{:S(2)}) collective-permute-start(bf16[8,512,128]{2,1,0:T(8,128)(2,1)} %get-tuple-element.47), channel_id=1, source_target_pairs={{0,1},{1,0},{2,3},{3,2},{4,5},{5,4},{6,7},{7,6},{8,9},{9,8},{10,11... | collective-permute-start | bytes 3145736 | tf_op jit(solution)/shard_map/ppermute | solution.py:523
  144.6 2.5 %collective-permute-done.7 = bf16[8,512,128]{2,1,0:T(8,128)(2,1)S(1)} collective-permute-done((bf16[8,512,128]{2,1,0:T(8,128)(2,1)}, bf16[8,512,128]{2,1,0:T(8,128)(2,1)S(1)}, u32[]{:S(2)}, u32[]{:S(2)}) %collective-permute-start.7) | collective-permute-done | bytes 1048608 | tf_op jit(solution)/shard_map/ppermute | solution.py:523
  147.1 2.5 %add_convert_fusion = bf16[8,512,128]{2,1,0:T(8,128)(2,1)} fusion(bf16[8,512,128]{2,1,0:T(8,128)(2,1)S(1)} %collective-permute-done.7, bf16[8,512,128]{2,1,0:T(8,128)(2,1)} %get-tuple-element.46), kind=kLoop, calls=%fused_computation.1 | loop fusion | flops 2097152 | bytes 3145728 | tf_op jit(solution)/shard_map/convert_element_type | solution.py:524
  149.6 11.3 %all-to-all-start = ((bf16[8,512,128]{2,1,0:T(8,128)(2,1)}), bf16[8,512,128]{2,1,0:T(8,128)(2,1)S(1)}, u32[]{:S(2)}, u32[]{:S(2)}) async-start(bf16[8,512,128]{2,1,0:T(8,128)(2,1)} %add_convert_fusion), calls=%async_computation | async-start | bytes 2097152 | tf_op jit(solution)/shard_map/all_to_all | solution.py:525
  160.9 3.9 %collective-permute-start.5 = (bf16[3,32,128]{2,1,0:T(8,128)(2,1)S(1)}, bf16[3,32,128]{2,1,0:T(8,128)(2,1)S(1)}, u32[]{:S(2)}, u32[]{:S(2)}) collective-permute-start(bf16[3,32,128]{2,1,0:T(8,128)(2,1)S(1)} %get-tuple-element.49), channel_id=1, source_target_pairs={{0,16},{16,32},{32,48},{48,64},{64,80},{80,96},{96,112},{112,128},... | collective-permute-start | bytes 73736 | tf_op jit(solution)/shard_map/ppermute | solution.py:529
  164.8 2.9 %collective-permute-start.6 = (bf16[3,32,128]{2,1,0:T(8,128)(2,1)S(1)}, bf16[3,32,128]{2,1,0:T(8,128)(2,1)S(1)}, u32[]{:S(2)}, u32[]{:S(2)}) collective-permute-start(bf16[3,32,128]{2,1,0:T(8,128)(2,1)S(1)} %get-tuple-element.48), channel_id=1, source_target_pairs={{16,0},{32,16},{48,32},{64,48},{80,64},{96,80},{112,96},{128,112},... | collective-permute-start | bytes 73736 | tf_op jit(solution)/shard_map/ppermute | solution.py:530
  167.7 0.9 copy.16.token
  168.5 8.9 %collective-permute-done.5.from_left = bf16[3,32,128]{2,1,0:T(8,128)(2,1)S(1)} collective-permute-done((bf16[3,32,128]{2,1,0:T(8,128)(2,1)S(1)}, bf16[3,32,128]{2,1,0:T(8,128)(2,1)S(1)}, u32[]{:S(2)}, u32[]{:S(2)}) %collective-permute-start.5) | collective-permute-done | bytes 24608 | tf_op jit(solution)/shard_map/ppermute | solution.py:529
  178.1 2.2 %decode.1 = bf16[3,512,128]{2,1,0:T(8,128)(2,1)} custom-call(s32[1]{0:T(128)S(6)} %copy.17.count, s32[512,1]{1,0:T(8,128)} %copy.16.token, bf16[3,512,128]{2,1,0:T(8,128)(2,1)} %get-tuple-element.26.hidden, bf16[3,64,128]{2,1,0:T(8,128)(2,1)} %bitcast.18, bf16[3,32,128]{2,1,0:T(8,128)(2,1)} %copy-done.5, bf16[3,32,128]{2,1,0:T(8,128)(2,1)} %copy-done.6), custom_call_target="tpu_custom_call" | custom-call | tf_op jit(solution)/shard_map/decode/pallas_call | solution.py:531
  (30 shorter events, 3.6 us)
Async XLA Ops:
  7.2 81.3 %all-gather.8.cloned.1.call-start = ((), (), s32[]{:S(2)}) async-start(), calls=%async_computation.2 | async-start | bytes 3342336 | tf_op jit(solution)/shard_map/all_gather | solution.py:411
  8.8 99.5 %all-gather.6.cloned.1.call-start = ((), (), s32[]{:S(2)}) async-start(), calls=%async_computation.1 | async-start | bytes 3342336 | tf_op jit(solution)/shard_map/all_gather | solution.py:453
  13.4 26.9 %collective-permute-start.2 = (f32[7,32,128]{2,1,0:T(8,128)}, f32[7,32,128]{2,1,0:T(8,128)S(1)}, u32[]{:S(2)}, u32[]{:S(2)}) collective-permute-start(f32[7,32,128]{2,1,0:T(8,128)} %get-tuple-element.28), channel_id=1, source_target_pairs={{0,16},{16,32},{32,48},{48,64},{64,80},{80,96},{96,112},{112,128},... | collective-permute-start | bytes 344072 | tf_op jit(solution)/shard_map/ppermute | solution.py:440
  17.6 22.7 %collective-permute-start.3 = (f32[7,32,128]{2,1,0:T(8,128)}, f32[7,32,128]{2,1,0:T(8,128)S(1)}, u32[]{:S(2)}, u32[]{:S(2)}) collective-permute-start(f32[7,32,128]{2,1,0:T(8,128)} %get-tuple-element.29), channel_id=1, source_target_pairs={{16,0},{32,16},{48,32},{64,48},{80,64},{96,80},{112,96},{128,112},... | collective-permute-start | bytes 344072 | tf_op jit(solution)/shard_map/ppermute | solution.py:441
  20.2 22.6 %collective-permute-start = (bf16[64,768]{1,0:T(8,128)(2,1)}, bf16[64,768]{1,0:T(8,128)(2,1)S(1)}, u32[]{:S(2)}, u32[]{:S(2)}) collective-permute-start(bf16[64,768]{1,0:T(8,128)(2,1)} %t_own.1), channel_id=1, source_target_pairs={{0,0},{33,1},{66,2},{99,3},{132,4},{165,5},{198,6},{231,7},{264,8}... | collective-permute-start | bytes 294920 | tf_op jit(solution)/shard_map/ppermute | solution.py:420
  30.3 23.1 %collective-permute-start.1 = (bf16[64,768]{1,0:T(8,128)(2,1)}, bf16[64,768]{1,0:T(8,128)(2,1)S(1)}, u32[]{:S(2)}, u32[]{:S(2)}) collective-permute-start(bf16[64,768]{1,0:T(8,128)(2,1)} %t_own.1), channel_id=1, source_target_pairs={{16,0},{49,1},{82,2},{115,3},{148,4},{181,5},{214,6},{247,7},{280,... | collective-permute-start | bytes 294920 | tf_op jit(solution)/shard_map/ppermute | solution.py:420
  40.3 0.6 copy-start.3
  40.3 0.7 copy-start.4
  84.1 8.7 %copy-start = (bf16[3072,128]{1,0:T(8,128)(2,1)}, bf16[3072,128]{1,0:T(8,128)(2,1)S(1)}, u32[]{:S(2)}) copy-start(bf16[3072,128]{1,0:T(8,128)(2,1)S(1)} %all-gather) | copy-start | bytes 2359300
  84.1 14.2 %collective-permute-start.4 = (bf16[16,192,128]{2,1,0:T(8,128)(2,1)S(1)}, bf16[16,192,128]{2,1,0:T(8,128)(2,1)S(1)}, u32[]{:S(2)}, u32[]{:S(2)}) collective-permute-start(bf16[16,192,128]{2,1,0:T(8,128)(2,1)S(1)} %bitcast.11), channel_id=1, source_target_pairs={{0,16},{16,0},{32,48},{48,32},{64,80},{80,64},{96,112},{112,96},{1... | collective-permute-start | bytes 2359304 | tf_op jit(solution)/shard_map/ppermute | solution.py:456
  98.4 9.9 %copy-start.1 = (bf16[16,192,128]{2,1,0:T(8,128)(2,1)}, bf16[16,192,128]{2,1,0:T(8,128)(2,1)S(1)}, u32[]{:S(2)}) copy-start(bf16[16,192,128]{2,1,0:T(8,128)(2,1)S(1)} %collective-permute-done.4.pooled_y) | copy-start | bytes 2359300
  142.1 4.9 %collective-permute-start.7 = (bf16[8,512,128]{2,1,0:T(8,128)(2,1)}, bf16[8,512,128]{2,1,0:T(8,128)(2,1)S(1)}, u32[]{:S(2)}, u32[]{:S(2)}) collective-permute-start(bf16[8,512,128]{2,1,0:T(8,128)(2,1)} %get-tuple-element.47), channel_id=1, source_target_pairs={{0,1},{1,0},{2,3},{3,2},{4,5},{5,4},{6,7},{7,6},{8,9},{9,8},{10,11... | collective-permute-start | bytes 3145736 | tf_op jit(solution)/shard_map/ppermute | solution.py:523
  147.1 13.8 %copy-start.2 = (bf16[192,128]{1,0:T(8,128)(2,1)S(1)}, bf16[192,128]{1,0:T(8,128)(2,1)}, u32[]{:S(2)}) copy-start(bf16[192,128]{1,0:T(8,128)(2,1)} %get-tuple-element.45) | copy-start | bytes 147460
  147.1 20.6 %copy-start.7 = (s32[512]{0:T(512)S(1)}, s32[512]{0:T(512)}, u32[]{:S(2)}) copy-start(s32[512]{0:T(512)} %broadcast_subtract_fusion) | copy-start | bytes 6148
  149.6 30.7 %all-to-all-start = ((bf16[8,512,128]{2,1,0:T(8,128)(2,1)}), bf16[8,512,128]{2,1,0:T(8,128)(2,1)S(1)}, u32[]{:S(2)}, u32[]{:S(2)}) async-start(bf16[8,512,128]{2,1,0:T(8,128)(2,1)} %add_convert_fusion), calls=%async_computation | async-start | bytes 2097152 | tf_op jit(solution)/shard_map/all_to_all | solution.py:525
  160.9 16.6 %collective-permute-start.5 = (bf16[3,32,128]{2,1,0:T(8,128)(2,1)S(1)}, bf16[3,32,128]{2,1,0:T(8,128)(2,1)S(1)}, u32[]{:S(2)}, u32[]{:S(2)}) collective-permute-start(bf16[3,32,128]{2,1,0:T(8,128)(2,1)S(1)} %get-tuple-element.49), channel_id=1, source_target_pairs={{0,16},{16,32},{32,48},{48,64},{64,80},{80,96},{96,112},{112,128},... | collective-permute-start | bytes 73736 | tf_op jit(solution)/shard_map/ppermute | solution.py:529
  164.8 12.7 %collective-permute-start.6 = (bf16[3,32,128]{2,1,0:T(8,128)(2,1)S(1)}, bf16[3,32,128]{2,1,0:T(8,128)(2,1)S(1)}, u32[]{:S(2)}, u32[]{:S(2)}) collective-permute-start(bf16[3,32,128]{2,1,0:T(8,128)(2,1)S(1)} %get-tuple-element.48), channel_id=1, source_target_pairs={{16,0},{32,16},{48,32},{64,48},{80,64},{96,80},{112,96},{128,112},... | collective-permute-start | bytes 73736 | tf_op jit(solution)/shard_map/ppermute | solution.py:530
  177.5 0.6 copy-start.5
  177.5 0.6 copy-start.6
Sparse Core Ops, SparseCore 0:
  10.7 47.5 all-gather.7
  60.5 47.7 all-gather.5

commit v6 on v5

--- a/solution.py
+++ b/solution.py
@@ -79,41 +79,46 @@
         d_token[s * middle : (s + 1) * middle] = settled(samples + 1 + s).astype(BF16)
 
 
-def select(rows, cols, size, padded, offset):
-    line = lax.broadcasted_iota(jnp.int32, (rows, cols), 0)
-    column = lax.broadcasted_iota(jnp.int32, (rows, cols), 1)
-    group = line // size
-    return jnp.where(column == group * padded + offset + (line - group * size), 1.0, 0.0).astype(BF16)
-
-
 def pack_kernel(w_query, w_key, w_value, w_down, w_out, w_up, out):
     cut, inner = w_query.shape
-    width = out.shape[1]
-    end = inner + w_down.shape[1]
+    channels = w_down.shape[1]
     out[:cut, :inner] = w_query[...]
     out[:cut, inner:] = w_key[...]
-    out[cut : 2 * cut, :inner] = w_value[...]
-    out[cut : 2 * cut, inner:end] = w_down[...]
-    out[cut : 2 * cut, end:] = jnp.zeros((cut, width - end), BF16)
-    both = jnp.concatenate([w_out[...].astype(F32), w_up[...].astype(F32)], axis=0)
-    out[2 * cut :] = both.astype(BF16)
-
-
-def prep_kernel(head_dim, weights, pooled, d_token, t_own, w_big, w_mix, tokens_in, queries, d_normed):
-    members, height, width = weights.shape
+    value = w_value[...].astype(F32)
+    down = w_down[...].astype(F32)
+    piece = cut * channels // out.shape[1]
+    rest = [
+        jnp.concatenate([value[: cut // 2], value[cut // 2 :]], axis=1),
+        w_out[...].astype(F32),
+        jnp.concatenate([down[i : i + piece] for i in range(0, cut, piece)], axis=1),
+        w_up[...].astype(F32),
+    ]
+    out[cut:] = jnp.concatenate(rest, axis=0).astype(BF16)
+
+
+def prep_kernel(
+    head_dim, got, pooled, d_token, t_own, w_big, w_mix, tokens_in, queries, d_normed, w_out, w_down
+):
+    members, height, width = got.shape
     tok = t_own.shape[0]
     channels = pooled.shape[1]
     samples = pooled.shape[0] // tok
     inner = queries.shape[1]
     cut = width // members
-    tail = height - 2 * cut
-    up_rows = channels // members
-
-    rest = weights[:, 2 * cut :, :].reshape(members * tail, width)
-    up_raw = dot(select(channels, members * tail, up_rows, tail, tail - up_rows), rest)
-    up = (up_raw - jnp.mean(up_raw, axis=-1, keepdims=True)).astype(BF16)
-    w_big[:, :inner] = weights[:, :cut, inner:].reshape(width, inner)
-    w_big[:, inner : 2 * inner] = weights[:, cut : 2 * cut, :inner].reshape(width, inner)
+    half = cut // 2
+    out_rows = inner // members
+    piece = cut * channels // width
+
+    rest = got[:, cut:, :].astype(F32)
+    value = jnp.concatenate([rest[:, :half, :inner], rest[:, :half, inner:]], axis=1).reshape(width, inner)
+    at = half + out_rows
+    w_out[...] = rest[:, half:at].reshape(inner, width).astype(BF16)
+    down = [rest[:, at : at + piece, i : i + channels] for i in range(0, width, channels)]
+    w_down[...] = jnp.concatenate(down, axis=1).reshape(width, channels).astype(BF16)
+    up_exact = rest[:, at + piece :].reshape(channels, width)
+    up = (up_exact - jnp.mean(up_exact, axis=-1, keepdims=True)).astype(BF16)
+    w_big[:, :inner] = got[:, :cut, inner:].reshape(width, inner)
+    w_big[:, inner : 2 * inner] = value.astype(BF16)
     w_big[:, 2 * inner :] = up.astype(F32).T.astype(BF16)
     mix = dot(up, w_big[...])
     w_mix[:, : 2 * inner] = mix[:, : 2 * inner].astype(BF16)
@@ -122,34 +127,14 @@
     w_mix[:, 2 * inner : 2 * inner + channels] = high
     w_mix[:, 2 * inner + channels :] = (gram - high.astype(F32)).astype(BF16)
 
-    w_query = weights[:, :cut, :inner].reshape(width, inner)
-    w_down = weights[:, cut : 2 * cut, inner : inner + channels].reshape(width, channels)
+    w_query = got[:, :cut, :inner].reshape(width, inner)
     t_f = t_own[...].astype(F32)
-    up_exact = up_raw.astype(BF16)
     for s in range(samples):
         own_rows = slice(s * tok, (s + 1) * tok)
-        tokens_in[own_rows] = dot(pooled[own_rows], up_exact) + t_f
+        tokens_in[own_rows] = dot(pooled[own_rows], up_exact.astype(BF16)) + t_f
     normed, _ = normalize(tokens_in[...])
     queries[...] = (dot(normed.astype(BF16), w_query) * (head_dim**-0.5)).astype(BF16)
-    d_normed[...] = dot_nt(d_token[...], w_down)
-
-
-def key_value(tables, bases, extras, w_mix):
-    lines, channels = tables[0].shape
-    tok, deep = bases[0].shape
-    repeat = lines // tok
-    y_all = dot(jnp.concatenate(tables, axis=0), w_mix)
-    results = []
-    for i, (p, base, extra) in enumerate(zip(tables, bases, extras)):
-        y = y_all[i * lines : (i + 1) * lines]
-        gram = y[:, deep : deep + channels] + y[:, deep + channels :]
-        cross = jnp.concatenate([extra[:, :channels]] * repeat, axis=0)
-        square = jnp.concatenate([extra[:, channels : channels + 1]] * repeat, axis=0)
-        variance = jnp.sum(p.astype(F32) * (gram + cross), axis=-1, keepdims=True) + square
-        inverse = lax.rsqrt(jnp.maximum(variance, 0.0) + EPSILON)
-        tiled = jnp.concatenate([base.astype(F32)] * repeat, axis=0)
-        results.append(((y[:, :deep] + tiled) * inverse).astype(BF16))
-    return results
+    d_normed[...] = dot_nt(d_token[...], w_down[...])
 
 
 def attend_kernel(
@@ -164,7 +149,8 @@
     tokens_hbm,
     queries,
     d_normed_hbm,
-    got,
+    w_out_hbm,
+    w_down_hbm,
     bias_hbm,
     proj,
     keep,
@@ -177,7 +163,7 @@
     bias,
     tokens_in,
     d_normed,
-    w_rest,
+    w_out,
     w_down,
     scores,
     probs,
@@ -189,7 +175,7 @@
 ):
     blocks, lines, channels = pooled_y.shape
     samples, _, _, tok, deep = kv.shape
-    members, height, width = got.shape
+    width = tokens_in.shape[1]
     total = 2 * blocks * tok
     inner = deep // 2
     head_dim = inner // heads
@@ -200,8 +186,6 @@
     first_z = place[0]
     high = place[1]
     core = place[2]
-    tail = w_rest.shape[1]
-    cut = w_down.shape[1]
     pieces_in = min(4, blocks // 2)
     run = blocks // pieces_in
 
@@ -215,14 +199,12 @@
     for piece in range(pieces_in):
         part = pl.ds(piece * run, run)
         copies.append(copy(got_t.at[part], t_all.at[part], piece))
-    down_rows = slice(height - tail - cut, height - tail)
-    down_lanes = slice(inner, inner + channels)
     late = [
         copy(bias_hbm, bias, 7),
         copy(tokens_hbm, tokens_in, 9),
         copy(d_normed_hbm, d_normed, 10),
-        copy(got.at[:, height - tail :], w_rest, 11),
-        copy(got.at[:, down_rows, down_lanes], w_down, 12),
+        copy(w_out_hbm, w_out, 11),
+        copy(w_down_hbm, w_down, 12),
     ]
 
     big_copy.wait()
@@ -242,15 +224,28 @@
     def step(b, carry):
         near = lax.rem(first_z + b, blocks)
         far = lax.rem(near + high, blocks)
-        results = key_value(
-            [pooled_z[near], pooled_y[far]],
-            [base[b, :tok], base[b, tok:]],
-            [extra[b, :tok], extra[b, tok:]],
-            w_mix[...],
-        )
-        for s in range(samples):
-            kv[s, near, high] = results[0][s * tok : (s + 1) * tok]
-            kv[s, far, 1 - high] = results[1][s * tok : (s + 1) * tok]
+        p = jnp.concatenate([pooled_z[near], pooled_y[far]], axis=0)
+        pf = p.astype(F32)
+        gram = dot(p, w_mix[:, deep:])
+        inverse = []
+        for part in range(2):
+            own = slice(part * tok, (part + 1) * tok)
+            cross = extra[b, own, :channels]
+            square = extra[b, own, channels:]
+            for s in range(samples):
+                lane = slice(part * lines + s * tok, part * lines + (s + 1) * tok)
+                form = pf[lane] * (gram[lane, :channels] + gram[lane, channels:] + cross)
+                variance = jnp.sum(form, axis=-1, keepdims=True) + square[:, :1]
+                inverse.append(lax.rsqrt(jnp.maximum(variance, 0.0) + EPSILON))
+        for c in range(0, deep, span):
+            y = dot(p, w_mix[:, c : c + span])
+            for part, (z, y_half) in enumerate(((near, high), (far, 1 - high))):
+                shared = base[b, part * tok : (part + 1) * tok, c : c + span].astype(F32)
+                for s in range(samples):
+                    lane = slice(part * lines + s * tok, part * lines + (s + 1) * tok)
+                    kv[s, z, y_half, :, c : c + span] = (
+                        (y[lane] + shared) * inverse[part * samples + s]
+                    ).astype(BF16)
         return carry
 
     lax.fori_loop(0, blocks, step, 0)
@@ -313,18 +308,13 @@
 
     lax.fori_loop(0, samples, forward, 0)
 
-    rest = w_rest[...].reshape(members * tail, width)
-    down = w_down[...].reshape(width, channels)
-    pick = select(inner, members * tail, inner // members, tail, 0)
-    mixed_wide = dot(mixed[...], pick).astype(BF16)
-    normed_out, inverse_out = normalize(tokens_in[...] + dot(mixed_wide, rest))
-    proj[...] = dot(normed_out.astype(BF16), down).astype(BF16)
+    normed_out, inverse_out = normalize(tokens_in[...] + dot(mixed[...], w_out[...]))
+    proj[...] = dot(normed_out.astype(BF16), w_down[...]).astype(BF16)
     d_norm = d_normed[...]
     first = jnp.mean(d_norm, axis=-1, keepdims=True)
     second = jnp.mean(d_norm * normed_out, axis=-1, keepdims=True)
     d_tokens = inverse_out * (d_norm - first - normed_out * second)
-    d_mixed_wide = dot_nt(d_tokens.astype(BF16), rest).astype(BF16)
-    d_mixed[...] = dot_nt(d_mixed_wide, pick).astype(BF16)
+    d_mixed[...] = dot_nt(d_tokens.astype(BF16), w_out[...]).astype(BF16)
 
     for g in range(2):
         value_lanes = slice(inner + starts[g], inner + starts[g] + span)
@@ -398,10 +388,10 @@
     swap = [(s, s ^ 1) for s in range(n_samp)]
 
     shape = jax.ShapeDtypeStruct
-    tail = w_out.shape[0] + w_up.shape[0]
+    packed = sum(w.size for w in (w_query, w_key, w_value, w_down, w_out, w_up))
     w_own = pl.pallas_call(
         pack_kernel,
-        out_shape=shape((2 * w_query.shape[0] + tail, width), BF16),
+        out_shape=shape((packed // width, width), BF16),
         in_specs=[WHOLE] * 6,
         out_specs=WHOLE,
         compiler_params=params(),
@@ -458,7 +448,7 @@
     got_t, pooled_y = lax.optimization_barrier((got_t, pooled_y))
 
     place = jnp.stack([rank // 2, rank % 2, group % 2]).astype(jnp.int32)
-    w_big, w_mix, tokens_in, queries, d_normed = pl.pallas_call(
+    w_big, w_mix, tokens_in, queries, d_normed, w_out_all, w_down_all = pl.pallas_call(
         functools.partial(prep_kernel, inner // heads),
         out_shape=(
             shape((width, 2 * inner + channels), BF16),
@@ -466,9 +456,11 @@
             shape((samples * tok, width), F32),
             shape((samples * tok, inner), BF16),
             shape((samples * tok, width), F32),
+            shape((inner, width), BF16),
+            shape((width, channels), BF16),
         ),
         in_specs=[WHOLE] * 4,
-        out_specs=(WHOLE,) * 5,
+        out_specs=(WHOLE,) * 7,
         compiler_params=params(),
         cost_estimate=pl.CostEstimate(flops=2 * 10**9, bytes_accessed=8 * 10**6, transcendentals=0),
         name="prep",
@@ -483,7 +475,7 @@
             shape((chips, heads * tok, 128), BF16),
             shape((chips, heads * tok, 128), BF16),
         ),
-        in_specs=[SCALAR, WHOLE, WHOLE, WHOLE, ANY, ANY, ANY, WHOLE, ANY, ANY, ANY],
+        in_specs=[SCALAR, WHOLE, WHOLE, WHOLE, ANY, ANY, ANY, WHOLE, ANY, ANY, ANY, ANY],
         out_specs=(WHOLE,) * 3,
         scratch_shapes=[
             pltpu.VMEM((width, 2 * inner + channels), BF16),
@@ -494,8 +486,8 @@
             pltpu.VMEM((heads * tok, total), BF16),
             pltpu.VMEM((samples * tok, width), F32),
             pltpu.VMEM((samples * tok, width), F32),
-            pltpu.VMEM((n_samp, tail, width), BF16),
-            pltpu.VMEM((n_samp, w_down.shape[0], channels), BF16),
+            pltpu.VMEM((inner, width), BF16),
+            pltpu.VMEM((width, channels), BF16),
             pltpu.VMEM((2, rows, total), F32),
             pltpu.VMEM((samples, 2, rows, total), BF16),
             pltpu.VMEM((samples, 2, rows, 256), F32),
@@ -516,18 +508,20 @@
         tokens_in,
         queries,
         d_normed,
-        got,
+        w_out_all,
+        w_down_all,
         pair_bias.reshape(heads * tok, total),
     )
 
     other = lax.ppermute(send, "samp", swap)
+    proj = proj.reshape(samples, tok, channels)
+    proj_left = lax.ppermute(proj[:, margin:], "rows", up)
+    proj_right = lax.ppermute(proj[:, :margin], "rows", down)
+    other, proj_left, proj_right = lax.optimization_barrier((other, proj_left, proj_right))
     both = (keep.astype(F32) + other.astype(F32)).astype(BF16)
     shares = lax.all_to_all(both, "samp", 0, 0, axis_index_groups=sets, tiled=True)
     bias_grad = jnp.sum(shares.astype(F32), axis=0).reshape(heads, tok, 128)
 
-    proj = proj.reshape(samples, tok, channels)
-    proj_left = lax.ppermute(proj[:, margin:], "rows", up)
-    proj_right = lax.ppermute(proj[:, :margin], "rows", down)
     atom_out = pl.pallas_call(
         decode_kernel,
         out_shape=shape((samples, atoms, channels), BF16),

time: 189 us -> 192 us (1.016)
  the two profiles are of different devices: /device:TPU:29 before, /device:TPU:112 now
where the time goes in v6:
time: 192 us
  waiting for transfers between devices  53.8 us (28%)
  Pallas kernels  45 us (23%)
  blocking collectives  35.6 us (19%)
  starting transfers between devices  34.1 us (18%)
  between operations  14.8 us (8%)
  other arithmetic  5.97 us (3%)
  local copies, waits for them, and re-layouts  2.29 us (1%)
    all_gather x1, blocking collectives, local(): lax.all_gather(pooled, 'rows', axis=0, tiled=False, axis_index_groups=z_s...  35.6 us
    pallas_call x1, Pallas kernels, local(): pl.pallas_call(functools.partial(attend_kernel, heads, factor), out_shape...  32.2 us
    ppermute x1, waiting for transfers between devices, local(): lax.ppermute(pooled_z, 'rows', [(r, r ^ 1) for r in range(n_rows)])  17.4 us
    all_to_all x1, waiting for transfers between devices, local(): lax.all_to_all(both, 'samp', 0, 0, axis_index_groups=sets, tiled=True)  11.8 us
    all_gather x1, waiting for transfers between devices, local(): got_t = lax.all_gather(t_own_pair, 'samp', axis=0, tiled=False)  11.7 us
    all_to_all x1, starting transfers between devices, local(): lax.all_to_all(both, 'samp', 0, 0, axis_index_groups=sets, tiled=True)  8.49 us
    ppermute x1, waiting for transfers between devices, local(): proj_right = lax.ppermute(proj[:, :margin], 'rows', down)  7.39 us
    ppermute x1, starting transfers between devices, local(): proj_left = lax.ppermute(proj[:, margin:], 'rows', up)  6.04 us
  transfers between devices with their start and end apart: 11, of which 6 were waited for; matrix products, arithmetic and copies ran while one was open for 2% of the time, Pallas kernels for 6%

profile of v6, /device:TPU:112, one launch (start us, length us, event | category | flops | bytes accessed | tf_op | source)
XLA Modules:
  0.0 191.6 jit_solution(1937047335576779485)
XLA Ops:
  7.2 1.5 pack.1
  9.5 1.3 broadcast_subtract_fusion
  10.7 2.6 %pool.1 = (bf16[3,512,128]{2,1,0:T(8,128)(2,1)}, f32[7,64,128]{2,1,0:T(8,128)}, f32[7,32,128]{2,1,0:T(8,128)}, f32[7,32,128]{2,1,0:T(8,128)}) custom-call(s32[1]{0:T(128)S(6)} %copy.17.count, s32[1,512]{1,0:T(1,128)} %bitcast.18, bf16[3,512,128]{2,1,0:T(8,128)(2,1)} %noised, bf16[512,128]{1,0:T(8,128)(2,1)} %single.1, bf16[128,128]{1,0:T(8,128)(2,1)} %w_atom.1, ...), custom_call_target="tpu_custom_call" | custom-call | tf_op jit(solution)/shard_map/pool/pallas_call | solution.py:414
  13.4 4.8 %collective-permute-start.2 = (f32[7,32,128]{2,1,0:T(8,128)}, f32[7,32,128]{2,1,0:T(8,128)S(1)}, u32[]{:S(2)}, u32[]{:S(2)}) collective-permute-start(f32[7,32,128]{2,1,0:T(8,128)} %get-tuple-element.33), channel_id=1, source_target_pairs={{0,16},{16,32},{32,48},{48,64},{64,80},{80,96},{96,112},{112,128},... | collective-permute-start | bytes 344072 | tf_op jit(solution)/shard_map/ppermute | solution.py:430
  18.2 2.5 %collective-permute-start.3 = (f32[7,32,128]{2,1,0:T(8,128)}, f32[7,32,128]{2,1,0:T(8,128)S(1)}, u32[]{:S(2)}, u32[]{:S(2)}) collective-permute-start(f32[7,32,128]{2,1,0:T(8,128)} %get-tuple-element.34), channel_id=1, source_target_pairs={{16,0},{32,16},{48,32},{64,48},{80,64},{96,80},{112,96},{128,112},... | collective-permute-start | bytes 344072 | tf_op jit(solution)/shard_map/ppermute | solution.py:431
  20.7 1.6 collective-permute-start
  22.3 3.1 %collective-permute-start.1 = (bf16[64,768]{1,0:T(8,128)(2,1)}, bf16[64,768]{1,0:T(8,128)(2,1)S(1)}, u32[]{:S(2)}, u32[]{:S(2)}) collective-permute-start(bf16[64,768]{1,0:T(8,128)(2,1)} %t_own.1), channel_id=1, source_target_pairs={{16,0},{49,1},{82,2},{115,3},{148,4},{181,5},{214,6},{247,7},{280,... | collective-permute-start | bytes 294920 | tf_op jit(solution)/shard_map/ppermute | solution.py:410
  25.4 4.0 %collective-permute-done.3.from_right = f32[7,32,128]{2,1,0:T(8,128)S(1)} collective-permute-done((f32[7,32,128]{2,1,0:T(8,128)}, f32[7,32,128]{2,1,0:T(8,128)S(1)}, u32[]{:S(2)}, u32[]{:S(2)}) %collective-permute-start.3) | collective-permute-done | bytes 114720 | tf_op jit(solution)/shard_map/ppermute | solution.py:431
  30.1 1.8 settle.1
  32.0 1.4 collective-permute-done.1
  34.1 35.6 %all-gather = bf16[3072,128]{1,0:T(8,128)(2,1)S(1)} all-gather(bf16[192,128]{1,0:T(8,128)(2,1)} %get-tuple-element.39.pooled), channel_id=2, replica_groups={{0,32,64,96,128,160,192,224,256,288,320,352,384,416,448,480},{16,48,80,..., dimensions={0}, use_global_device_ids=true | all-gather | bytes 835584 | tf_op jit(solution)/shard_map/all_gather | solution.py:445
  69.7 3.4 %collective-permute-start.4 = (bf16[16,192,128]{2,1,0:T(8,128)(2,1)S(1)}, bf16[16,192,128]{2,1,0:T(8,128)(2,1)S(1)}, u32[]{:S(2)}, u32[]{:S(2)}) collective-permute-start(bf16[16,192,128]{2,1,0:T(8,128)(2,1)S(1)} %bitcast.12), channel_id=1, source_target_pairs={{0,16},{16,0},{32,48},{48,32},{64,80},{80,64},{96,112},{112,96},{1... | collective-permute-start | bytes 2359304 | tf_op jit(solution)/shard_map/ppermute | solution.py:446
  73.8 4.6 %prep.1 = (bf16[768,896]{1,0:T(8,128)(2,1)}, bf16[128,1024]{1,0:T(8,128)(2,1)}, f32[192,768]{1,0:T(8,128)}, bf16[192,384]{1,0:T(8,128)(2,1)}, f32[192,768]{1,0:T...) custom-call(bf16[16,112,768]{2,1,0:T(8,128)(2,1)} %bitcast.20, bf16[192,128]{1,0:T(8,128)(2,1)} %get-tuple-element.39.pooled, ...), custom_call_target="tpu_custom_call" | custom-call | flops 2000000000 | bytes 8000000 | tf_op jit(solution)/shard_map/prep/pallas_call | solution.py:451
  78.3 17.4 %collective-permute-done.4.pooled_y = bf16[16,192,128]{2,1,0:T(8,128)(2,1)S(1)} collective-permute-done((bf16[16,192,128]{2,1,0:T(8,128)(2,1)S(1)}, bf16[16,192,128]{2,1,0:T(8,128)(2,1)S(1)}, u32[]{:S(2)}, u32[]{:S(2)}) %collective-permute-start.4) | collective-permute-done | bytes 786464 | tf_op jit(solution)/shard_map/ppermute | solution.py:446
  95.8 11.7 %all-gather.6.cloned.1.call-done = bf16[2048,768]{1,0:T(8,128)(2,1)} async-done(((bf16[128,768]{1,0:T(8,128)(2,1)}), bf16[2048,768]{1,0:T(8,128)(2,1)}) %all-gather.6.cloned.1.call-update) | async-done | bytes 3145744 | tf_op jit(solution)/shard_map/all_gather | solution.py:443
  107.5 32.2 %attend.1 = (bf16[192,128]{1,0:T(8,128)(2,1)}, bf16[8,512,128]{2,1,0:T(8,128)(2,1)}, bf16[8,512,128]{2,1,0:T(8,128)(2,1)}) custom-call(s32[3]{0:T(128)} %pad_add_fusion.place, bf16[16,192,128]{2,1,0:T(8,128)(2,1)} %bitcast.13, bf16[16,192,128]{2,1,0:T(8,128)(2,1)} %copy-done.1, bf16[128,1024]{1,0:T(8,128)(2,1)} %get-tuple-element.44.w_mix, ...), custom_call_target="tpu_custom_call" | custom-call | tf_op jit(solution)/shard_map/attend/pallas_call | solution.py:471
  139.7 2.1 %collective-permute-start.5 = (bf16[8,512,128]{2,1,0:T(8,128)(2,1)}, bf16[8,512,128]{2,1,0:T(8,128)(2,1)S(1)}, u32[]{:S(2)}, u32[]{:S(2)}) collective-permute-start(bf16[8,512,128]{2,1,0:T(8,128)(2,1)} %get-tuple-element.53), channel_id=1, source_target_pairs={{0,1},{1,0},{2,3},{3,2},{4,5},{5,4},{6,7},{7,6},{8,9},{9,8},{10,11... | collective-permute-start | bytes 3145736 | tf_op jit(solution)/shard_map/ppermute | solution.py:516
  142.7 6.0 %collective-permute-start.6 = (bf16[3,32,128]{2,1,0:T(8,128)(2,1)S(1)}, bf16[3,32,128]{2,1,0:T(8,128)(2,1)S(1)}, u32[]{:S(2)}, u32[]{:S(2)}) collective-permute-start(bf16[3,32,128]{2,1,0:T(8,128)(2,1)S(1)} %get-tuple-element.59), channel_id=1, source_target_pairs={{0,16},{16,32},{32,48},{48,64},{64,80},{80,96},{96,112},{112,128},... | collective-permute-start | bytes 73736 | tf_op jit(solution)/shard_map/ppermute | solution.py:518
  148.7 1.9 %collective-permute-start.7 = (bf16[3,32,128]{2,1,0:T(8,128)(2,1)S(1)}, bf16[3,32,128]{2,1,0:T(8,128)(2,1)S(1)}, u32[]{:S(2)}, u32[]{:S(2)}) collective-permute-start(bf16[3,32,128]{2,1,0:T(8,128)(2,1)S(1)} %get-tuple-element.58), channel_id=1, source_target_pairs={{16,0},{32,16},{48,32},{64,48},{80,64},{96,80},{112,96},{128,112},... | collective-permute-start | bytes 73736 | tf_op jit(solution)/shard_map/ppermute | solution.py:519
  150.6 7.4 %collective-permute-done.7.from_right = bf16[3,32,128]{2,1,0:T(8,128)(2,1)S(1)} collective-permute-done((bf16[3,32,128]{2,1,0:T(8,128)(2,1)S(1)}, bf16[3,32,128]{2,1,0:T(8,128)(2,1)S(1)}, u32[]{:S(2)}, u32[]{:S(2)}) %collective-permute-start.7) | collective-permute-done | bytes 24608 | tf_op jit(solution)/shard_map/ppermute | solution.py:519
  158.0 2.5 %add_convert_fusion = bf16[8,512,128]{2,1,0:T(8,128)(2,1)} fusion(bf16[8,512,128]{2,1,0:T(8,128)(2,1)S(1)} %collective-permute-done.5, bf16[8,512,128]{2,1,0:T(8,128)(2,1)} %get-tuple-element.56), kind=kLoop, calls=%fused_computation.1 | loop fusion | flops 2097152 | bytes 3145728 | tf_op jit(solution)/shard_map/convert_element_type | solution.py:521
  160.6 8.5 %all-to-all-start = ((bf16[8,512,128]{2,1,0:T(8,128)(2,1)}), bf16[8,512,128]{2,1,0:T(8,128)(2,1)S(1)}, u32[]{:S(2)}, u32[]{:S(2)}) async-start(bf16[8,512,128]{2,1,0:T(8,128)(2,1)} %add_convert_fusion), calls=%async_computation | async-start | bytes 2097152 | tf_op jit(solution)/shard_map/all_to_all | solution.py:522
  169.9 2.2 %decode.1 = bf16[3,512,128]{2,1,0:T(8,128)(2,1)} custom-call(s32[1]{0:T(128)S(6)} %copy.17.count, s32[512,1]{1,0:T(8,128)} %copy.16.token, bf16[3,512,128]{2,1,0:T(8,128)(2,1)} %get-tuple-element.31.hidden, bf16[3,64,128]{2,1,0:T(8,128)(2,1)} %bitcast.17, bf16[3,32,128]{2,1,0:T(8,128)(2,1)} %copy-done.4, bf16[3,32,128]{2,1,0:T(8,128)(2,1)} %copy-done.5), custom_call_target="tpu_custom_call" | custom-call | tf_op jit(solution)/shard_map/decode/pallas_call | solution.py:525
  172.1 11.8 %all-to-all-done = bf16[8,512,128]{2,1,0:T(8,128)(2,1)S(1)} async-done(((bf16[8,512,128]{2,1,0:T(8,128)(2,1)}), bf16[8,512,128]{2,1,0:T(8,128)(2,1)S(1)}, u32[]{:S(2)}, u32[]{:S(2)}) %all-to-all-start) | async-done | bytes 1048608 | tf_op jit(solution)/shard_map/all_to_all | solution.py:522
  (28 shorter events, 4.6 us)
Async XLA Ops:
  7.2 66.6 %all-gather.8.cloned.1.call-start = ((), (), s32[]{:S(2)}) async-start(), calls=%async_computation.2 | async-start | bytes 2924544 | tf_op jit(solution)/shard_map/all_gather | solution.py:401
  8.8 98.7 %all-gather.6.cloned.1.call-start = ((), (), s32[]{:S(2)}) async-start(), calls=%async_computation.1 | async-start | bytes 3342336 | tf_op jit(solution)/shard_map/all_gather | solution.py:443
  13.4 12.0 %collective-permute-start.2 = (f32[7,32,128]{2,1,0:T(8,128)}, f32[7,32,128]{2,1,0:T(8,128)S(1)}, u32[]{:S(2)}, u32[]{:S(2)}) collective-permute-start(f32[7,32,128]{2,1,0:T(8,128)} %get-tuple-element.33), channel_id=1, source_target_pairs={{0,16},{16,32},{32,48},{48,64},{64,80},{80,96},{96,112},{112,128},... | collective-permute-start | bytes 344072 | tf_op jit(solution)/shard_map/ppermute | solution.py:430
  18.2 11.3 %collective-permute-start.3 = (f32[7,32,128]{2,1,0:T(8,128)}, f32[7,32,128]{2,1,0:T(8,128)S(1)}, u32[]{:S(2)}, u32[]{:S(2)}) collective-permute-start(f32[7,32,128]{2,1,0:T(8,128)} %get-tuple-element.34), channel_id=1, source_target_pairs={{16,0},{32,16},{48,32},{64,48},{80,64},{96,80},{112,96},{128,112},... | collective-permute-start | bytes 344072 | tf_op jit(solution)/shard_map/ppermute | solution.py:431
  20.7 11.2 %collective-permute-start = (bf16[64,768]{1,0:T(8,128)(2,1)}, bf16[64,768]{1,0:T(8,128)(2,1)S(1)}, u32[]{:S(2)}, u32[]{:S(2)}) collective-permute-start(bf16[64,768]{1,0:T(8,128)(2,1)} %t_own.1), channel_id=1, source_target_pairs={{0,0},{33,1},{66,2},{99,3},{132,4},{165,5},{198,6},{231,7},{264,8}... | collective-permute-start | bytes 294920 | tf_op jit(solution)/shard_map/ppermute | solution.py:410
  22.3 11.1 %collective-permute-start.1 = (bf16[64,768]{1,0:T(8,128)(2,1)}, bf16[64,768]{1,0:T(8,128)(2,1)S(1)}, u32[]{:S(2)}, u32[]{:S(2)}) collective-permute-start(bf16[64,768]{1,0:T(8,128)(2,1)} %t_own.1), channel_id=1, source_target_pairs={{16,0},{49,1},{82,2},{115,3},{148,4},{181,5},{214,6},{247,7},{280,... | collective-permute-start | bytes 294920 | tf_op jit(solution)/shard_map/ppermute | solution.py:410
  25.4 4.0 %copy-start.2 = (f32[7,32,128]{2,1,0:T(8,128)}, f32[7,32,128]{2,1,0:T(8,128)S(1)}, u32[]{:S(2)}) copy-start(f32[7,32,128]{2,1,0:T(8,128)S(1)} %collective-permute-done.2.from_left) | copy-start | bytes 344068
  29.5 0.6 copy-start.3
  69.7 8.6 %copy-start = (bf16[3072,128]{1,0:T(8,128)(2,1)}, bf16[3072,128]{1,0:T(8,128)(2,1)S(1)}, u32[]{:S(2)}) copy-start(bf16[3072,128]{1,0:T(8,128)(2,1)S(1)} %all-gather) | copy-start | bytes 2359300
  69.7 26.1 %collective-permute-start.4 = (bf16[16,192,128]{2,1,0:T(8,128)(2,1)S(1)}, bf16[16,192,128]{2,1,0:T(8,128)(2,1)S(1)}, u32[]{:S(2)}, u32[]{:S(2)}) collective-permute-start(bf16[16,192,128]{2,1,0:T(8,128)(2,1)S(1)} %bitcast.12), channel_id=1, source_target_pairs={{0,16},{16,0},{32,48},{48,32},{64,80},{80,64},{96,112},{112,96},{1... | collective-permute-start | bytes 2359304 | tf_op jit(solution)/shard_map/ppermute | solution.py:446
  95.8 11.7 %copy-start.1 = (bf16[16,192,128]{2,1,0:T(8,128)(2,1)}, bf16[16,192,128]{2,1,0:T(8,128)(2,1)S(1)}, u32[]{:S(2)}) copy-start(bf16[16,192,128]{2,1,0:T(8,128)(2,1)S(1)} %collective-permute-done.4.pooled_y) | copy-start | bytes 2359300
  139.7 18.3 %collective-permute-start.5 = (bf16[8,512,128]{2,1,0:T(8,128)(2,1)}, bf16[8,512,128]{2,1,0:T(8,128)(2,1)S(1)}, u32[]{:S(2)}, u32[]{:S(2)}) collective-permute-start(bf16[8,512,128]{2,1,0:T(8,128)(2,1)} %get-tuple-element.53), channel_id=1, source_target_pairs={{0,1},{1,0},{2,3},{3,2},{4,5},{5,4},{6,7},{7,6},{8,9},{9,8},{10,11... | collective-permute-start | bytes 3145736 | tf_op jit(solution)/shard_map/ppermute | solution.py:516
  142.7 8.0 %collective-permute-start.6 = (bf16[3,32,128]{2,1,0:T(8,128)(2,1)S(1)}, bf16[3,32,128]{2,1,0:T(8,128)(2,1)S(1)}, u32[]{:S(2)}, u32[]{:S(2)}) collective-permute-start(bf16[3,32,128]{2,1,0:T(8,128)(2,1)S(1)} %get-tuple-element.59), channel_id=1, source_target_pairs={{0,16},{16,32},{32,48},{48,64},{64,80},{80,96},{96,112},{112,128},... | collective-permute-start | bytes 73736 | tf_op jit(solution)/shard_map/ppermute | solution.py:518
  148.7 9.3 %collective-permute-start.7 = (bf16[3,32,128]{2,1,0:T(8,128)(2,1)S(1)}, bf16[3,32,128]{2,1,0:T(8,128)(2,1)S(1)}, u32[]{:S(2)}, u32[]{:S(2)}) collective-permute-start(bf16[3,32,128]{2,1,0:T(8,128)(2,1)S(1)} %get-tuple-element.58), channel_id=1, source_target_pairs={{16,0},{32,16},{48,32},{64,48},{80,64},{96,80},{112,96},{128,112},... | collective-permute-start | bytes 73736 | tf_op jit(solution)/shard_map/ppermute | solution.py:519
  150.6 9.9 %copy-start.4 = (bf16[3,32,128]{2,1,0:T(8,128)(2,1)}, bf16[3,32,128]{2,1,0:T(8,128)(2,1)S(1)}, u32[]{:S(2)}) copy-start(bf16[3,32,128]{2,1,0:T(8,128)(2,1)S(1)} %collective-permute-done.6.from_left) | copy-start | bytes 73732
  158.0 2.5 %copy-start.5 = (bf16[3,32,128]{2,1,0:T(8,128)(2,1)}, bf16[3,32,128]{2,1,0:T(8,128)(2,1)S(1)}, u32[]{:S(2)}) copy-start(bf16[3,32,128]{2,1,0:T(8,128)(2,1)S(1)} %collective-permute-done.7.from_right) | copy-start | bytes 73732
  158.0 11.0 %copy-start.6 = (s32[512]{0:T(512)S(1)}, s32[512]{0:T(512)}, u32[]{:S(2)}) copy-start(s32[512]{0:T(512)} %broadcast_subtract_fusion) | copy-start | bytes 6148
  160.6 23.3 %all-to-all-start = ((bf16[8,512,128]{2,1,0:T(8,128)(2,1)}), bf16[8,512,128]{2,1,0:T(8,128)(2,1)S(1)}, u32[]{:S(2)}, u32[]{:S(2)}) async-start(bf16[8,512,128]{2,1,0:T(8,128)(2,1)} %add_convert_fusion), calls=%async_computation | async-start | bytes 2097152 | tf_op jit(solution)/shard_map/all_to_all | solution.py:522
Sparse Core Ops, SparseCore 0:
  10.7 46.5 all-gather.7
  59.4 48.0 all-gather.5

commit v7 on v6

--- a/solution.py
+++ b/solution.py
@@ -276,11 +276,11 @@
             lanes = slice(starts[g], starts[g] + span)
             value_lanes = slice(inner + starts[g], inner + starts[g] + span)
             top = jnp.full((rows, 128), -jnp.inf, F32)
-            for j in range(0, total, chunk):
-                part = dot_nt(q, keys(s, j, chunk, lanes))
-                part = part + bias[g * rows : (g + 1) * rows, j : j + chunk].astype(F32)
-                scores[g, :, j : j + chunk] = part
-                for c in range(0, chunk, 128):
+            for j in range(0, total, span):
+                part = dot_nt(q, keys(s, j, span, lanes))
+                part = part + bias[g * rows : (g + 1) * rows, j : j + span].astype(F32)
+                scores[g, :, j : j + span] = part
+                for c in range(0, span, 128):
                     top = jnp.maximum(top, part[:, c : c + 128])
             top = jnp.max(top, axis=-1, keepdims=True)
             amount = jnp.zeros((rows, 128), F32)
@@ -514,14 +514,13 @@
     )
 
     other = lax.ppermute(send, "samp", swap)
+    both = (keep.astype(F32) + other.astype(F32)).astype(BF16)
+    shares = lax.all_to_all(both, "samp", 0, 0, axis_index_groups=sets, tiled=True)
+    bias_grad = jnp.sum(shares.astype(F32), axis=0).reshape(heads, tok, 128)
+
     proj = proj.reshape(samples, tok, channels)
     proj_left = lax.ppermute(proj[:, margin:], "rows", up)
     proj_right = lax.ppermute(proj[:, :margin], "rows", down)
-    other, proj_left, proj_right = lax.optimization_barrier((other, proj_left, proj_right))
-    both = (keep.astype(F32) + other.astype(F32)).astype(BF16)
-    shares = lax.all_to_all(both, "samp", 0, 0, axis_index_groups=sets, tiled=True)
-    bias_grad = jnp.sum(shares.astype(F32), axis=0).reshape(heads, tok, 128)
-
     atom_out = pl.pallas_call(
         decode_kernel,
         out_shape=shape((samples, atoms, channels), BF16),

time: 192 us -> 187 us (0.974)
  the two profiles are of different devices: /device:TPU:112 before, /device:TPU:29 now
where the time goes in v7:
time: 187 us; the launch traced here: 186 us
  starting transfers between devices  51.4 us (27%)
  Pallas kernels  44.9 us (24%)
  waiting for transfers between devices  37.3 us (20%)
  blocking collectives  29.8 us (16%)
  between operations  14.9 us (8%)
  other arithmetic  5.92 us (3%)
  local copies, waits for them, and re-layouts  2.17 us (1%)
    pallas_call x1, Pallas kernels, local(): pl.pallas_call(functools.partial(attend_kernel, heads, factor), out_shape...  32.2 us
    all_gather x1, blocking collectives, local(): lax.all_gather(pooled, 'rows', axis=0, tiled=False, axis_index_groups=z_s...  29.8 us
    ppermute x2, starting transfers between devices, local(): fetched.append(lax.ppermute(token_single, ('rows', 'samp'), perm))  20.1 us
    all_to_all x1, starting transfers between devices, local(): lax.all_to_all(both, 'samp', 0, 0, axis_index_groups=sets, tiled=True)  11.3 us
    ppermute x2, waiting for transfers between devices, local(): fetched.append(lax.ppermute(token_single, ('rows', 'samp'), perm))  10.7 us
    all_gather x1, waiting for transfers between devices, local(): got_t = lax.all_gather(t_own_pair, 'samp', axis=0, tiled=False)  10 us
    ppermute x1, waiting for transfers between devices, local(): proj_left = lax.ppermute(proj[:, margin:], 'rows', up)  8.91 us
    ppermute x1, waiting for transfers between devices, local(): lax.ppermute(pooled_z, 'rows', [(r, r ^ 1) for r in range(n_rows)])  5.13 us
  transfers between devices with their start and end apart: 11, of which 5 were waited for; matrix products, arithmetic and copies ran while one was open for 2% of the time, Pallas kernels for 6%

profile of v7, /device:TPU:29, one launch (start us, length us, event | category | flops | bytes accessed | tf_op | source)
XLA Modules:
  0.0 186.3 jit_solution(8140082260743201499)
XLA Ops:
  7.2 1.5 pack.1
  9.5 1.3 broadcast_subtract_fusion
  10.7 2.6 %pool.1 = (bf16[3,512,128]{2,1,0:T(8,128)(2,1)}, f32[7,64,128]{2,1,0:T(8,128)}, f32[7,32,128]{2,1,0:T(8,128)}, f32[7,32,128]{2,1,0:T(8,128)}) custom-call(s32[1]{0:T(128)S(6)} %copy.17.count, s32[1,512]{1,0:T(1,128)} %bitcast.18, bf16[3,512,128]{2,1,0:T(8,128)(2,1)} %noised, bf16[512,128]{1,0:T(8,128)(2,1)} %single.1, bf16[128,128]{1,0:T(8,128)(2,1)} %w_atom.1, ...), custom_call_target="tpu_custom_call" | custom-call | tf_op jit(solution)/shard_map/pool/pallas_call | solution.py:414
  13.4 4.2 %collective-permute-start.2 = (f32[7,32,128]{2,1,0:T(8,128)}, f32[7,32,128]{2,1,0:T(8,128)S(1)}, u32[]{:S(2)}, u32[]{:S(2)}) collective-permute-start(f32[7,32,128]{2,1,0:T(8,128)} %get-tuple-element.30), channel_id=1, source_target_pairs={{0,16},{16,32},{32,48},{48,64},{64,80},{80,96},{96,112},{112,128},... | collective-permute-start | bytes 344072 | tf_op jit(solution)/shard_map/ppermute | solution.py:430
  17.6 2.6 %collective-permute-start.3 = (f32[7,32,128]{2,1,0:T(8,128)}, f32[7,32,128]{2,1,0:T(8,128)S(1)}, u32[]{:S(2)}, u32[]{:S(2)}) collective-permute-start(f32[7,32,128]{2,1,0:T(8,128)} %get-tuple-element.31), channel_id=1, source_target_pairs={{16,0},{32,16},{48,32},{64,48},{80,64},{96,80},{112,96},{128,112},... | collective-permute-start | bytes 344072 | tf_op jit(solution)/shard_map/ppermute | solution.py:431
  20.2 10.2 %collective-permute-start = (bf16[64,768]{1,0:T(8,128)(2,1)}, bf16[64,768]{1,0:T(8,128)(2,1)S(1)}, u32[]{:S(2)}, u32[]{:S(2)}) collective-permute-start(bf16[64,768]{1,0:T(8,128)(2,1)} %t_own.1), channel_id=1, source_target_pairs={{0,0},{33,1},{66,2},{99,3},{132,4},{165,5},{198,6},{231,7},{264,8}... | collective-permute-start | bytes 294920 | tf_op jit(solution)/shard_map/ppermute | solution.py:410
  30.3 9.9 %collective-permute-start.1 = (bf16[64,768]{1,0:T(8,128)(2,1)}, bf16[64,768]{1,0:T(8,128)(2,1)S(1)}, u32[]{:S(2)}, u32[]{:S(2)}) collective-permute-start(bf16[64,768]{1,0:T(8,128)(2,1)} %t_own.1), channel_id=1, source_target_pairs={{16,0},{49,1},{82,2},{115,3},{148,4},{181,5},{214,6},{247,7},{280,... | collective-permute-start | bytes 294920 | tf_op jit(solution)/shard_map/ppermute | solution.py:410
  41.0 1.7 settle.1
  42.7 10.7 %collective-permute-done.1 = bf16[64,768]{1,0:T(8,128)(2,1)S(1)} collective-permute-done((bf16[64,768]{1,0:T(8,128)(2,1)}, bf16[64,768]{1,0:T(8,128)(2,1)S(1)}, u32[]{:S(2)}, u32[]{:S(2)}) %collective-permute-start.1) | collective-permute-done | bytes 98336 | tf_op jit(solution)/shard_map/ppermute | solution.py:410
  54.1 29.8 %all-gather = bf16[3072,128]{1,0:T(8,128)(2,1)S(1)} all-gather(bf16[192,128]{1,0:T(8,128)(2,1)} %get-tuple-element.36.pooled), channel_id=2, replica_groups={{0,32,64,96,128,160,192,224,256,288,320,352,384,416,448,480},{16,48,80,..., dimensions={0}, use_global_device_ids=true | all-gather | bytes 835584 | tf_op jit(solution)/shard_map/all_gather | solution.py:445
  84.0 3.9 %collective-permute-start.4 = (bf16[16,192,128]{2,1,0:T(8,128)(2,1)S(1)}, bf16[16,192,128]{2,1,0:T(8,128)(2,1)S(1)}, u32[]{:S(2)}, u32[]{:S(2)}) collective-permute-start(bf16[16,192,128]{2,1,0:T(8,128)(2,1)S(1)} %bitcast.12), channel_id=1, source_target_pairs={{0,16},{16,0},{32,48},{48,32},{64,80},{80,64},{96,112},{112,96},{1... | collective-permute-start | bytes 2359304 | tf_op jit(solution)/shard_map/ppermute | solution.py:446
  88.5 4.6 %prep.1 = (bf16[768,896]{1,0:T(8,128)(2,1)}, bf16[128,1024]{1,0:T(8,128)(2,1)}, f32[192,768]{1,0:T(8,128)}, bf16[192,384]{1,0:T(8,128)(2,1)}, f32[192,768]{1,0:T...) custom-call(bf16[16,112,768]{2,1,0:T(8,128)(2,1)} %bitcast.20, bf16[192,128]{1,0:T(8,128)(2,1)} %get-tuple-element.36.pooled, ...), custom_call_target="tpu_custom_call" | custom-call | flops 2000000000 | bytes 8000000 | tf_op jit(solution)/shard_map/prep/pallas_call | solution.py:451
  93.1 5.1 %collective-permute-done.4.pooled_y = bf16[16,192,128]{2,1,0:T(8,128)(2,1)S(1)} collective-permute-done((bf16[16,192,128]{2,1,0:T(8,128)(2,1)S(1)}, bf16[16,192,128]{2,1,0:T(8,128)(2,1)S(1)}, u32[]{:S(2)}, u32[]{:S(2)}) %collective-permute-start.4) | collective-permute-done | bytes 786464 | tf_op jit(solution)/shard_map/ppermute | solution.py:446
  98.2 10.0 %all-gather.6.cloned.1.call-done = bf16[2048,768]{1,0:T(8,128)(2,1)} async-done(((bf16[128,768]{1,0:T(8,128)(2,1)}), bf16[2048,768]{1,0:T(8,128)(2,1)}) %all-gather.6.cloned.1.call-update) | async-done | bytes 3145744 | tf_op jit(solution)/shard_map/all_gather | solution.py:443
  108.2 32.2 %attend.1 = (bf16[192,128]{1,0:T(8,128)(2,1)}, bf16[8,512,128]{2,1,0:T(8,128)(2,1)}, bf16[8,512,128]{2,1,0:T(8,128)(2,1)}) custom-call(s32[3]{0:T(128)} %pad_add_fusion.place, bf16[16,192,128]{2,1,0:T(8,128)(2,1)} %bitcast.13, bf16[16,192,128]{2,1,0:T(8,128)(2,1)} %copy-done.1, bf16[128,1024]{1,0:T(8,128)(2,1)} %get-tuple-element.41.w_mix, ...), custom_call_target="tpu_custom_call" | custom-call | tf_op jit(solution)/shard_map/attend/pallas_call | solution.py:471
  140.5 2.5 %collective-permute-start.7 = (bf16[8,512,128]{2,1,0:T(8,128)(2,1)}, bf16[8,512,128]{2,1,0:T(8,128)(2,1)S(1)}, u32[]{:S(2)}, u32[]{:S(2)}) collective-permute-start(bf16[8,512,128]{2,1,0:T(8,128)(2,1)} %get-tuple-element.51), channel_id=1, source_target_pairs={{0,1},{1,0},{2,3},{3,2},{4,5},{5,4},{6,7},{7,6},{8,9},{9,8},{10,11... | collective-permute-start | bytes 3145736 | tf_op jit(solution)/shard_map/ppermute | solution.py:516
  143.0 2.5 %collective-permute-done.7 = bf16[8,512,128]{2,1,0:T(8,128)(2,1)S(1)} collective-permute-done((bf16[8,512,128]{2,1,0:T(8,128)(2,1)}, bf16[8,512,128]{2,1,0:T(8,128)(2,1)S(1)}, u32[]{:S(2)}, u32[]{:S(2)}) %collective-permute-start.7) | collective-permute-done | bytes 1048608 | tf_op jit(solution)/shard_map/ppermute | solution.py:516
  145.5 2.5 %add_convert_fusion = bf16[8,512,128]{2,1,0:T(8,128)(2,1)} fusion(bf16[8,512,128]{2,1,0:T(8,128)(2,1)S(1)} %collective-permute-done.7, bf16[8,512,128]{2,1,0:T(8,128)(2,1)} %get-tuple-element.50), kind=kLoop, calls=%fused_computation.1 | loop fusion | flops 2097152 | bytes 3145728 | tf_op jit(solution)/shard_map/convert_element_type | solution.py:517
  148.0 11.3 %all-to-all-start = ((bf16[8,512,128]{2,1,0:T(8,128)(2,1)}), bf16[8,512,128]{2,1,0:T(8,128)(2,1)S(1)}, u32[]{:S(2)}, u32[]{:S(2)}) async-start(bf16[8,512,128]{2,1,0:T(8,128)(2,1)} %add_convert_fusion), calls=%async_computation | async-start | bytes 2097152 | tf_op jit(solution)/shard_map/all_to_all | solution.py:518
  159.3 3.9 %collective-permute-start.5 = (bf16[3,32,128]{2,1,0:T(8,128)(2,1)S(1)}, bf16[3,32,128]{2,1,0:T(8,128)(2,1)S(1)}, u32[]{:S(2)}, u32[]{:S(2)}) collective-permute-start(bf16[3,32,128]{2,1,0:T(8,128)(2,1)S(1)} %get-tuple-element.53), channel_id=1, source_target_pairs={{0,16},{16,32},{32,48},{48,64},{64,80},{80,96},{96,112},{112,128},... | collective-permute-start | bytes 73736 | tf_op jit(solution)/shard_map/ppermute | solution.py:522
  163.1 2.9 %collective-permute-start.6 = (bf16[3,32,128]{2,1,0:T(8,128)(2,1)S(1)}, bf16[3,32,128]{2,1,0:T(8,128)(2,1)S(1)}, u32[]{:S(2)}, u32[]{:S(2)}) collective-permute-start(bf16[3,32,128]{2,1,0:T(8,128)(2,1)S(1)} %get-tuple-element.52), channel_id=1, source_target_pairs={{16,0},{32,16},{48,32},{64,48},{80,64},{96,80},{112,96},{128,112},... | collective-permute-start | bytes 73736 | tf_op jit(solution)/shard_map/ppermute | solution.py:523
  166.1 0.9 copy.16.token
  166.9 8.9 %collective-permute-done.5.from_left = bf16[3,32,128]{2,1,0:T(8,128)(2,1)S(1)} collective-permute-done((bf16[3,32,128]{2,1,0:T(8,128)(2,1)S(1)}, bf16[3,32,128]{2,1,0:T(8,128)(2,1)S(1)}, u32[]{:S(2)}, u32[]{:S(2)}) %collective-permute-start.5) | collective-permute-done | bytes 24608 | tf_op jit(solution)/shard_map/ppermute | solution.py:522
  176.5 2.2 %decode.1 = bf16[3,512,128]{2,1,0:T(8,128)(2,1)} custom-call(s32[1]{0:T(128)S(6)} %copy.17.count, s32[512,1]{1,0:T(8,128)} %copy.16.token, bf16[3,512,128]{2,1,0:T(8,128)(2,1)} %get-tuple-element.28.hidden, bf16[3,64,128]{2,1,0:T(8,128)(2,1)} %bitcast.16, bf16[3,32,128]{2,1,0:T(8,128)(2,1)} %copy-done.5, bf16[3,32,128]{2,1,0:T(8,128)(2,1)} %copy-done.6), custom_call_target="tpu_custom_call" | custom-call | tf_op jit(solution)/shard_map/decode/pallas_call | solution.py:524
  (30 shorter events, 3.6 us)
Async XLA Ops:
  7.2 81.3 %all-gather.8.cloned.1.call-start = ((), (), s32[]{:S(2)}) async-start(), calls=%async_computation.2 | async-start | bytes 2924544 | tf_op jit(solution)/shard_map/all_gather | solution.py:401
  8.8 99.5 %all-gather.6.cloned.1.call-start = ((), (), s32[]{:S(2)}) async-start(), calls=%async_computation.1 | async-start | bytes 3342336 | tf_op jit(solution)/shard_map/all_gather | solution.py:443
  13.4 26.9 %collective-permute-start.2 = (f32[7,32,128]{2,1,0:T(8,128)}, f32[7,32,128]{2,1,0:T(8,128)S(1)}, u32[]{:S(2)}, u32[]{:S(2)}) collective-permute-start(f32[7,32,128]{2,1,0:T(8,128)} %get-tuple-element.30), channel_id=1, source_target_pairs={{0,16},{16,32},{32,48},{48,64},{64,80},{80,96},{96,112},{112,128},... | collective-permute-start | bytes 344072 | tf_op jit(solution)/shard_map/ppermute | solution.py:430
  17.6 22.7 %collective-permute-start.3 = (f32[7,32,128]{2,1,0:T(8,128)}, f32[7,32,128]{2,1,0:T(8,128)S(1)}, u32[]{:S(2)}, u32[]{:S(2)}) collective-permute-start(f32[7,32,128]{2,1,0:T(8,128)} %get-tuple-element.31), channel_id=1, source_target_pairs={{16,0},{32,16},{48,32},{64,48},{80,64},{96,80},{112,96},{128,112},... | collective-permute-start | bytes 344072 | tf_op jit(solution)/shard_map/ppermute | solution.py:431
  20.2 22.6 %collective-permute-start = (bf16[64,768]{1,0:T(8,128)(2,1)}, bf16[64,768]{1,0:T(8,128)(2,1)S(1)}, u32[]{:S(2)}, u32[]{:S(2)}) collective-permute-start(bf16[64,768]{1,0:T(8,128)(2,1)} %t_own.1), channel_id=1, source_target_pairs={{0,0},{33,1},{66,2},{99,3},{132,4},{165,5},{198,6},{231,7},{264,8}... | collective-permute-start | bytes 294920 | tf_op jit(solution)/shard_map/ppermute | solution.py:410
  30.3 23.1 %collective-permute-start.1 = (bf16[64,768]{1,0:T(8,128)(2,1)}, bf16[64,768]{1,0:T(8,128)(2,1)S(1)}, u32[]{:S(2)}, u32[]{:S(2)}) collective-permute-start(bf16[64,768]{1,0:T(8,128)(2,1)} %t_own.1), channel_id=1, source_target_pairs={{16,0},{49,1},{82,2},{115,3},{148,4},{181,5},{214,6},{247,7},{280,... | collective-permute-start | bytes 294920 | tf_op jit(solution)/shard_map/ppermute | solution.py:410
  40.3 0.6 copy-start.3
  40.3 0.7 copy-start.4
  84.0 9.1 %copy-start = (bf16[3072,128]{1,0:T(8,128)(2,1)}, bf16[3072,128]{1,0:T(8,128)(2,1)S(1)}, u32[]{:S(2)}) copy-start(bf16[3072,128]{1,0:T(8,128)(2,1)S(1)} %all-gather) | copy-start | bytes 2359300
  84.0 14.2 %collective-permute-start.4 = (bf16[16,192,128]{2,1,0:T(8,128)(2,1)S(1)}, bf16[16,192,128]{2,1,0:T(8,128)(2,1)S(1)}, u32[]{:S(2)}, u32[]{:S(2)}) collective-permute-start(bf16[16,192,128]{2,1,0:T(8,128)(2,1)S(1)} %bitcast.12), channel_id=1, source_target_pairs={{0,16},{16,0},{32,48},{48,32},{64,80},{80,64},{96,112},{112,96},{1... | collective-permute-start | bytes 2359304 | tf_op jit(solution)/shard_map/ppermute | solution.py:446
  98.2 10.0 %copy-start.1 = (bf16[16,192,128]{2,1,0:T(8,128)(2,1)}, bf16[16,192,128]{2,1,0:T(8,128)(2,1)S(1)}, u32[]{:S(2)}) copy-start(bf16[16,192,128]{2,1,0:T(8,128)(2,1)S(1)} %collective-permute-done.4.pooled_y) | copy-start | bytes 2359300
  140.5 5.0 %collective-permute-start.7 = (bf16[8,512,128]{2,1,0:T(8,128)(2,1)}, bf16[8,512,128]{2,1,0:T(8,128)(2,1)S(1)}, u32[]{:S(2)}, u32[]{:S(2)}) collective-permute-start(bf16[8,512,128]{2,1,0:T(8,128)(2,1)} %get-tuple-element.51), channel_id=1, source_target_pairs={{0,1},{1,0},{2,3},{3,2},{4,5},{5,4},{6,7},{7,6},{8,9},{9,8},{10,11... | collective-permute-start | bytes 3145736 | tf_op jit(solution)/shard_map/ppermute | solution.py:516
  145.5 13.8 %copy-start.2 = (bf16[192,128]{1,0:T(8,128)(2,1)S(1)}, bf16[192,128]{1,0:T(8,128)(2,1)}, u32[]{:S(2)}) copy-start(bf16[192,128]{1,0:T(8,128)(2,1)} %get-tuple-element.49) | copy-start | bytes 147460
  145.5 20.6 %copy-start.7 = (s32[512]{0:T(512)S(1)}, s32[512]{0:T(512)}, u32[]{:S(2)}) copy-start(s32[512]{0:T(512)} %broadcast_subtract_fusion) | copy-start | bytes 6148
  148.0 30.7 %all-to-all-start = ((bf16[8,512,128]{2,1,0:T(8,128)(2,1)}), bf16[8,512,128]{2,1,0:T(8,128)(2,1)S(1)}, u32[]{:S(2)}, u32[]{:S(2)}) async-start(bf16[8,512,128]{2,1,0:T(8,128)(2,1)} %add_convert_fusion), calls=%async_computation | async-start | bytes 2097152 | tf_op jit(solution)/shard_map/all_to_all | solution.py:518
  159.3 16.6 %collective-permute-start.5 = (bf16[3,32,128]{2,1,0:T(8,128)(2,1)S(1)}, bf16[3,32,128]{2,1,0:T(8,128)(2,1)S(1)}, u32[]{:S(2)}, u32[]{:S(2)}) collective-permute-start(bf16[3,32,128]{2,1,0:T(8,128)(2,1)S(1)} %get-tuple-element.53), channel_id=1, source_target_pairs={{0,16},{16,32},{32,48},{48,64},{64,80},{80,96},{96,112},{112,128},... | collective-permute-start | bytes 73736 | tf_op jit(solution)/shard_map/ppermute | solution.py:522
  163.1 12.7 %collective-permute-start.6 = (bf16[3,32,128]{2,1,0:T(8,128)(2,1)S(1)}, bf16[3,32,128]{2,1,0:T(8,128)(2,1)S(1)}, u32[]{:S(2)}, u32[]{:S(2)}) collective-permute-start(bf16[3,32,128]{2,1,0:T(8,128)(2,1)S(1)} %get-tuple-element.52), channel_id=1, source_target_pairs={{16,0},{32,16},{48,32},{64,48},{80,64},{96,80},{112,96},{128,112},... | collective-permute-start | bytes 73736 | tf_op jit(solution)/shard_map/ppermute | solution.py:523
  175.8 0.6 copy-start.5
  175.8 0.6 copy-start.6
Sparse Core Ops, SparseCore 0:
  10.7 46.8 all-gather.7
  59.8 48.4 all-gather.5

commit v8 on v7

--- a/solution.py
+++ b/solution.py
@@ -248,7 +248,7 @@
                     ).astype(BF16)
         return carry
 
-    lax.fori_loop(0, blocks, step, 0)
+    lax.fori_loop(0, blocks // 2, lambda i, c: step(2 * i + 1, step(2 * i, c)), 0)
     for made in late:
         made.wait()
 
@@ -340,7 +340,7 @@
             send[k, g * rows : (g + 1) * rows, :] = jnp.where(core == 0, high, low).astype(BF16)
             return carry
 
-        lax.fori_loop(0, total // 256, backward, 0)
+        lax.fori_loop(0, total // 512, lambda i, c: backward(2 * i + 1, backward(2 * i, c)), 0)
 
 
 def decode_kernel(count, token, hidden, proj, from_left, from_right, out):

time: 187 us -> 184 us (0.984)
  Pallas kernels: 44.9 us -> 41.8 us
    pallas_call x1, Pallas kernels: 32.2 us -> 29.2 us  [local(): pl.pallas_call(functools.partial(attend_kernel, heads, factor), out_shape...]
where the time goes in v8:
time: 184 us; the launch traced here: 183 us
  starting transfers between devices  51.4 us (28%)
  Pallas kernels  41.8 us (23%)
  waiting for transfers between devices  37.3 us (20%)
  blocking collectives  29.8 us (16%)
  between operations  14.9 us (8%)
  other arithmetic  5.92 us (3%)
  local copies, waits for them, and re-layouts  2.17 us (1%)
    all_gather x1, blocking collectives, local(): lax.all_gather(pooled, 'rows', axis=0, tiled=False, axis_index_groups=z_s...  29.8 us
    pallas_call x1, Pallas kernels, local(): pl.pallas_call(functools.partial(attend_kernel, heads, factor), out_shape...  29.2 us
    ppermute x2, starting transfers between devices, local(): fetched.append(lax.ppermute(token_single, ('rows', 'samp'), perm))  20.1 us
    all_to_all x1, starting transfers between devices, local(): lax.all_to_all(both, 'samp', 0, 0, axis_index_groups=sets, tiled=True)  11.3 us
    ppermute x2, waiting for transfers between devices, local(): fetched.append(lax.ppermute(token_single, ('rows', 'samp'), perm))  10.7 us
    all_gather x1, waiting for transfers between devices, local(): got_t = lax.all_gather(t_own_pair, 'samp', axis=0, tiled=False)  10 us
    ppermute x1, waiting for transfers between devices, local(): proj_left = lax.ppermute(proj[:, margin:], 'rows', up)  8.91 us
    ppermute x1, waiting for transfers between devices, local(): lax.ppermute(pooled_z, 'rows', [(r, r ^ 1) for r in range(n_rows)])  5.13 us
  transfers between devices with their start and end apart: 11, of which 5 were waited for; matrix products, arithmetic and copies ran while one was open for 2% of the time, Pallas kernels for 6%

profile of v8, /device:TPU:29, one launch (start us, length us, event | category | flops | bytes accessed | tf_op | source)
XLA Modules:
  0.0 183.3 jit_solution(11847958768702134967)
XLA Ops:
  7.2 1.5 pack.1
  9.5 1.3 broadcast_subtract_fusion
  10.7 2.6 %pool.1 = (bf16[3,512,128]{2,1,0:T(8,128)(2,1)}, f32[7,64,128]{2,1,0:T(8,128)}, f32[7,32,128]{2,1,0:T(8,128)}, f32[7,32,128]{2,1,0:T(8,128)}) custom-call(s32[1]{0:T(128)S(6)} %copy.17.count, s32[1,512]{1,0:T(1,128)} %bitcast.18, bf16[3,512,128]{2,1,0:T(8,128)(2,1)} %noised, bf16[512,128]{1,0:T(8,128)(2,1)} %single.1, bf16[128,128]{1,0:T(8,128)(2,1)} %w_atom.1, ...), custom_call_target="tpu_custom_call" | custom-call | tf_op jit(solution)/shard_map/pool/pallas_call | solution.py:414
  13.4 4.2 %collective-permute-start.2 = (f32[7,32,128]{2,1,0:T(8,128)}, f32[7,32,128]{2,1,0:T(8,128)S(1)}, u32[]{:S(2)}, u32[]{:S(2)}) collective-permute-start(f32[7,32,128]{2,1,0:T(8,128)} %get-tuple-element.30), channel_id=1, source_target_pairs={{0,16},{16,32},{32,48},{48,64},{64,80},{80,96},{96,112},{112,128},... | collective-permute-start | bytes 344072 | tf_op jit(solution)/shard_map/ppermute | solution.py:430
  17.6 2.6 %collective-permute-start.3 = (f32[7,32,128]{2,1,0:T(8,128)}, f32[7,32,128]{2,1,0:T(8,128)S(1)}, u32[]{:S(2)}, u32[]{:S(2)}) collective-permute-start(f32[7,32,128]{2,1,0:T(8,128)} %get-tuple-element.31), channel_id=1, source_target_pairs={{16,0},{32,16},{48,32},{64,48},{80,64},{96,80},{112,96},{128,112},... | collective-permute-start | bytes 344072 | tf_op jit(solution)/shard_map/ppermute | solution.py:431
  20.2 10.2 %collective-permute-start = (bf16[64,768]{1,0:T(8,128)(2,1)}, bf16[64,768]{1,0:T(8,128)(2,1)S(1)}, u32[]{:S(2)}, u32[]{:S(2)}) collective-permute-start(bf16[64,768]{1,0:T(8,128)(2,1)} %t_own.1), channel_id=1, source_target_pairs={{0,0},{33,1},{66,2},{99,3},{132,4},{165,5},{198,6},{231,7},{264,8}... | collective-permute-start | bytes 294920 | tf_op jit(solution)/shard_map/ppermute | solution.py:410
  30.3 9.9 %collective-permute-start.1 = (bf16[64,768]{1,0:T(8,128)(2,1)}, bf16[64,768]{1,0:T(8,128)(2,1)S(1)}, u32[]{:S(2)}, u32[]{:S(2)}) collective-permute-start(bf16[64,768]{1,0:T(8,128)(2,1)} %t_own.1), channel_id=1, source_target_pairs={{16,0},{49,1},{82,2},{115,3},{148,4},{181,5},{214,6},{247,7},{280,... | collective-permute-start | bytes 294920 | tf_op jit(solution)/shard_map/ppermute | solution.py:410
  41.0 1.7 settle.1
  42.7 10.7 %collective-permute-done.1 = bf16[64,768]{1,0:T(8,128)(2,1)S(1)} collective-permute-done((bf16[64,768]{1,0:T(8,128)(2,1)}, bf16[64,768]{1,0:T(8,128)(2,1)S(1)}, u32[]{:S(2)}, u32[]{:S(2)}) %collective-permute-start.1) | collective-permute-done | bytes 98336 | tf_op jit(solution)/shard_map/ppermute | solution.py:410
  54.1 29.8 %all-gather = bf16[3072,128]{1,0:T(8,128)(2,1)S(1)} all-gather(bf16[192,128]{1,0:T(8,128)(2,1)} %get-tuple-element.36.pooled), channel_id=2, replica_groups={{0,32,64,96,128,160,192,224,256,288,320,352,384,416,448,480},{16,48,80,..., dimensions={0}, use_global_device_ids=true | all-gather | bytes 835584 | tf_op jit(solution)/shard_map/all_gather | solution.py:445
  84.0 3.9 %collective-permute-start.4 = (bf16[16,192,128]{2,1,0:T(8,128)(2,1)S(1)}, bf16[16,192,128]{2,1,0:T(8,128)(2,1)S(1)}, u32[]{:S(2)}, u32[]{:S(2)}) collective-permute-start(bf16[16,192,128]{2,1,0:T(8,128)(2,1)S(1)} %bitcast.12), channel_id=1, source_target_pairs={{0,16},{16,0},{32,48},{48,32},{64,80},{80,64},{96,112},{112,96},{1... | collective-permute-start | bytes 2359304 | tf_op jit(solution)/shard_map/ppermute | solution.py:446
  88.5 4.6 %prep.1 = (bf16[768,896]{1,0:T(8,128)(2,1)}, bf16[128,1024]{1,0:T(8,128)(2,1)}, f32[192,768]{1,0:T(8,128)}, bf16[192,384]{1,0:T(8,128)(2,1)}, f32[192,768]{1,0:T...) custom-call(bf16[16,112,768]{2,1,0:T(8,128)(2,1)} %bitcast.20, bf16[192,128]{1,0:T(8,128)(2,1)} %get-tuple-element.36.pooled, ...), custom_call_target="tpu_custom_call" | custom-call | flops 2000000000 | bytes 8000000 | tf_op jit(solution)/shard_map/prep/pallas_call | solution.py:451
  93.1 5.1 %collective-permute-done.4.pooled_y = bf16[16,192,128]{2,1,0:T(8,128)(2,1)S(1)} collective-permute-done((bf16[16,192,128]{2,1,0:T(8,128)(2,1)S(1)}, bf16[16,192,128]{2,1,0:T(8,128)(2,1)S(1)}, u32[]{:S(2)}, u32[]{:S(2)}) %collective-permute-start.4) | collective-permute-done | bytes 786464 | tf_op jit(solution)/shard_map/ppermute | solution.py:446
  98.2 10.0 %all-gather.6.cloned.1.call-done = bf16[2048,768]{1,0:T(8,128)(2,1)} async-done(((bf16[128,768]{1,0:T(8,128)(2,1)}), bf16[2048,768]{1,0:T(8,128)(2,1)}) %all-gather.6.cloned.1.call-update) | async-done | bytes 3145744 | tf_op jit(solution)/shard_map/all_gather | solution.py:443
  108.2 29.2 %attend.1 = (bf16[192,128]{1,0:T(8,128)(2,1)}, bf16[8,512,128]{2,1,0:T(8,128)(2,1)}, bf16[8,512,128]{2,1,0:T(8,128)(2,1)}) custom-call(s32[3]{0:T(128)} %pad_add_fusion.place, bf16[16,192,128]{2,1,0:T(8,128)(2,1)} %bitcast.13, bf16[16,192,128]{2,1,0:T(8,128)(2,1)} %copy-done.1, bf16[128,1024]{1,0:T(8,128)(2,1)} %get-tuple-element.41.w_mix, ...), custom_call_target="tpu_custom_call" | custom-call | tf_op jit(solution)/shard_map/attend/pallas_call | solution.py:471
  137.4 2.5 %collective-permute-start.7 = (bf16[8,512,128]{2,1,0:T(8,128)(2,1)}, bf16[8,512,128]{2,1,0:T(8,128)(2,1)S(1)}, u32[]{:S(2)}, u32[]{:S(2)}) collective-permute-start(bf16[8,512,128]{2,1,0:T(8,128)(2,1)} %get-tuple-element.51), channel_id=1, source_target_pairs={{0,1},{1,0},{2,3},{3,2},{4,5},{5,4},{6,7},{7,6},{8,9},{9,8},{10,11... | collective-permute-start | bytes 3145736 | tf_op jit(solution)/shard_map/ppermute | solution.py:516
  139.9 2.5 %collective-permute-done.7 = bf16[8,512,128]{2,1,0:T(8,128)(2,1)S(1)} collective-permute-done((bf16[8,512,128]{2,1,0:T(8,128)(2,1)}, bf16[8,512,128]{2,1,0:T(8,128)(2,1)S(1)}, u32[]{:S(2)}, u32[]{:S(2)}) %collective-permute-start.7) | collective-permute-done | bytes 1048608 | tf_op jit(solution)/shard_map/ppermute | solution.py:516
  142.4 2.5 %add_convert_fusion = bf16[8,512,128]{2,1,0:T(8,128)(2,1)} fusion(bf16[8,512,128]{2,1,0:T(8,128)(2,1)S(1)} %collective-permute-done.7, bf16[8,512,128]{2,1,0:T(8,128)(2,1)} %get-tuple-element.50), kind=kLoop, calls=%fused_computation.1 | loop fusion | flops 2097152 | bytes 3145728 | tf_op jit(solution)/shard_map/convert_element_type | solution.py:517
  144.9 11.3 %all-to-all-start = ((bf16[8,512,128]{2,1,0:T(8,128)(2,1)}), bf16[8,512,128]{2,1,0:T(8,128)(2,1)S(1)}, u32[]{:S(2)}, u32[]{:S(2)}) async-start(bf16[8,512,128]{2,1,0:T(8,128)(2,1)} %add_convert_fusion), calls=%async_computation | async-start | bytes 2097152 | tf_op jit(solution)/shard_map/all_to_all | solution.py:518
  156.2 3.9 %collective-permute-start.5 = (bf16[3,32,128]{2,1,0:T(8,128)(2,1)S(1)}, bf16[3,32,128]{2,1,0:T(8,128)(2,1)S(1)}, u32[]{:S(2)}, u32[]{:S(2)}) collective-permute-start(bf16[3,32,128]{2,1,0:T(8,128)(2,1)S(1)} %get-tuple-element.53), channel_id=1, source_target_pairs={{0,16},{16,32},{32,48},{48,64},{64,80},{80,96},{96,112},{112,128},... | collective-permute-start | bytes 73736 | tf_op jit(solution)/shard_map/ppermute | solution.py:522
  160.1 2.9 %collective-permute-start.6 = (bf16[3,32,128]{2,1,0:T(8,128)(2,1)S(1)}, bf16[3,32,128]{2,1,0:T(8,128)(2,1)S(1)}, u32[]{:S(2)}, u32[]{:S(2)}) collective-permute-start(bf16[3,32,128]{2,1,0:T(8,128)(2,1)S(1)} %get-tuple-element.52), channel_id=1, source_target_pairs={{16,0},{32,16},{48,32},{64,48},{80,64},{96,80},{112,96},{128,112},... | collective-permute-start | bytes 73736 | tf_op jit(solution)/shard_map/ppermute | solution.py:523
  163.0 0.9 copy.16.token
  163.9 8.9 %collective-permute-done.5.from_left = bf16[3,32,128]{2,1,0:T(8,128)(2,1)S(1)} collective-permute-done((bf16[3,32,128]{2,1,0:T(8,128)(2,1)S(1)}, bf16[3,32,128]{2,1,0:T(8,128)(2,1)S(1)}, u32[]{:S(2)}, u32[]{:S(2)}) %collective-permute-start.5) | collective-permute-done | bytes 24608 | tf_op jit(solution)/shard_map/ppermute | solution.py:522
  173.4 2.2 %decode.1 = bf16[3,512,128]{2,1,0:T(8,128)(2,1)} custom-call(s32[1]{0:T(128)S(6)} %copy.17.count, s32[512,1]{1,0:T(8,128)} %copy.16.token, bf16[3,512,128]{2,1,0:T(8,128)(2,1)} %get-tuple-element.28.hidden, bf16[3,64,128]{2,1,0:T(8,128)(2,1)} %bitcast.16, bf16[3,32,128]{2,1,0:T(8,128)(2,1)} %copy-done.5, bf16[3,32,128]{2,1,0:T(8,128)(2,1)} %copy-done.6), custom_call_target="tpu_custom_call" | custom-call | tf_op jit(solution)/shard_map/decode/pallas_call | solution.py:524
  (30 shorter events, 3.6 us)
Async XLA Ops:
  7.2 81.3 %all-gather.8.cloned.1.call-start = ((), (), s32[]{:S(2)}) async-start(), calls=%async_computation.2 | async-start | bytes 2924544 | tf_op jit(solution)/shard_map/all_gather | solution.py:401
  8.8 99.5 %all-gather.6.cloned.1.call-start = ((), (), s32[]{:S(2)}) async-start(), calls=%async_computation.1 | async-start | bytes 3342336 | tf_op jit(solution)/shard_map/all_gather | solution.py:443
  13.4 26.9 %collective-permute-start.2 = (f32[7,32,128]{2,1,0:T(8,128)}, f32[7,32,128]{2,1,0:T(8,128)S(1)}, u32[]{:S(2)}, u32[]{:S(2)}) collective-permute-start(f32[7,32,128]{2,1,0:T(8,128)} %get-tuple-element.30), channel_id=1, source_target_pairs={{0,16},{16,32},{32,48},{48,64},{64,80},{80,96},{96,112},{112,128},... | collective-permute-start | bytes 344072 | tf_op jit(solution)/shard_map/ppermute | solution.py:430
  17.6 22.7 %collective-permute-start.3 = (f32[7,32,128]{2,1,0:T(8,128)}, f32[7,32,128]{2,1,0:T(8,128)S(1)}, u32[]{:S(2)}, u32[]{:S(2)}) collective-permute-start(f32[7,32,128]{2,1,0:T(8,128)} %get-tuple-element.31), channel_id=1, source_target_pairs={{16,0},{32,16},{48,32},{64,48},{80,64},{96,80},{112,96},{128,112},... | collective-permute-start | bytes 344072 | tf_op jit(solution)/shard_map/ppermute | solution.py:431
  20.2 22.6 %collective-permute-start = (bf16[64,768]{1,0:T(8,128)(2,1)}, bf16[64,768]{1,0:T(8,128)(2,1)S(1)}, u32[]{:S(2)}, u32[]{:S(2)}) collective-permute-start(bf16[64,768]{1,0:T(8,128)(2,1)} %t_own.1), channel_id=1, source_target_pairs={{0,0},{33,1},{66,2},{99,3},{132,4},{165,5},{198,6},{231,7},{264,8}... | collective-permute-start | bytes 294920 | tf_op jit(solution)/shard_map/ppermute | solution.py:410
  30.3 23.1 %collective-permute-start.1 = (bf16[64,768]{1,0:T(8,128)(2,1)}, bf16[64,768]{1,0:T(8,128)(2,1)S(1)}, u32[]{:S(2)}, u32[]{:S(2)}) collective-permute-start(bf16[64,768]{1,0:T(8,128)(2,1)} %t_own.1), channel_id=1, source_target_pairs={{16,0},{49,1},{82,2},{115,3},{148,4},{181,5},{214,6},{247,7},{280,... | collective-permute-start | bytes 294920 | tf_op jit(solution)/shard_map/ppermute | solution.py:410
  40.3 0.6 copy-start.3
  40.3 0.7 copy-start.4
  84.0 9.1 %copy-start = (bf16[3072,128]{1,0:T(8,128)(2,1)}, bf16[3072,128]{1,0:T(8,128)(2,1)S(1)}, u32[]{:S(2)}) copy-start(bf16[3072,128]{1,0:T(8,128)(2,1)S(1)} %all-gather) | copy-start | bytes 2359300
  84.0 14.2 %collective-permute-start.4 = (bf16[16,192,128]{2,1,0:T(8,128)(2,1)S(1)}, bf16[16,192,128]{2,1,0:T(8,128)(2,1)S(1)}, u32[]{:S(2)}, u32[]{:S(2)}) collective-permute-start(bf16[16,192,128]{2,1,0:T(8,128)(2,1)S(1)} %bitcast.12), channel_id=1, source_target_pairs={{0,16},{16,0},{32,48},{48,32},{64,80},{80,64},{96,112},{112,96},{1... | collective-permute-start | bytes 2359304 | tf_op jit(solution)/shard_map/ppermute | solution.py:446
  98.2 10.0 %copy-start.1 = (bf16[16,192,128]{2,1,0:T(8,128)(2,1)}, bf16[16,192,128]{2,1,0:T(8,128)(2,1)S(1)}, u32[]{:S(2)}) copy-start(bf16[16,192,128]{2,1,0:T(8,128)(2,1)S(1)} %collective-permute-done.4.pooled_y) | copy-start | bytes 2359300
  137.4 5.0 %collective-permute-start.7 = (bf16[8,512,128]{2,1,0:T(8,128)(2,1)}, bf16[8,512,128]{2,1,0:T(8,128)(2,1)S(1)}, u32[]{:S(2)}, u32[]{:S(2)}) collective-permute-start(bf16[8,512,128]{2,1,0:T(8,128)(2,1)} %get-tuple-element.51), channel_id=1, source_target_pairs={{0,1},{1,0},{2,3},{3,2},{4,5},{5,4},{6,7},{7,6},{8,9},{9,8},{10,11... | collective-permute-start | bytes 3145736 | tf_op jit(solution)/shard_map/ppermute | solution.py:516
  142.4 13.8 %copy-start.2 = (bf16[192,128]{1,0:T(8,128)(2,1)S(1)}, bf16[192,128]{1,0:T(8,128)(2,1)}, u32[]{:S(2)}) copy-start(bf16[192,128]{1,0:T(8,128)(2,1)} %get-tuple-element.49) | copy-start | bytes 147460
  142.4 20.6 %copy-start.7 = (s32[512]{0:T(512)S(1)}, s32[512]{0:T(512)}, u32[]{:S(2)}) copy-start(s32[512]{0:T(512)} %broadcast_subtract_fusion) | copy-start | bytes 6148
  144.9 30.7 %all-to-all-start = ((bf16[8,512,128]{2,1,0:T(8,128)(2,1)}), bf16[8,512,128]{2,1,0:T(8,128)(2,1)S(1)}, u32[]{:S(2)}, u32[]{:S(2)}) async-start(bf16[8,512,128]{2,1,0:T(8,128)(2,1)} %add_convert_fusion), calls=%async_computation | async-start | bytes 2097152 | tf_op jit(solution)/shard_map/all_to_all | solution.py:518
  156.2 16.6 %collective-permute-start.5 = (bf16[3,32,128]{2,1,0:T(8,128)(2,1)S(1)}, bf16[3,32,128]{2,1,0:T(8,128)(2,1)S(1)}, u32[]{:S(2)}, u32[]{:S(2)}) collective-permute-start(bf16[3,32,128]{2,1,0:T(8,128)(2,1)S(1)} %get-tuple-element.53), channel_id=1, source_target_pairs={{0,16},{16,32},{32,48},{48,64},{64,80},{80,96},{96,112},{112,128},... | collective-permute-start | bytes 73736 | tf_op jit(solution)/shard_map/ppermute | solution.py:522
  160.1 12.7 %collective-permute-start.6 = (bf16[3,32,128]{2,1,0:T(8,128)(2,1)S(1)}, bf16[3,32,128]{2,1,0:T(8,128)(2,1)S(1)}, u32[]{:S(2)}, u32[]{:S(2)}) collective-permute-start(bf16[3,32,128]{2,1,0:T(8,128)(2,1)S(1)} %get-tuple-element.52), channel_id=1, source_target_pairs={{16,0},{32,16},{48,32},{64,48},{80,64},{96,80},{112,96},{128,112},... | collective-permute-start | bytes 73736 | tf_op jit(solution)/shard_map/ppermute | solution.py:523
  172.8 0.6 copy-start.5
  172.8 0.6 copy-start.6
Sparse Core Ops, SparseCore 0:
  10.7 46.8 all-gather.7
  59.8 48.4 all-gather.5
